TPU v7x, 512 devices: a whole 4x8x8 slice. The times are simulated.
512 devices in a mesh: row: 8 (over x, y_hi), col: 64 (over y_lo, z, core).
Axes of the slice: x: 4, y: 8 (y_hi: 2, y_lo: 4; y = y_hi * 4 + y_lo), z: 8, core: 2. Of those that a mesh axis runs over, the one named last changes fastest.
Arguments:
- row_emb: float32 [300, 4096], P(None, ('row', 'col')), may hold values from -1.5 to 1.5
- row_acc: float32 [300, 4096], P(None, ('row', 'col')), may hold values from 0.05 to 0.5
- col_emb: float32 [300, 65536], P(None, ('col', 'row')), may hold values from -1.5 to 1.5
- col_acc: float32 [300, 65536], P(None, ('col', 'row')), may hold values from 0.05 to 0.5
- counts: int32 [4096, 65536], P('row', 'col'), may hold values from 0 to 1000, as said below
- row_marg: int32 [4096], P('row'), may hold values from 100 to 9999
- col_marg: int32 [65536], P('col'), may hold values from 100 to 9999
Outputs:
- row_emb_out: float32 [300, 4096], P(None, ('row', 'col'))
- row_acc_out: float32 [300, 4096], P(None, ('row', 'col'))
- col_emb_out: float32 [300, 65536], P(None, ('col', 'row'))
- col_acc_out: float32 [300, 65536], P(None, ('col', 'row'))
Inputs may be any that keep to these rules, and one draw needn't show every extreme that they name: Roughly half of the counts are zero.
All inputs are finite; a program needn't handle non-finite values.
Results may differ from a plain program's by a relative error of at most 0.0076.
Values may be sent and summed in bfloat16 or wider, within the bound.
No kernel may reach another device: no remote copies, remote signals or barrier semaphores. Data moves between devices by JAX's collectives and lax.ppermute only.
A program may use at most 64 MiB of HBM per device.

v0:
```python
import jax
import jax.numpy as jnp
from jax import lax
from jax.sharding import PartitionSpec as P


def pair_slope(score, counts, row_marg, col_marg):
    values = counts.astype(jnp.float32)
    pmi = (
        jnp.log(jnp.maximum(values, 1.0))
        + 12.0
        - jnp.log(row_marg.astype(jnp.float32))[:, None]
        - jnp.log(col_marg.astype(jnp.float32))[None, :]
    )
    diff = score - pmi
    weight = 0.1 + 0.25 * jnp.sqrt(values)
    return jnp.where(counts > 0, weight * diff, jax.nn.sigmoid(diff))


def tile_grads(row_half, col_half, counts, row_marg, col_marg):
    score = lax.dot_general(
        row_half, col_half, (((0,), (0,)), ((), ())), preferred_element_type=jnp.float32
    )
    slope = pair_slope(score, counts, row_marg, col_marg).astype(jnp.bfloat16)
    grad_rows = lax.dot_general(
        col_half, slope, (((1,), (1,)), ((), ())), preferred_element_type=jnp.float32
    )
    grad_cols = lax.dot_general(
        row_half, slope, (((1,), (0,)), ((), ())), preferred_element_type=jnp.float32
    )
    return (grad_rows, grad_cols)


def adagrad(emb, acc, grad):
    acc = acc + grad * grad
    return (emb - 0.1 * grad / jnp.sqrt(acc), acc)


def on_device(row_emb, row_acc, col_emb, col_acc, counts, row_marg, col_marg):
    row_scale = 1.0 / jnp.sqrt(jnp.float32(counts.shape[1] * lax.axis_size("col")))
    col_scale = 1.0 / jnp.sqrt(jnp.float32(counts.shape[0] * lax.axis_size("row")))
    for step in range(2):
        row_half = lax.all_gather(row_emb.astype(jnp.bfloat16), "col", axis=1, tiled=True)
        col_half = lax.all_gather(col_emb.astype(jnp.bfloat16), "row", axis=1, tiled=True)
        grad_rows, grad_cols = tile_grads(row_half, col_half, counts, row_marg, col_marg)
        row_grad = lax.psum_scatter(grad_rows, "col", scatter_dimension=1, tiled=True) * row_scale
        col_grad = lax.psum_scatter(grad_cols, "row", scatter_dimension=1, tiled=True) * col_scale
        row_emb, row_acc = adagrad(row_emb, row_acc, row_grad)
        col_emb, col_acc = adagrad(col_emb, col_acc, col_grad)
    return (row_emb, row_acc, col_emb, col_acc)


def solution(mesh):
    in_specs = (
        P(None, ("row", "col")),
        P(None, ("row", "col")),
        P(None, ("col", "row")),
        P(None, ("col", "row")),
        P("row", "col"),
        P("row"),
        P("col"),
    )
    out_specs = (
        P(None, ("row", "col")),
        P(None, ("row", "col")),
        P(None, ("col", "row")),
        P(None, ("col", "row")),
    )
    return jax.shard_map(
        on_device, mesh=mesh, in_specs=in_specs, out_specs=out_specs, check_vma=False
    )
```

profile of v0, /device:TPU:1, one launch (start us, length us, event | category | flops | bytes accessed | tf_op | source)
XLA Modules:
  0.0 1289.1 jit_solution(15213436555038311146)
XLA Ops:
  8.0 0.9 convert_element_type.32
  9.0 45.0 %all_gather.13 = bf16[300,1024]{1,0:T(8,128)(2,1)S(1)} all-gather(bf16[300,128]{1,0:T(8,128)(2,1)S(1)} %convert_element_type.32), channel_id=1, replica_groups=mesh['row'=8,'col'=64] {'row'}, dimensions={1}, use_global_device_ids=true | all-gather | bytes 691200 | tf_op jit(solution)/shard_map/all_gather | solution.py:44
  54.0 0.7 convert_element_type.31
  54.7 87.6 %all_gather.12 = bf16[300,512]{0,1:T(8,128)(2,1)S(1)} all-gather(bf16[300,8]{0,1:T(8,128)(2,1)S(1)} %convert_element_type.31), channel_id=1, replica_groups=mesh['row'=8,'col'=64] {'col'}, dimensions={1}, use_global_device_ids=true | all-gather | bytes 312000 | tf_op jit(solution)/shard_map/all_gather | solution.py:43
  142.3 0.7 convert_log_fusion
  143.0 0.7 convert_log_fusion.1
  143.7 4.2 select_convert_fusion.1
  147.8 1.4 convolution_bitcast_fusion.1
  149.3 1.6 convolution_bitcast_fusion
  151.0 1.3 dynamic-slice
  152.9 496.5 %all-reduce.5.cloned.1.call-done = f32[300,512]{1,0:T(8,128)} async-done(((f32[300,512]{1,0:T(8,128)}), f32[300,512]{1,0:T(8,128)}) %all-reduce.5.cloned.1.call-update) | async-done | bytes 614416
  649.4 1.0 constant_dynamic-slice_fusion.1
  650.4 0.1 copy.22
  650.5 78.9 %all_gather.15 = bf16[300,512]{0,1:T(8,128)(2,1)S(1)} all-gather(bf16[300,8]{0,1:T(8,128)(2,1)S(1)} %fusion), channel_id=1, replica_groups=mesh['row'=8,'col'=64] {'col'}, dimensions={1}, use_global_device_ids=true | all-gather | bytes 312000 | tf_op jit(solution)/shard_map/all_gather | solution.py:43
  729.4 1.0 fusion.1
  730.4 40.2 %all_gather.14 = bf16[300,1024]{1,0:T(8,128)(2,1)S(1)} all-gather(bf16[300,128]{1,0:T(8,128)(2,1)S(1)} %fusion.1), channel_id=1, replica_groups=mesh['row'=8,'col'=64] {'row'}, dimensions={1}, use_global_device_ids=true | all-gather | bytes 691200 | tf_op jit(solution)/shard_map/all_gather | solution.py:44
  770.6 4.2 select_convert_fusion
  774.8 1.4 fusion.2
  776.3 1.6 fusion.3
  777.9 500.4 %all-reduce.7.cloned.1.call-done = f32[300,512]{1,0:T(8,128)} async-done(((f32[300,512]{1,0:T(8,128)}), f32[300,512]{1,0:T(8,128)}) %all-reduce.7.cloned.1.call-update) | async-done | bytes 614416
  1278.2 1.0 constant_dynamic-slice_fusion
  1279.2 0.1 copy.25
  1279.3 0.6 multiply_subtract_fusion.2
  1280.0 1.7 multiply_subtract_fusion
  (21 shorter events, 0.3 us)
Async XLA Ops:
  8.0 641.4 %all-reduce.5.cloned.1.call-start = ((), (), s32[]{:S(2)}) async-start(), calls=%async_computation.4 | async-start | bytes 1245184
  149.2 501.3 %copy-start.3 = (f32[300,8]{0,1:T(8,128)S(1)}, f32[300,8]{0,1:T(8,128)}, u32[]{:S(2)}) copy-start(f32[300,8]{0,1:T(8,128)} %param.7) | copy-start | bytes 28804
  149.2 501.3 %copy-start.4 = (f32[300,8]{0,1:T(8,128)S(1)}, f32[300,8]{0,1:T(8,128)}, u32[]{:S(2)}) copy-start(f32[300,8]{0,1:T(8,128)} %param.8) | copy-start | bytes 28804
  149.2 580.2 %copy-start = (f32[300,128]{1,0:T(8,128)S(1)}, f32[300,128]{1,0:T(8,128)}, u32[]{:S(2)}) copy-start(f32[300,128]{1,0:T(8,128)} %param.9) | copy-start | bytes 460804
  149.3 580.2 %copy-start.1 = (f32[300,128]{1,0:T(8,128)S(1)}, f32[300,128]{1,0:T(8,128)}, u32[]{:S(2)}) copy-start(f32[300,128]{1,0:T(8,128)} %param.10) | copy-start | bytes 460804
  149.3 580.2 %reduce-scatter.5.cloned.1.call-start = ((), (), s32[]{:S(2)}) async-start(), calls=%async_computation.2 | async-start | bytes 1400832 | tf_op jit(solution)/shard_map/reduce_scatter | solution.py:47
  150.9 1127.3 %all-reduce.7.cloned.1.call-start = ((), (), s32[]{:S(2)}) async-start(), calls=%async_computation.5 | async-start | bytes 1245184
  776.2 503.8 %copy-start.2 = (f32[300,128]{1,0:T(8,128)S(1)}, f32[300,128]{1,0:T(8,128)}, u32[]{:S(2)}) copy-start(f32[300,128]{1,0:T(8,128)} %reduce-scatter.5.cloned.1.call-done) | copy-start | bytes 460804
  776.2 503.8 %reduce-scatter.7.cloned.1.call-start = ((), (), s32[]{:S(2)}) async-start(), calls=%async_computation.3 | async-start | bytes 1400832 | tf_op jit(solution)/shard_map/reduce_scatter | solution.py:47
Sparse Core Ops, SparseCore 0:
  149.3 500.0 all-reduce.4
  776.3 501.8 all-reduce.6
Sparse Core Ops, SparseCore 1:
  154.9 81.2 reduce-scatter.4
  781.2 83.4 reduce-scatter.6
where the time goes:
time: 1290 us
  waiting for transfers between devices  997 us (77%)
  blocking collectives  252 us (20%)
  between operations  16.2 us (1%)
  matrix products  14.2 us (1%)
    unnamed x6, waiting for transfers between devices  997 us
    all_gather x2, blocking collectives, on_device(): lax.all_gather(row_emb.astype(jnp.bfloat16), 'col', axis=1, tiled=True)  166 us
    all_gather x2, blocking collectives, on_device(): lax.all_gather(col_emb.astype(jnp.bfloat16), 'row', axis=1, tiled=True)  85.2 us
  transfers between devices with their start and end apart: 4, of which 2 were waited for; matrix products, arithmetic and copies ran while one was open for 1% of the time, Pallas kernels for 0%

commit v1 on v0

v1 whole, which is shorter than its diff:
```python
import jax
import jax.numpy as jnp
from jax import lax
from jax.sharding import PartitionSpec as P


def pair_slope(score, counts, log_row, log_col):
    values = counts.astype(jnp.float32)
    pmi = jnp.log(jnp.maximum(values, 1.0)) + 12.0 - log_row[:, None] - log_col[None, :]
    diff = score - pmi
    weight = 0.1 + 0.25 * jnp.sqrt(values)
    return jnp.where(counts > 0, weight * diff, jax.nn.sigmoid(diff))


def gather(shard, axis):
    size = lax.axis_size(axis)
    return lax.all_to_all(jnp.broadcast_to(shard[None], (size,) + shard.shape), axis, 0, 0)


def scatter_sum(parts, axis):
    return jnp.sum(lax.all_to_all(parts, axis, 0, 0).astype(jnp.float32), axis=0)


def adagrad(emb, acc, grad):
    acc = acc + grad * grad
    return (emb - 0.1 * grad / jnp.sqrt(acc), acc)


def on_device(row_emb, row_acc, col_emb, col_acc, counts, row_marg, col_marg):
    n_row, n_col = lax.axis_size("row"), lax.axis_size("col")
    width = row_emb.shape[0]
    rows, cols = counts.shape
    row_scale = 1.0 / jnp.sqrt(jnp.float32(cols * n_col))
    col_scale = 1.0 / jnp.sqrt(jnp.float32(rows * n_row))
    log_row = jnp.log(row_marg.astype(jnp.float32))
    log_col = jnp.log(col_marg.astype(jnp.float32))
    row_emb, row_acc = row_emb.T, row_acc.T
    for step in range(2):
        row_half = gather(row_emb.astype(jnp.bfloat16), "col").reshape(rows, width)
        col_half = gather(col_emb.astype(jnp.bfloat16), "row").transpose(1, 0, 2).reshape(width, cols)
        score = jnp.dot(row_half, col_half, preferred_element_type=jnp.float32)
        slope = pair_slope(score, counts, log_row, log_col).astype(jnp.bfloat16)
        grad_rows = lax.dot_general(
            slope, col_half, (((1,), (1,)), ((), ())), preferred_element_type=jnp.float32
        ).astype(jnp.bfloat16)
        grad_cols = lax.dot_general(
            row_half, slope, (((0,), (0,)), ((), ())), preferred_element_type=jnp.float32
        ).astype(jnp.bfloat16)
        row_grad = scatter_sum(grad_rows.reshape(n_col, rows // n_col, width), "col") * row_scale
        grad_cols = grad_cols.reshape(width, n_row, cols // n_row).transpose(1, 0, 2)
        col_grad = scatter_sum(grad_cols, "row") * col_scale
        row_emb, row_acc = adagrad(row_emb, row_acc, row_grad)
        col_emb, col_acc = adagrad(col_emb, col_acc, col_grad)
    return (row_emb.T, row_acc.T, col_emb, col_acc)


def solution(mesh):
    by_row, by_col = P(None, ("row", "col")), P(None, ("col", "row"))
    return jax.shard_map(
        on_device,
        mesh=mesh,
        in_specs=(by_row, by_row, by_col, by_col, P("row", "col"), P("row"), P("col")),
        out_specs=(by_row, by_row, by_col, by_col),
        check_vma=False,
    )
```

time: 1290 us -> 212 us (0.16)
  the two profiles are of different devices: /device:TPU:1 before, /device:TPU:8 now
where the time goes in v1:
time: 212 us; the launch traced here: 211 us
  waiting for transfers between devices  142 us (67%)
  starting transfers between devices  47.2 us (22%)
  matrix products  10.4 us (5%)
  local copies, waits for them, and re-layouts  7.98 us (4%)
  other arithmetic  2.78 us (1%)
    all_to_all x4, waiting for transfers between devices, gather(): lax.all_to_all(jnp.broadcast_to(shard[None], (size,) + shard.shape), axis...  72.2 us
    all_to_all x4, waiting for transfers between devices, scatter_sum(): lax.all_to_all(parts, axis, 0, 0).astype(jnp.float32)  69.8 us
    all_to_all x4, starting transfers between devices, gather(): lax.all_to_all(jnp.broadcast_to(shard[None], (size,) + shard.shape), axis...  29.4 us
    all_to_all x4, starting transfers between devices, scatter_sum(): lax.all_to_all(parts, axis, 0, 0).astype(jnp.float32)  17.9 us
    dot_general x2, matrix products, on_device(): score = jnp.dot(row_half, col_half, preferred_element_type=jnp.float32)  8.32 us
  transfers between devices with their start and end apart: 8, of which 8 were waited for; matrix products, arithmetic and copies ran while one was open for 2% of the time, Pallas kernels for 0%

profile of v1, /device:TPU:8, one launch (start us, length us, event | category | flops | bytes accessed | tf_op | source)
XLA Modules:
  0.0 211.4 jit_solution(13753757072518537689)
XLA Ops:
  0.7 0.9 convert_element_type.57
  1.6 0.9 broadcast_in_dim.9
  2.5 8.7 %all-to-all-start.1 = ((bf16[8,300,128]{2,1,0:T(8,128)(2,1)}), bf16[8,300,128]{2,1,0:T(8,128)(2,1)S(1)}, u32[]{:S(2)}, u32[]{:S(2)}) async-start(bf16[8,300,128]{2,1,0:T(8,128)(2,1)} %broadcast_in_dim.9), calls=%async_computation.1 | async-start | bytes 1245184 | tf_op jit(solution)/shard_map/all_to_all | solution.py:17
  11.2 21.7 %all-to-all-done.1 = bf16[8,300,128]{2,1,0:T(8,128)(2,1)S(1)} async-done(((bf16[8,300,128]{2,1,0:T(8,128)(2,1)}), bf16[8,300,128]{2,1,0:T(8,128)(2,1)S(1)}, u32[]{:S(2)}, u32[]{:S(2)}) %all-to-all-start.1) | async-done | bytes 614432 | tf_op jit(solution)/shard_map/all_to_all | solution.py:17
  33.7 12.5 %all-to-all-start = ((bf16[64,8,300]{2,1,0:T(8,128)(2,1)}), bf16[64,8,300]{2,1,0:T(8,128)(2,1)S(1)}, u32[]{:S(2)}, u32[]{:S(2)}) async-start(bf16[64,8,300]{2,1,0:T(8,128)(2,1)} %broadcast_in_dim.8), calls=%async_computation | async-start | bytes 786432 | tf_op jit(solution)/shard_map/all_to_all | solution.py:17
  46.5 14.1 %all-to-all-done = bf16[64,8,300]{2,1,0:T(8,128)(2,1)S(1)} async-done(((bf16[64,8,300]{2,1,0:T(8,128)(2,1)}), bf16[64,8,300]{2,1,0:T(8,128)(2,1)S(1)}, u32[]{:S(2)}, u32[]{:S(2)}) %all-to-all-start) | async-done | bytes 307232 | tf_op jit(solution)/shard_map/all_to_all | solution.py:17
  60.6 4.2 %select_convert_fusion.1 = bf16[512,1024]{1,0:T(8,128)(2,1)S(1)} fusion(s32[512,1024]{1,0:T(8,128)} %param.11, bf16[300,1024]{1,0:T(8,128)(2,1)S(1)} %bitcast.82, f32[1024]{0:T(1024)S(1)} %convert_log_fusion, f32[512]{0:T(512)S(1)} %convert_log_fusion.1, bf16[64,8,300]{2,1,0:T(8,128)(2,1)S(1)} %all-to-all-done), kind=kOutput, calls=%fused_computation.1 | convolution fusion | flops 322437120 | bytes 4073472 | tf_op jit(solution)/shard_map/dot_general | solution.py:41
  65.4 0.9 copy.26
  66.4 3.5 %all-to-all-start.4 = ((bf16[8,300,128]{2,1,0:T(8,128)(2,1)}), bf16[8,300,128]{2,1,0:T(8,128)(2,1)S(1)}, u32[]{:S(2)}, u32[]{:S(2)}) async-start(bf16[8,300,128]{2,1,0:T(8,128)(2,1)} %bitcast.73), calls=%async_computation.4 | async-start | bytes 1245184 | tf_op jit(solution)/shard_map/all_to_all | solution.py:21
  70.5 0.9 copy.14
  71.4 21.0 %all-to-all-done.4 = bf16[8,300,128]{2,1,0:T(8,128)(2,1)S(1)} async-done(((bf16[8,300,128]{2,1,0:T(8,128)(2,1)}), bf16[8,300,128]{2,1,0:T(8,128)(2,1)S(1)}, u32[]{:S(2)}, u32[]{:S(2)}) %all-to-all-start.4) | async-done | bytes 614432 | tf_op jit(solution)/shard_map/all_to_all | solution.py:21
  92.4 4.8 %all-to-all-start.2 = ((bf16[64,8,300]{2,1,0:T(8,128)(2,1)}), bf16[64,8,300]{2,1,0:T(8,128)(2,1)S(1)}, u32[]{:S(2)}, u32[]{:S(2)}) async-start(bf16[64,8,300]{2,1,0:T(8,128)(2,1)} %bitcast.3), calls=%async_computation.2 | async-start | bytes 786432 | tf_op jit(solution)/shard_map/all_to_all | solution.py:21
  97.4 14.3 %all-to-all-done.2 = bf16[64,8,300]{2,1,0:T(8,128)(2,1)S(1)} async-done(((bf16[64,8,300]{2,1,0:T(8,128)(2,1)}), bf16[64,8,300]{2,1,0:T(8,128)(2,1)S(1)}, u32[]{:S(2)}, u32[]{:S(2)}) %all-to-all-start.2) | async-done | bytes 307232 | tf_op jit(solution)/shard_map/all_to_all | solution.py:21
  112.5 3.5 %all-to-all-start.5 = ((bf16[8,300,128]{2,1,0:T(8,128)(2,1)}), bf16[8,300,128]{2,1,0:T(8,128)(2,1)S(1)}, u32[]{:S(2)}, u32[]{:S(2)}) async-start(bf16[8,300,128]{2,1,0:T(8,128)(2,1)} %broadcast_in_dim.11), calls=%async_computation.5 | async-start | bytes 1245184 | tf_op jit(solution)/shard_map/all_to_all | solution.py:17
  116.2 22.3 %all-to-all-done.5 = bf16[8,300,128]{2,1,0:T(8,128)(2,1)S(1)} async-done(((bf16[8,300,128]{2,1,0:T(8,128)(2,1)}), bf16[8,300,128]{2,1,0:T(8,128)(2,1)S(1)}, u32[]{:S(2)}, u32[]{:S(2)}) %all-to-all-start.5) | async-done | bytes 614432 | tf_op jit(solution)/shard_map/all_to_all | solution.py:17
  139.3 4.7 %all-to-all-start.3 = ((bf16[64,8,300]{2,1,0:T(8,128)(2,1)}), bf16[64,8,300]{2,1,0:T(8,128)(2,1)S(1)}, u32[]{:S(2)}, u32[]{:S(2)}) async-start(bf16[64,8,300]{2,1,0:T(8,128)(2,1)} %broadcast_in_dim.10), calls=%async_computation.3 | async-start | bytes 786432 | tf_op jit(solution)/shard_map/all_to_all | solution.py:17
  144.3 14.1 %all-to-all-done.3 = bf16[64,8,300]{2,1,0:T(8,128)(2,1)S(1)} async-done(((bf16[64,8,300]{2,1,0:T(8,128)(2,1)}), bf16[64,8,300]{2,1,0:T(8,128)(2,1)S(1)}, u32[]{:S(2)}, u32[]{:S(2)}) %all-to-all-start.3) | async-done | bytes 307232 | tf_op jit(solution)/shard_map/all_to_all | solution.py:17
  158.5 4.2 %select_convert_fusion = bf16[512,1024]{1,0:T(8,128)(2,1)S(1)} fusion(s32[512,1024]{1,0:T(8,128)} %param.11, bf16[300,1024]{1,0:T(8,128)(2,1)S(1)} %bitcast.84, f32[1024]{0:T(1024)S(1)} %convert_log_fusion, f32[512]{0:T(512)S(1)} %convert_log_fusion.1, bf16[64,8,300]{2,1,0:T(8,128)(2,1)S(1)} %all-to-all-done.3), kind=kOutput, calls=%fused_computation | convolution fusion | flops 322437120 | bytes 4073472 | tf_op jit(solution)/shard_map/dot_general | solution.py:41
  163.2 0.9 copy.17
  164.1 6.0 %all-to-all-start.6 = ((bf16[64,8,300]{2,1,0:T(8,128)(2,1)}), bf16[64,8,300]{2,1,0:T(8,128)(2,1)S(1)}, u32[]{:S(2)}, u32[]{:S(2)}) async-start(bf16[64,8,300]{2,1,0:T(8,128)(2,1)} %bitcast.11), calls=%async_computation.6 | async-start | bytes 786432 | tf_op jit(solution)/shard_map/all_to_all | solution.py:21
  170.8 0.9 copy.25
  171.7 12.8 %all-to-all-done.6 = bf16[64,8,300]{2,1,0:T(8,128)(2,1)S(1)} async-done(((bf16[64,8,300]{2,1,0:T(8,128)(2,1)}), bf16[64,8,300]{2,1,0:T(8,128)(2,1)S(1)}, u32[]{:S(2)}, u32[]{:S(2)}) %all-to-all-start.6) | async-done | bytes 307232 | tf_op jit(solution)/shard_map/all_to_all | solution.py:21
  184.5 3.5 %all-to-all-start.7 = ((bf16[8,300,128]{2,1,0:T(8,128)(2,1)}), bf16[8,300,128]{2,1,0:T(8,128)(2,1)S(1)}, u32[]{:S(2)}, u32[]{:S(2)}) async-start(bf16[8,300,128]{2,1,0:T(8,128)(2,1)} %bitcast.72), calls=%async_computation.7 | async-start | bytes 1245184 | tf_op jit(solution)/shard_map/all_to_all | solution.py:21
  188.8 21.7 %all-to-all-done.7 = bf16[8,300,128]{2,1,0:T(8,128)(2,1)S(1)} async-done(((bf16[8,300,128]{2,1,0:T(8,128)(2,1)}), bf16[8,300,128]{2,1,0:T(8,128)(2,1)S(1)}, u32[]{:S(2)}, u32[]{:S(2)}) %all-to-all-start.7) | async-done | bytes 614432 | tf_op jit(solution)/shard_map/all_to_all | solution.py:21
  (42 shorter events, 7.3 us)
Async XLA Ops:
  0.6 10.6 %copy-start.2 = (f32[300,8]{0,1:T(8,128)S(1)}, f32[300,8]{0,1:T(8,128)}, u32[]{:S(2)}) copy-start(f32[300,8]{0,1:T(8,128)} %param.7) | copy-start | bytes 28804
  0.6 45.5 %copy-start.6 = (s32[512]{0:T(512)S(1)}, s32[512]{0:T(512)}, u32[]{:S(2)}) copy-start(s32[512]{0:T(512)} %param.12) | copy-start | bytes 6148
  0.7 45.5 %copy-start.5 = (s32[1024]{0:T(1024)S(1)}, s32[1024]{0:T(1024)}, u32[]{:S(2)}) copy-start(s32[1024]{0:T(1024)} %param.13) | copy-start | bytes 12292
  2.5 30.4 %all-to-all-start.1 = ((bf16[8,300,128]{2,1,0:T(8,128)(2,1)}), bf16[8,300,128]{2,1,0:T(8,128)(2,1)S(1)}, u32[]{:S(2)}, u32[]{:S(2)}) async-start(bf16[8,300,128]{2,1,0:T(8,128)(2,1)} %broadcast_in_dim.9), calls=%async_computation.1 | async-start | bytes 1245184 | tf_op jit(solution)/shard_map/all_to_all | solution.py:17
  33.7 26.9 %all-to-all-start = ((bf16[64,8,300]{2,1,0:T(8,128)(2,1)}), bf16[64,8,300]{2,1,0:T(8,128)(2,1)S(1)}, u32[]{:S(2)}, u32[]{:S(2)}) async-start(bf16[64,8,300]{2,1,0:T(8,128)(2,1)} %broadcast_in_dim.8), calls=%async_computation | async-start | bytes 786432 | tf_op jit(solution)/shard_map/all_to_all | solution.py:17
  66.4 26.0 %all-to-all-start.4 = ((bf16[8,300,128]{2,1,0:T(8,128)(2,1)}), bf16[8,300,128]{2,1,0:T(8,128)(2,1)S(1)}, u32[]{:S(2)}, u32[]{:S(2)}) async-start(bf16[8,300,128]{2,1,0:T(8,128)(2,1)} %bitcast.73), calls=%async_computation.4 | async-start | bytes 1245184 | tf_op jit(solution)/shard_map/all_to_all | solution.py:21
  69.9 27.4 %copy-start = (f32[300,128]{1,0:T(8,128)S(1)}, f32[300,128]{1,0:T(8,128)}, u32[]{:S(2)}) copy-start(f32[300,128]{1,0:T(8,128)} %param.9) | copy-start | bytes 460804
  69.9 27.4 %copy-start.1 = (f32[300,128]{1,0:T(8,128)S(1)}, f32[300,128]{1,0:T(8,128)}, u32[]{:S(2)}) copy-start(f32[300,128]{1,0:T(8,128)} %param.10) | copy-start | bytes 460804
  92.4 23.8 %copy-start.4 = (f32[300,8]{0,1:T(8,128)S(1)}, f32[300,8]{0,1:T(8,128)}, u32[]{:S(2)}) copy-start(f32[300,8]{0,1:T(8,128)} %param.8) | copy-start | bytes 28804
  92.4 19.3 %all-to-all-start.2 = ((bf16[64,8,300]{2,1,0:T(8,128)(2,1)}), bf16[64,8,300]{2,1,0:T(8,128)(2,1)S(1)}, u32[]{:S(2)}, u32[]{:S(2)}) async-start(bf16[64,8,300]{2,1,0:T(8,128)(2,1)} %bitcast.3), calls=%async_computation.2 | async-start | bytes 786432 | tf_op jit(solution)/shard_map/all_to_all | solution.py:21
  112.5 26.0 %all-to-all-start.5 = ((bf16[8,300,128]{2,1,0:T(8,128)(2,1)}), bf16[8,300,128]{2,1,0:T(8,128)(2,1)S(1)}, u32[]{:S(2)}, u32[]{:S(2)}) async-start(bf16[8,300,128]{2,1,0:T(8,128)(2,1)} %broadcast_in_dim.11), calls=%async_computation.5 | async-start | bytes 1245184 | tf_op jit(solution)/shard_map/all_to_all | solution.py:17
  139.3 19.1 %all-to-all-start.3 = ((bf16[64,8,300]{2,1,0:T(8,128)(2,1)}), bf16[64,8,300]{2,1,0:T(8,128)(2,1)S(1)}, u32[]{:S(2)}, u32[]{:S(2)}) async-start(bf16[64,8,300]{2,1,0:T(8,128)(2,1)} %broadcast_in_dim.10), calls=%async_computation.3 | async-start | bytes 786432 | tf_op jit(solution)/shard_map/all_to_all | solution.py:17
  164.1 20.4 %all-to-all-start.6 = ((bf16[64,8,300]{2,1,0:T(8,128)(2,1)}), bf16[64,8,300]{2,1,0:T(8,128)(2,1)S(1)}, u32[]{:S(2)}, u32[]{:S(2)}) async-start(bf16[64,8,300]{2,1,0:T(8,128)(2,1)} %bitcast.11), calls=%async_computation.6 | async-start | bytes 786432 | tf_op jit(solution)/shard_map/all_to_all | solution.py:21
  170.7 17.5 %copy-start.3 = (f32[300,8]{0,1:T(8,128)S(1)}, f32[300,8]{0,1:T(8,128)}, u32[]{:S(2)}) copy-start(f32[300,8]{0,1:T(8,128)} %param.7) | copy-start | bytes 28804
  184.5 26.0 %all-to-all-start.7 = ((bf16[8,300,128]{2,1,0:T(8,128)(2,1)}), bf16[8,300,128]{2,1,0:T(8,128)(2,1)S(1)}, u32[]{:S(2)}, u32[]{:S(2)}) async-start(bf16[8,300,128]{2,1,0:T(8,128)(2,1)} %bitcast.72), calls=%async_computation.7 | async-start | bytes 1245184 | tf_op jit(solution)/shard_map/all_to_all | solution.py:21

commit v2 on v1

v2 whole, which is shorter than its diff:
```python
import jax
import jax.numpy as jnp
from jax import lax
from jax.experimental import pallas as pl
from jax.experimental.pallas import tpu as pltpu
from jax.sharding import PartitionSpec as P

ROW_TILE = 128
VMEM_LIMIT = 24 * 1024 * 1024


def tile_kernel(place, rows_in, piece0, piece1, piece2, piece3, counts_in, row_term_in, col_term_in,
                rows_out, grad0, grad1, grad2, grad3,
                rows, rows_t, cols, counts, row_term, col_term, slope,
                grad_rows, grad_own, grad_away, in_sem, out_sem):
    n_rows = rows.shape[0]
    wide = piece0.shape[1]
    pieces = (piece0, piece1, piece2, piece3)
    outs = (grad0, grad1, grad2, grad3)

    def start(source, target, sem):
        copy = pltpu.make_async_copy(source, target, sem)
        copy.start()
        return copy

    def there(d):
        return pl.ds(pl.multiple_of(lax.rem(place[0] + d, 4) * wide, wide), wide)

    here = [pl.ds(d * wide, wide) for d in range(4)]
    rows_copy = start(rows_in, rows, in_sem.at[0])
    cols_copy, counts_copy = [], []
    for d in range(4):
        cols_copy.append(start(pieces[d], cols.at[:, here[d]], in_sem.at[1 + d]))
        counts_copy.append(
            start(counts_in.at[:, there(d)], counts.at[:, here[d]], in_sem.at[5 + d])
        )
        if d == 0:
            row_copy = start(row_term_in, row_term, in_sem.at[9])
            col_copy = start(col_term_in, col_term, in_sem.at[10])
    rows_copy.wait()
    rows_t[...] = rows[...].T
    done = []
    for d in range(4):
        cols_copy[d].wait()
        counts_copy[d].wait()
        if d == 0:
            row_copy.wait()
            col_copy.wait()
        col_part = col_term[:, there(d)]
        for first in range(0, n_rows, ROW_TILE):
            at = pl.ds(first, ROW_TILE)
            score = jnp.dot(rows[at, :], cols[:, here[d]], preferred_element_type=jnp.float32)
            count = counts[at, here[d]]
            value = jnp.maximum(count.astype(jnp.float32), 1.0)
            diff = score - (jnp.log(value) + (row_term[at, :] - col_part))
            weight = 0.1 + 0.25 * (value * lax.rsqrt(value))
            zero = 0.5 * jnp.tanh(0.5 * diff) + 0.5
            slope[at, here[d]] = jnp.where(count > 0, weight * diff, zero).astype(jnp.bfloat16)
        grad = jnp.dot(rows_t[...], slope[:, here[d]], preferred_element_type=jnp.float32)
        if d == 0:
            grad_own[...] = grad
            done.append(start(grad_own, outs[0], out_sem.at[0]))
        else:
            grad_away[d - 1] = grad.astype(jnp.bfloat16)
            done.append(start(grad_away.at[d - 1], outs[d], out_sem.at[d]))
    grad_rows[...] = lax.dot_general(
        slope[...], cols[...], (((1,), (1,)), ((), ())), preferred_element_type=jnp.float32
    ).astype(jnp.bfloat16)
    done.append(start(grad_rows, rows_out, out_sem.at[4]))
    for copy in done:
        copy.wait()


def tile_grads(place, rows, pieces, counts, row_term, col_term):
    n_rows, width = rows.shape
    wide = pieces[0].shape[1]
    hbm = pl.BlockSpec(memory_space=pltpu.HBM)
    out = jax.ShapeDtypeStruct((width, wide), jnp.bfloat16)
    return pl.pallas_call(
        tile_kernel,
        in_specs=[pl.BlockSpec(memory_space=pltpu.SMEM)] + [hbm] * 8,
        out_specs=[hbm] * 5,
        out_shape=[
            jax.ShapeDtypeStruct((n_rows, width), jnp.bfloat16),
            jax.ShapeDtypeStruct((width, wide), jnp.float32),
            out, out, out,
        ],
        scratch_shapes=[
            pltpu.VMEM((n_rows, width), jnp.bfloat16),
            pltpu.VMEM((width, n_rows), jnp.bfloat16),
            pltpu.VMEM((width, 4 * wide), jnp.bfloat16),
            pltpu.VMEM((n_rows, 4 * wide), jnp.int32),
            pltpu.VMEM((n_rows, 1), jnp.float32),
            pltpu.VMEM((1, 4 * wide), jnp.float32),
            pltpu.VMEM((n_rows, 4 * wide), jnp.bfloat16),
            pltpu.VMEM((n_rows, width), jnp.bfloat16),
            pltpu.VMEM((width, wide), jnp.float32),
            pltpu.VMEM((3, width, wide), jnp.bfloat16),
            pltpu.SemaphoreType.DMA((11,)),
            pltpu.SemaphoreType.DMA((5,)),
        ],
        compiler_params=pltpu.CompilerParams(vmem_limit_bytes=VMEM_LIMIT),
        cost_estimate=pl.CostEstimate(
            flops=6 * n_rows * 4 * wide * width,
            bytes_accessed=4 * n_rows * 4 * wide,
            transcendentals=3 * n_rows * 4 * wide,
        ),
    )(place, rows, *pieces, counts, row_term, col_term)


def adagrad(emb, acc, grad):
    acc = acc + grad * grad
    return (emb - 0.1 * grad / jnp.sqrt(acc), acc)


def on_device(row_emb, row_acc, col_emb, col_acc, counts, row_marg, col_marg):
    n_row, n_col = lax.axis_size("row"), lax.axis_size("col")
    width = row_emb.shape[0]
    rows, cols = counts.shape
    half = cols // n_row
    row_scale = 1.0 / jnp.sqrt(jnp.float32(cols * n_col))
    col_scale = 1.0 / jnp.sqrt(jnp.float32(rows * n_row))
    me = lax.axis_index("row")
    odd = me % 2 == 1
    place = (me // 2).astype(jnp.int32)[None]
    row_term = (12.0 - jnp.log(row_marg.astype(jnp.float32)))[:, None]
    col_term = jnp.log(col_marg.astype(jnp.float32))[None, :]
    pair = [(i, i ^ 1) for i in range(n_row)]
    step_by = lambda d: [(i, (i // 2 + d) % 4 * 2 + i % 2) for i in range(n_row)]
    row_emb, row_acc = row_emb.T, row_acc.T
    for step in range(2):
        col_half = col_emb.astype(jnp.bfloat16)
        other = lax.ppermute(col_half, "row", pair)
        row_half = jnp.broadcast_to(row_emb.astype(jnp.bfloat16)[None], (n_col,) + row_emb.shape)
        row_half = lax.all_to_all(row_half, "col", 0, 0).reshape(rows, width)
        mine = jnp.concatenate(
            [jnp.where(odd, other, col_half), jnp.where(odd, col_half, other)], axis=1
        )
        pieces = [mine] + [lax.ppermute(mine, "row", step_by(-d)) for d in (1, 2, 3)]
        grads = tile_grads(place, row_half, pieces, counts, row_term, col_term)
        parts = lax.all_to_all(grads[0].reshape(n_col, rows // n_col, width), "col", 0, 0)
        row_grad = jnp.sum(parts.astype(jnp.float32), axis=0) * row_scale
        col_sum = grads[1]
        for d in (1, 2, 3):
            col_sum = col_sum + lax.ppermute(grads[1 + d], "row", step_by(d)).astype(jnp.float32)
        low, high = col_sum[:, :half], col_sum[:, half:]
        away = jnp.where(odd, low, high).astype(jnp.bfloat16)
        col_grad = jnp.where(odd, high, low) + lax.ppermute(away, "row", pair).astype(jnp.float32)
        row_emb, row_acc = adagrad(row_emb, row_acc, row_grad)
        col_emb, col_acc = adagrad(col_emb, col_acc, col_grad * col_scale)
    return (row_emb.T, row_acc.T, col_emb, col_acc)


def solution(mesh):
    by_row, by_col = P(None, ("row", "col")), P(None, ("col", "row"))
    return jax.shard_map(
        on_device,
        mesh=mesh,
        in_specs=(by_row, by_row, by_col, by_col, P("row", "col"), P("row"), P("col")),
        out_specs=(by_row, by_row, by_col, by_col),
        check_vma=False,
    )
```

time: 212 us -> 172 us (0.81)
  the two profiles are of different devices: /device:TPU:8 before, /device:TPU:1 now
where the time goes in v2:
time: 172 us; the launch traced here: 171 us
  starting transfers between devices  107 us (62%)
  waiting for transfers between devices  33.7 us (20%)
  Pallas kernels  11.3 us (7%)
  other arithmetic  8.76 us (5%)
  local copies, waits for them, and re-layouts  8.74 us (5%)
    all_to_all x2, starting transfers between devices, on_device(): lax.all_to_all(grads[0].reshape(n_col, rows // n_col, width), 'col', 0, 0)  26.8 us
    ppermute x6, starting transfers between devices, on_device(): lax.ppermute(grads[1 + d], 'row', step_by(d)).astype(jnp.float32)  21.1 us
    ppermute x6, starting transfers between devices, on_device(): lax.ppermute(mine, 'row', step_by(-d))  19.3 us
    all_to_all x2, starting transfers between devices, on_device(): row_half = lax.all_to_all(row_half, 'col', 0, 0).reshape(rows, width)  18 us
    all_to_all x2, waiting for transfers between devices, on_device(): lax.all_to_all(grads[0].reshape(n_col, rows // n_col, width), 'col', 0, 0)  16 us
    ppermute x2, starting transfers between devices, on_device(): other = lax.ppermute(col_half, 'row', pair)  12.7 us
    pallas_call x2, Pallas kernels, tile_grads(): pl.pallas_call(tile_kernel, in_specs=[pl.BlockSpec(memory_space=pltpu.SME...  11.3 us
    ppermute x2, starting transfers between devices, on_device(): lax.ppermute(away, 'row', pair).astype(jnp.float32)  9.09 us
  transfers between devices with their start and end apart: 20, of which 8 were waited for; matrix products, arithmetic and copies ran while one was open for 5% of the time, Pallas kernels for 0%

profile of v2, /device:TPU:1, one launch (start us, length us, event | category | flops | bytes accessed | tf_op | source)
XLA Modules:
  0.0 170.6 jit_solution(16921967821779775508)
XLA Ops:
  1.7 8.3 %collective-permute-start = (bf16[300,128]{1,0:T(8,128)(2,1)S(1)}, bf16[300,128]{1,0:T(8,128)(2,1)S(1)}, u32[]{:S(2)}, u32[]{:S(2)}) collective-permute-start(bf16[300,128]{1,0:T(8,128)(2,1)S(1)} %convert_element_type.55), channel_id=1, source_target_pairs={{0,64},{64,0},{128,192},{192,128},{256,320},{320,256},{384,448},{4... | collective-permute-start | bytes 230408 | tf_op jit(solution)/shard_map/ppermute | solution.py:133
  11.5 12.2 %all-to-all-start = ((bf16[64,8,300]{2,1,0:T(8,128)(2,1)}), bf16[64,8,300]{2,1,0:T(8,128)(2,1)S(1)}, u32[]{:S(2)}, u32[]{:S(2)}) async-start(bf16[64,8,300]{2,1,0:T(8,128)(2,1)} %broadcast_in_dim.22), calls=%async_computation | async-start | bytes 786432 | tf_op jit(solution)/shard_map/all_to_all | solution.py:135
  25.5 3.1 %collective-permute-start.3 = (bf16[300,256]{1,0:T(8,128)(2,1)S(1)}, bf16[300,256]{1,0:T(8,128)(2,1)S(1)}, u32[]{:S(2)}, u32[]{:S(2)}) collective-permute-start(bf16[300,256]{1,0:T(8,128)(2,1)S(1)} %pad_maximum_fusion.piece0), channel_id=1, source_target_pairs={{0,128},{64,192},{128,256},{192,320},{256,384},{320,448},{384,0},{... | collective-permute-start | bytes 460808 | tf_op jit(solution)/shard_map/ppermute | solution.py:139
  28.6 4.4 %collective-permute-start.2 = (bf16[300,256]{1,0:T(8,128)(2,1)S(1)}, bf16[300,256]{1,0:T(8,128)(2,1)S(1)}, u32[]{:S(2)}, u32[]{:S(2)}) collective-permute-start(bf16[300,256]{1,0:T(8,128)(2,1)S(1)} %pad_maximum_fusion.piece0), channel_id=1, source_target_pairs={{0,256},{64,320},{128,384},{192,448},{256,0},{320,64},{384,128},{4... | collective-permute-start | bytes 460808 | tf_op jit(solution)/shard_map/ppermute | solution.py:139
  33.0 3.1 %collective-permute-start.1 = (bf16[300,256]{1,0:T(8,128)(2,1)S(1)}, bf16[300,256]{1,0:T(8,128)(2,1)S(1)}, u32[]{:S(2)}, u32[]{:S(2)}) collective-permute-start(bf16[300,256]{1,0:T(8,128)(2,1)S(1)} %pad_maximum_fusion.piece0), channel_id=1, source_target_pairs={{0,384},{64,448},{128,0},{192,64},{256,128},{320,192},{384,256},{4... | collective-permute-start | bytes 460808 | tf_op jit(solution)/shard_map/ppermute | solution.py:139
  41.9 5.6 %shard_map.102 = (bf16[512,300]{1,0:T(8,128)(2,1)}, f32[300,256]{1,0:T(8,128)S(1)}, bf16[300,256]{1,0:T(8,128)(2,1)}, bf16[300,256]{1,0:T(8,128)(2,1)}, bf16[300,256]{1,0:T(8,128)(2,1)S(1)}) custom-call(s32[1]{0:T(128)} %bitcast.place, bf16[512,300]{1,0:T(8,128)(2,1)S(1)} %bitcast.40, bf16[300,256]{1,0:T(8,128)(2,1)S(1)} %pad_maximum_fusion.piece0, ...), custom_call_target="tpu_custom_call" | custom-call | flops 943718400 | bytes 2097152 | tf_op jit(solution)/shard_map/pallas_call | solution.py:79
  47.6 4.7 %collective-permute-start.4 = (bf16[300,256]{1,0:T(8,128)(2,1)}, bf16[300,256]{1,0:T(8,128)(2,1)}, u32[]{:S(2)}, u32[]{:S(2)}) collective-permute-start(bf16[300,256]{1,0:T(8,128)(2,1)} %get-tuple-element.16), channel_id=1, source_target_pairs={{0,128},{64,192},{128,256},{192,320},{256,384},{320,448},{384,0},{... | collective-permute-start | bytes 460808 | tf_op jit(solution)/shard_map/ppermute | solution.py:145
  54.9 3.7 %collective-permute-start.6 = (bf16[300,256]{1,0:T(8,128)(2,1)S(1)}, bf16[300,256]{1,0:T(8,128)(2,1)S(1)}, u32[]{:S(2)}, u32[]{:S(2)}) collective-permute-start(bf16[300,256]{1,0:T(8,128)(2,1)S(1)} %get-tuple-element.18), channel_id=1, source_target_pairs={{0,384},{64,448},{128,0},{192,64},{256,128},{320,192},{384,256},{4... | collective-permute-start | bytes 460808 | tf_op jit(solution)/shard_map/ppermute | solution.py:145
  58.6 12.2 %all-to-all-start.1 = ((bf16[64,8,300]{2,1,0:T(8,128)(2,1)}), bf16[64,8,300]{2,1,0:T(8,128)(2,1)S(1)}, u32[]{:S(2)}, u32[]{:S(2)}) async-start(bf16[64,8,300]{2,1,0:T(8,128)(2,1)} %bitcast.5), calls=%async_computation.1 | async-start | bytes 786432 | tf_op jit(solution)/shard_map/all_to_all | solution.py:141
  72.6 4.5 %collective-permute-start.7 = (bf16[300,128]{1,0:T(8,128)(2,1)S(1)}, bf16[300,128]{1,0:T(8,128)(2,1)S(1)}, u32[]{:S(2)}, u32[]{:S(2)}) collective-permute-start(bf16[300,128]{1,0:T(8,128)(2,1)S(1)} %select_convert_fusion.1), channel_id=1, source_target_pairs={{0,64},{64,0},{128,192},{192,128},{256,320},{320,256},{384,448},{4... | collective-permute-start | bytes 230408 | tf_op jit(solution)/shard_map/ppermute | solution.py:148
  77.1 10.8 %all-to-all-done.1 = bf16[64,8,300]{2,1,0:T(8,128)(2,1)S(1)} async-done(((bf16[64,8,300]{2,1,0:T(8,128)(2,1)}), bf16[64,8,300]{2,1,0:T(8,128)(2,1)S(1)}, u32[]{:S(2)}, u32[]{:S(2)}) %all-to-all-start.1) | async-done | bytes 307232 | tf_op jit(solution)/shard_map/all_to_all | solution.py:141
  89.5 5.8 %all-to-all-start.2 = ((bf16[64,8,300]{2,1,0:T(8,128)(2,1)}), bf16[64,8,300]{2,1,0:T(8,128)(2,1)S(1)}, u32[]{:S(2)}, u32[]{:S(2)}) async-start(bf16[64,8,300]{2,1,0:T(8,128)(2,1)} %broadcast_in_dim.25), calls=%async_computation.2 | async-start | bytes 786432 | tf_op jit(solution)/shard_map/all_to_all | solution.py:135
  97.0 4.4 %collective-permute-start.8 = (bf16[300,128]{1,0:T(8,128)(2,1)S(1)}, bf16[300,128]{1,0:T(8,128)(2,1)S(1)}, u32[]{:S(2)}, u32[]{:S(2)}) collective-permute-start(bf16[300,128]{1,0:T(8,128)(2,1)S(1)} %get-tuple-element.28), channel_id=1, source_target_pairs={{0,64},{64,0},{128,192},{192,128},{256,320},{320,256},{384,448},{4... | collective-permute-start | bytes 230408 | tf_op jit(solution)/shard_map/ppermute | solution.py:133
  101.4 4.9 %collective-permute-done.8 = bf16[300,128]{1,0:T(8,128)(2,1)S(1)} collective-permute-done((bf16[300,128]{1,0:T(8,128)(2,1)S(1)}, bf16[300,128]{1,0:T(8,128)(2,1)S(1)}, u32[]{:S(2)}, u32[]{:S(2)}) %collective-permute-start.8) | collective-permute-done | bytes 76832 | tf_op jit(solution)/shard_map/ppermute | solution.py:133
  106.4 2.6 %collective-permute-start.11 = (bf16[300,256]{1,0:T(8,128)(2,1)S(1)}, bf16[300,256]{1,0:T(8,128)(2,1)S(1)}, u32[]{:S(2)}, u32[]{:S(2)}) collective-permute-start(bf16[300,256]{1,0:T(8,128)(2,1)S(1)} %pad_maximum_fusion.1.piece0), channel_id=1, source_target_pairs={{0,128},{64,192},{128,256},{192,320},{256,384},{320,448},{384,0},{... | collective-permute-start | bytes 460808 | tf_op jit(solution)/shard_map/ppermute | solution.py:139
  109.0 3.0 %collective-permute-start.10 = (bf16[300,256]{1,0:T(8,128)(2,1)S(1)}, bf16[300,256]{1,0:T(8,128)(2,1)S(1)}, u32[]{:S(2)}, u32[]{:S(2)}) collective-permute-start(bf16[300,256]{1,0:T(8,128)(2,1)S(1)} %pad_maximum_fusion.1.piece0), channel_id=1, source_target_pairs={{0,256},{64,320},{128,384},{192,448},{256,0},{320,64},{384,128},{4... | collective-permute-start | bytes 460808 | tf_op jit(solution)/shard_map/ppermute | solution.py:139
  112.0 3.2 %collective-permute-start.9 = (bf16[300,256]{1,0:T(8,128)(2,1)S(1)}, bf16[300,256]{1,0:T(8,128)(2,1)S(1)}, u32[]{:S(2)}, u32[]{:S(2)}) collective-permute-start(bf16[300,256]{1,0:T(8,128)(2,1)S(1)} %pad_maximum_fusion.1.piece0), channel_id=1, source_target_pairs={{0,384},{64,448},{128,0},{192,64},{256,128},{320,192},{384,256},{4... | collective-permute-start | bytes 460808 | tf_op jit(solution)/shard_map/ppermute | solution.py:139
  122.0 5.7 %shard_map.103 = (bf16[512,300]{1,0:T(8,128)(2,1)}, f32[300,256]{1,0:T(8,128)S(1)}, bf16[300,256]{1,0:T(8,128)(2,1)}, bf16[300,256]{1,0:T(8,128)(2,1)}, bf16[300,256]{1,0:T(8,128)(2,1)S(1)}) custom-call(s32[1]{0:T(128)} %bitcast.place, bf16[512,300]{1,0:T(8,128)(2,1)S(1)} %bitcast.41, bf16[300,256]{1,0:T(8,128)(2,1)S(1)} %pad_maximum_fusion.1.piece0, ...), custom_call_target="tpu_custom_call" | custom-call | flops 943718400 | bytes 2097152 | tf_op jit(solution)/shard_map/pallas_call | solution.py:79
  127.8 2.8 %collective-permute-start.12 = (bf16[300,256]{1,0:T(8,128)(2,1)}, bf16[300,256]{1,0:T(8,128)(2,1)S(1)}, u32[]{:S(2)}, u32[]{:S(2)}) collective-permute-start(bf16[300,256]{1,0:T(8,128)(2,1)} %get-tuple-element.21), channel_id=1, source_target_pairs={{0,128},{64,192},{128,256},{192,320},{256,384},{320,448},{384,0},{... | collective-permute-start | bytes 460808 | tf_op jit(solution)/shard_map/ppermute | solution.py:145
  130.6 5.4 %collective-permute-start.13 = (bf16[300,256]{1,0:T(8,128)(2,1)}, bf16[300,256]{1,0:T(8,128)(2,1)S(1)}, u32[]{:S(2)}, u32[]{:S(2)}) collective-permute-start(bf16[300,256]{1,0:T(8,128)(2,1)} %get-tuple-element.22), channel_id=1, source_target_pairs={{0,256},{64,320},{128,384},{192,448},{256,0},{320,64},{384,128},{4... | collective-permute-start | bytes 460808 | tf_op jit(solution)/shard_map/ppermute | solution.py:145
  137.9 14.6 %all-to-all-start.3 = ((bf16[64,8,300]{2,1,0:T(8,128)(2,1)}), bf16[64,8,300]{2,1,0:T(8,128)(2,1)S(1)}, u32[]{:S(2)}, u32[]{:S(2)}) async-start(bf16[64,8,300]{2,1,0:T(8,128)(2,1)} %bitcast.10), calls=%async_computation.3 | async-start | bytes 786432 | tf_op jit(solution)/shard_map/all_to_all | solution.py:141
  152.7 4.6 %collective-permute-start.15 = (bf16[300,128]{1,0:T(8,128)(2,1)S(1)}, bf16[300,128]{1,0:T(8,128)(2,1)S(1)}, u32[]{:S(2)}, u32[]{:S(2)}) collective-permute-start(bf16[300,128]{1,0:T(8,128)(2,1)S(1)} %select_convert_fusion), channel_id=1, source_target_pairs={{0,64},{64,0},{128,192},{192,128},{256,320},{320,256},{384,448},{4... | collective-permute-start | bytes 230408 | tf_op jit(solution)/shard_map/ppermute | solution.py:148
  157.3 6.6 %collective-permute-done.15 = bf16[300,128]{1,0:T(8,128)(2,1)S(1)} collective-permute-done((bf16[300,128]{1,0:T(8,128)(2,1)S(1)}, bf16[300,128]{1,0:T(8,128)(2,1)S(1)}, u32[]{:S(2)}, u32[]{:S(2)}) %collective-permute-start.15) | collective-permute-done | bytes 76832 | tf_op jit(solution)/shard_map/ppermute | solution.py:148
  164.7 5.2 %all-to-all-done.3 = bf16[64,8,300]{2,1,0:T(8,128)(2,1)S(1)} async-done(((bf16[64,8,300]{2,1,0:T(8,128)(2,1)}), bf16[64,8,300]{2,1,0:T(8,128)(2,1)S(1)}, u32[]{:S(2)}, u32[]{:S(2)}) %all-to-all-start.3) | async-done | bytes 307232 | tf_op jit(solution)/shard_map/all_to_all | solution.py:141
  (79 shorter events, 28.3 us)
Async XLA Ops:
  0.6 39.4 %copy-start = (s32[512,1024]{1,0:T(8,128)S(1)}, s32[512,1024]{1,0:T(8,128)}, u32[]{:S(2)}) copy-start(s32[512,1024]{1,0:T(8,128)} %counts_in.3) | copy-start | bytes 6291460
  1.7 22.8 %collective-permute-start = (bf16[300,128]{1,0:T(8,128)(2,1)S(1)}, bf16[300,128]{1,0:T(8,128)(2,1)S(1)}, u32[]{:S(2)}, u32[]{:S(2)}) collective-permute-start(bf16[300,128]{1,0:T(8,128)(2,1)S(1)} %convert_element_type.55), channel_id=1, source_target_pairs={{0,64},{64,0},{128,192},{192,128},{256,320},{320,256},{384,448},{4... | collective-permute-start | bytes 230408 | tf_op jit(solution)/shard_map/ppermute | solution.py:133
  11.5 28.6 %all-to-all-start = ((bf16[64,8,300]{2,1,0:T(8,128)(2,1)}), bf16[64,8,300]{2,1,0:T(8,128)(2,1)S(1)}, u32[]{:S(2)}, u32[]{:S(2)}) async-start(bf16[64,8,300]{2,1,0:T(8,128)(2,1)} %broadcast_in_dim.22), calls=%async_computation | async-start | bytes 786432 | tf_op jit(solution)/shard_map/all_to_all | solution.py:135
  25.5 10.6 %collective-permute-start.3 = (bf16[300,256]{1,0:T(8,128)(2,1)S(1)}, bf16[300,256]{1,0:T(8,128)(2,1)S(1)}, u32[]{:S(2)}, u32[]{:S(2)}) collective-permute-start(bf16[300,256]{1,0:T(8,128)(2,1)S(1)} %pad_maximum_fusion.piece0), channel_id=1, source_target_pairs={{0,128},{64,192},{128,256},{192,320},{256,384},{320,448},{384,0},{... | collective-permute-start | bytes 460808 | tf_op jit(solution)/shard_map/ppermute | solution.py:139
  28.6 9.5 %collective-permute-start.2 = (bf16[300,256]{1,0:T(8,128)(2,1)S(1)}, bf16[300,256]{1,0:T(8,128)(2,1)S(1)}, u32[]{:S(2)}, u32[]{:S(2)}) collective-permute-start(bf16[300,256]{1,0:T(8,128)(2,1)S(1)} %pad_maximum_fusion.piece0), channel_id=1, source_target_pairs={{0,256},{64,320},{128,384},{192,448},{256,0},{320,64},{384,128},{4... | collective-permute-start | bytes 460808 | tf_op jit(solution)/shard_map/ppermute | solution.py:139
  33.0 6.4 %collective-permute-start.1 = (bf16[300,256]{1,0:T(8,128)(2,1)S(1)}, bf16[300,256]{1,0:T(8,128)(2,1)S(1)}, u32[]{:S(2)}, u32[]{:S(2)}) collective-permute-start(bf16[300,256]{1,0:T(8,128)(2,1)S(1)} %pad_maximum_fusion.piece0), channel_id=1, source_target_pairs={{0,384},{64,448},{128,0},{192,64},{256,128},{320,192},{384,256},{4... | collective-permute-start | bytes 460808 | tf_op jit(solution)/shard_map/ppermute | solution.py:139
  47.6 47.7 %copy-start.11 = (f32[300,128]{1,0:T(8,128)S(1)}, f32[300,128]{1,0:T(8,128)}, u32[]{:S(2)}) copy-start(f32[300,128]{1,0:T(8,128)} %param.9) | copy-start | bytes 460804
  47.6 23.2 %collective-permute-start.4 = (bf16[300,256]{1,0:T(8,128)(2,1)}, bf16[300,256]{1,0:T(8,128)(2,1)}, u32[]{:S(2)}, u32[]{:S(2)}) collective-permute-start(bf16[300,256]{1,0:T(8,128)(2,1)} %get-tuple-element.16), channel_id=1, source_target_pairs={{0,128},{64,192},{128,256},{192,320},{256,384},{320,448},{384,0},{... | collective-permute-start | bytes 460808 | tf_op jit(solution)/shard_map/ppermute | solution.py:145
  52.3 18.4 %collective-permute-start.5 = (bf16[300,256]{1,0:T(8,128)(2,1)}, bf16[300,256]{1,0:T(8,128)(2,1)}, u32[]{:S(2)}, u32[]{:S(2)}) collective-permute-start(bf16[300,256]{1,0:T(8,128)(2,1)} %get-tuple-element.17), channel_id=1, source_target_pairs={{0,256},{64,320},{128,384},{192,448},{256,0},{320,64},{384,128},{4... | collective-permute-start | bytes 460808 | tf_op jit(solution)/shard_map/ppermute | solution.py:145
  54.9 15.9 %collective-permute-start.6 = (bf16[300,256]{1,0:T(8,128)(2,1)S(1)}, bf16[300,256]{1,0:T(8,128)(2,1)S(1)}, u32[]{:S(2)}, u32[]{:S(2)}) collective-permute-start(bf16[300,256]{1,0:T(8,128)(2,1)S(1)} %get-tuple-element.18), channel_id=1, source_target_pairs={{0,384},{64,448},{128,0},{192,64},{256,128},{320,192},{384,256},{4... | collective-permute-start | bytes 460808 | tf_op jit(solution)/shard_map/ppermute | solution.py:145
  58.6 29.3 %all-to-all-start.1 = ((bf16[64,8,300]{2,1,0:T(8,128)(2,1)}), bf16[64,8,300]{2,1,0:T(8,128)(2,1)S(1)}, u32[]{:S(2)}, u32[]{:S(2)}) async-start(bf16[64,8,300]{2,1,0:T(8,128)(2,1)} %bitcast.5), calls=%async_computation.1 | async-start | bytes 786432 | tf_op jit(solution)/shard_map/all_to_all | solution.py:141
  72.6 22.7 %collective-permute-start.7 = (bf16[300,128]{1,0:T(8,128)(2,1)S(1)}, bf16[300,128]{1,0:T(8,128)(2,1)S(1)}, u32[]{:S(2)}, u32[]{:S(2)}) collective-permute-start(bf16[300,128]{1,0:T(8,128)(2,1)S(1)} %select_convert_fusion.1), channel_id=1, source_target_pairs={{0,64},{64,0},{128,192},{192,128},{256,320},{320,256},{384,448},{4... | collective-permute-start | bytes 230408 | tf_op jit(solution)/shard_map/ppermute | solution.py:148
  89.5 30.7 %all-to-all-start.2 = ((bf16[64,8,300]{2,1,0:T(8,128)(2,1)}), bf16[64,8,300]{2,1,0:T(8,128)(2,1)S(1)}, u32[]{:S(2)}, u32[]{:S(2)}) async-start(bf16[64,8,300]{2,1,0:T(8,128)(2,1)} %broadcast_in_dim.25), calls=%async_computation.2 | async-start | bytes 786432 | tf_op jit(solution)/shard_map/all_to_all | solution.py:135
  97.0 9.3 %collective-permute-start.8 = (bf16[300,128]{1,0:T(8,128)(2,1)S(1)}, bf16[300,128]{1,0:T(8,128)(2,1)S(1)}, u32[]{:S(2)}, u32[]{:S(2)}) collective-permute-start(bf16[300,128]{1,0:T(8,128)(2,1)S(1)} %get-tuple-element.28), channel_id=1, source_target_pairs={{0,64},{64,0},{128,192},{192,128},{256,320},{320,256},{384,448},{4... | collective-permute-start | bytes 230408 | tf_op jit(solution)/shard_map/ppermute | solution.py:133
  106.4 8.8 %collective-permute-start.11 = (bf16[300,256]{1,0:T(8,128)(2,1)S(1)}, bf16[300,256]{1,0:T(8,128)(2,1)S(1)}, u32[]{:S(2)}, u32[]{:S(2)}) collective-permute-start(bf16[300,256]{1,0:T(8,128)(2,1)S(1)} %pad_maximum_fusion.1.piece0), channel_id=1, source_target_pairs={{0,128},{64,192},{128,256},{192,320},{256,384},{320,448},{384,0},{... | collective-permute-start | bytes 460808 | tf_op jit(solution)/shard_map/ppermute | solution.py:139
  109.0 7.6 %collective-permute-start.10 = (bf16[300,256]{1,0:T(8,128)(2,1)S(1)}, bf16[300,256]{1,0:T(8,128)(2,1)S(1)}, u32[]{:S(2)}, u32[]{:S(2)}) collective-permute-start(bf16[300,256]{1,0:T(8,128)(2,1)S(1)} %pad_maximum_fusion.1.piece0), channel_id=1, source_target_pairs={{0,256},{64,320},{128,384},{192,448},{256,0},{320,64},{384,128},{4... | collective-permute-start | bytes 460808 | tf_op jit(solution)/shard_map/ppermute | solution.py:139
  112.0 7.5 %collective-permute-start.9 = (bf16[300,256]{1,0:T(8,128)(2,1)S(1)}, bf16[300,256]{1,0:T(8,128)(2,1)S(1)}, u32[]{:S(2)}, u32[]{:S(2)}) collective-permute-start(bf16[300,256]{1,0:T(8,128)(2,1)S(1)} %pad_maximum_fusion.1.piece0), channel_id=1, source_target_pairs={{0,384},{64,448},{128,0},{192,64},{256,128},{320,192},{384,256},{4... | collective-permute-start | bytes 460808 | tf_op jit(solution)/shard_map/ppermute | solution.py:139
  127.7 42.3 %copy-start.17 = (f32[300,8]{0,1:T(8,128)S(1)}, f32[300,8]{0,1:T(8,128)}, u32[]{:S(2)}) copy-start(f32[300,8]{0,1:T(8,128)} %param.7) | copy-start | bytes 28804
  127.7 42.2 %copy-start.18 = (f32[300,8]{0,1:T(8,128)S(1)}, f32[300,8]{0,1:T(8,128)}, u32[]{:S(2)}) copy-start(f32[300,8]{0,1:T(8,128)} %param.8) | copy-start | bytes 28804
  127.8 24.8 %collective-permute-start.12 = (bf16[300,256]{1,0:T(8,128)(2,1)}, bf16[300,256]{1,0:T(8,128)(2,1)S(1)}, u32[]{:S(2)}, u32[]{:S(2)}) collective-permute-start(bf16[300,256]{1,0:T(8,128)(2,1)} %get-tuple-element.21), channel_id=1, source_target_pairs={{0,128},{64,192},{128,256},{192,320},{256,384},{320,448},{384,0},{... | collective-permute-start | bytes 460808 | tf_op jit(solution)/shard_map/ppermute | solution.py:145
  130.6 21.9 %collective-permute-start.13 = (bf16[300,256]{1,0:T(8,128)(2,1)}, bf16[300,256]{1,0:T(8,128)(2,1)S(1)}, u32[]{:S(2)}, u32[]{:S(2)}) collective-permute-start(bf16[300,256]{1,0:T(8,128)(2,1)} %get-tuple-element.22), channel_id=1, source_target_pairs={{0,256},{64,320},{128,384},{192,448},{256,0},{320,64},{384,128},{4... | collective-permute-start | bytes 460808 | tf_op jit(solution)/shard_map/ppermute | solution.py:145
  136.0 16.5 %collective-permute-start.14 = (bf16[300,256]{1,0:T(8,128)(2,1)S(1)}, bf16[300,256]{1,0:T(8,128)(2,1)S(1)}, u32[]{:S(2)}, u32[]{:S(2)}) collective-permute-start(bf16[300,256]{1,0:T(8,128)(2,1)S(1)} %get-tuple-element.23), channel_id=1, source_target_pairs={{0,384},{64,448},{128,0},{192,64},{256,128},{320,192},{384,256},{4... | collective-permute-start | bytes 460808 | tf_op jit(solution)/shard_map/ppermute | solution.py:145
  137.9 31.9 %all-to-all-start.3 = ((bf16[64,8,300]{2,1,0:T(8,128)(2,1)}), bf16[64,8,300]{2,1,0:T(8,128)(2,1)S(1)}, u32[]{:S(2)}, u32[]{:S(2)}) async-start(bf16[64,8,300]{2,1,0:T(8,128)(2,1)} %bitcast.10), calls=%async_computation.3 | async-start | bytes 786432 | tf_op jit(solution)/shard_map/all_to_all | solution.py:141
  152.7 11.2 %collective-permute-start.15 = (bf16[300,128]{1,0:T(8,128)(2,1)S(1)}, bf16[300,128]{1,0:T(8,128)(2,1)S(1)}, u32[]{:S(2)}, u32[]{:S(2)}) collective-permute-start(bf16[300,128]{1,0:T(8,128)(2,1)S(1)} %select_convert_fusion), channel_id=1, source_target_pairs={{0,64},{64,0},{128,192},{192,128},{256,320},{320,256},{384,448},{4... | collective-permute-start | bytes 230408 | tf_op jit(solution)/shard_map/ppermute | solution.py:148
  (16 other events, 245.8 us)

commit v3 on v2

--- a/solution.py
+++ b/solution.py
@@ -1,3 +1,5 @@
+import functools
+
 import jax
 import jax.numpy as jnp
 from jax import lax
@@ -7,6 +9,8 @@
 
 ROW_TILE = 128
 VMEM_LIMIT = 24 * 1024 * 1024
+ROW_COST = 1 << 36
+PAIR_COST = 1 << 36
 
 
 def tile_kernel(place, rows_in, piece0, piece1, piece2, piece3, counts_in, row_term_in, col_term_in,
@@ -113,13 +117,40 @@
     return (emb - 0.1 * grad / jnp.sqrt(acc), acc)
 
 
+def whole_call(kernel, outs, cost, extra=None):
+    specs = {} if extra is None else {"in_specs": extra}
+    return pl.pallas_call(
+        kernel,
+        **specs,
+        out_shape=outs,
+        compiler_params=pltpu.CompilerParams(vmem_limit_bytes=VMEM_LIMIT),
+        cost_estimate=pl.CostEstimate(flops=cost, bytes_accessed=cost, transcendentals=cost >> 4),
+    )
+
+
+def row_kernel(scale, parts, emb, acc, after, emb_out, acc_out, send):
+    grad = jnp.sum(parts[...].astype(jnp.float32), axis=0) * scale
+    new_emb, new_acc = adagrad(emb[...], acc[...], grad)
+    emb_out[...] = new_emb
+    acc_out[...] = new_acc
+    send[...] = jnp.broadcast_to(new_emb.astype(jnp.bfloat16)[None], send.shape)
+
+
+def pair_kernel(scale, col_sum, away, emb, acc, emb_out, acc_out, send):
+    grad = (col_sum[...] + away[...].astype(jnp.float32)) * scale
+    new_emb, new_acc = adagrad(emb[...], acc[...], grad)
+    emb_out[...] = new_emb
+    acc_out[...] = new_acc
+    send[...] = new_emb.astype(jnp.bfloat16)
+
+
 def on_device(row_emb, row_acc, col_emb, col_acc, counts, row_marg, col_marg):
     n_row, n_col = lax.axis_size("row"), lax.axis_size("col")
     width = row_emb.shape[0]
     rows, cols = counts.shape
     half = cols // n_row
-    row_scale = 1.0 / jnp.sqrt(jnp.float32(cols * n_col))
-    col_scale = 1.0 / jnp.sqrt(jnp.float32(rows * n_row))
+    row_scale = float((cols * n_col) ** -0.5)
+    col_scale = float((rows * n_row) ** -0.5)
     me = lax.axis_index("row")
     odd = me % 2 == 1
     place = (me // 2).astype(jnp.int32)[None]
@@ -128,26 +159,49 @@
     pair = [(i, i ^ 1) for i in range(n_row)]
     step_by = lambda d: [(i, (i // 2 + d) % 4 * 2 + i % 2) for i in range(n_row)]
     row_emb, row_acc = row_emb.T, row_acc.T
+    full = lambda like, dtype=jnp.float32: jax.ShapeDtypeStruct(like, dtype)
+    to_all = full((n_col,) + row_emb.shape, jnp.bfloat16)
+    both = jnp.stack([col_emb.astype(jnp.bfloat16), col_acc.astype(jnp.bfloat16)])
+    row_send = jnp.broadcast_to(row_emb.astype(jnp.bfloat16)[None], to_all.shape)
+    other = lax.ppermute(both, "row", pair).astype(jnp.float32)
+    in_order = lambda mine, theirs: jnp.concatenate(
+        [jnp.where(odd, theirs, mine), jnp.where(odd, mine, theirs)], axis=1
+    )
+    pair_emb = in_order(col_emb, other[0])
+    pair_acc = in_order(col_acc, other[1])
+    pair_send = pair_emb.astype(jnp.bfloat16)
+    vmem = pl.BlockSpec(memory_space=pltpu.VMEM)
+    in_hbm = lambda values: pltpu.with_memory_space_constraint(values, pltpu.HBM)
+    own = lambda wide: jnp.where(odd, wide[:, half:], wide[:, :half])
     for step in range(2):
-        col_half = col_emb.astype(jnp.bfloat16)
-        other = lax.ppermute(col_half, "row", pair)
-        row_half = jnp.broadcast_to(row_emb.astype(jnp.bfloat16)[None], (n_col,) + row_emb.shape)
-        row_half = lax.all_to_all(row_half, "col", 0, 0).reshape(rows, width)
-        mine = jnp.concatenate(
-            [jnp.where(odd, other, col_half), jnp.where(odd, col_half, other)], axis=1
-        )
-        pieces = [mine] + [lax.ppermute(mine, "row", step_by(-d)) for d in (1, 2, 3)]
-        grads = tile_grads(place, row_half, pieces, counts, row_term, col_term)
+        row_half = lax.all_to_all(row_send, "col", 0, 0).reshape(rows, width)
+        pieces = [pair_send] + [lax.ppermute(pair_send, "row", step_by(-d)) for d in (1, 2, 3)]
+        grads = tile_grads(place, row_half, pieces, in_hbm(counts), row_term, col_term)
         parts = lax.all_to_all(grads[0].reshape(n_col, rows // n_col, width), "col", 0, 0)
-        row_grad = jnp.sum(parts.astype(jnp.float32), axis=0) * row_scale
         col_sum = grads[1]
         for d in (1, 2, 3):
             col_sum = col_sum + lax.ppermute(grads[1 + d], "row", step_by(d)).astype(jnp.float32)
-        low, high = col_sum[:, :half], col_sum[:, half:]
-        away = jnp.where(odd, low, high).astype(jnp.bfloat16)
-        col_grad = jnp.where(odd, high, low) + lax.ppermute(away, "row", pair).astype(jnp.float32)
-        row_emb, row_acc = adagrad(row_emb, row_acc, row_grad)
-        col_emb, col_acc = adagrad(col_emb, col_acc, col_grad * col_scale)
+        if step == 0:
+            half_sum = col_sum.astype(jnp.bfloat16)
+            away = lax.ppermute(half_sum, "row", pair)
+            row_emb, row_acc, row_send = whole_call(
+                functools.partial(row_kernel, row_scale),
+                [full(row_emb.shape), full(row_emb.shape), to_all],
+                ROW_COST,
+                [vmem, vmem, vmem, pl.BlockSpec(memory_space=pl.ANY)],
+            )(parts, row_emb, row_acc, half_sum)
+            pair_emb, pair_acc, pair_send = whole_call(
+                functools.partial(pair_kernel, col_scale),
+                [full(pair_emb.shape), full(pair_emb.shape), full(pair_emb.shape, jnp.bfloat16)],
+                PAIR_COST,
+            )(col_sum, away, pair_emb, pair_acc)
+        else:
+            row_grad = jnp.sum(parts.astype(jnp.float32), axis=0) * row_scale
+            row_emb, row_acc = adagrad(row_emb, row_acc, row_grad)
+            away = jnp.where(odd, col_sum[:, :half], col_sum[:, half:]).astype(jnp.bfloat16)
+            away = lax.ppermute(away, "row", pair).astype(jnp.float32)
+            col_grad = (own(col_sum) + away) * col_scale
+            col_emb, col_acc = adagrad(own(pair_emb), own(pair_acc), col_grad)
     return (row_emb.T, row_acc.T, col_emb, col_acc)
 
 

time: 172 us -> 153 us (0.89)
  waiting for transfers between devices: 33.7 us -> 22.2 us
  local copies, waits for them, and re-layouts: 8.74 us -> 1 us
  other arithmetic: 8.76 us -> 4.95 us
  Pallas kernels: 11.3 us -> 14.6 us
    all_to_all x2, waiting for transfers between devices: 16 us -> 5.15 us  [on_device(): lax.all_to_all(grads[0].reshape(n_col, rows // n_col, width), 'col', 0, 0)]
    unnamed x40 -> x18, local copies, waits for them, and re-layouts: 7.01 us -> 0.05 us
    all_to_all x2, starting transfers between devices: 18 us -> 24.9 us  [on_device(): row_half = lax.all_to_all(row_send, 'col', 0, 0).reshape(rows, width)]
    ppermute x10 -> x9, waiting for transfers between devices: 17.8 us -> 13.5 us  [the longest x6 6.89 us: on_device(): lax.ppermute(pair_send, 'row', step_by(-d))]
    ppermute x6, waiting for transfers between devices: 0.02 us -> 3.61 us  [on_device(): lax.ppermute(grads[1 + d], 'row', step_by(d)).astype(jnp.float32)]
    ppermute x10 -> x9, starting transfers between devices: 41.1 us -> 37.7 us  [the longest x6 20.3 us: on_device(): lax.ppermute(pair_send, 'row', step_by(-d))]
    pallas_call x0 -> x2, Pallas kernels: none -> 2.01 us  [the longest x1 1.13 us: on_device(): whole_call(functools.partial(pair_kernel, col_scale), [full(pair_emb.shap...]
    all_to_all x2, starting transfers between devices: 26.8 us -> 24.8 us  [on_device(): lax.all_to_all(grads[0].reshape(n_col, rows // n_col, width), 'col', 0, 0)]
  transfers between devices with their start and end apart: 20 -> 19, of which waited for: 8 -> 8; matrix products, arithmetic and copies ran while one was open for 5% -> 3% of each run, Pallas kernels for 0% -> 1%
where the time goes in v3:
time: 153 us; the launch traced here: 152 us
  starting transfers between devices  108 us (71%)
  waiting for transfers between devices  22.2 us (15%)
  Pallas kernels  14.6 us (10%)
  other arithmetic  4.95 us (3%)
    all_to_all x2, starting transfers between devices, on_device(): row_half = lax.all_to_all(row_send, 'col', 0, 0).reshape(rows, width)  24.9 us
    all_to_all x2, starting transfers between devices, on_device(): lax.all_to_all(grads[0].reshape(n_col, rows // n_col, width), 'col', 0, 0)  24.8 us
    ppermute x6, starting transfers between devices, on_device(): lax.ppermute(grads[1 + d], 'row', step_by(d)).astype(jnp.float32)  20.6 us
    ppermute x6, starting transfers between devices, on_device(): lax.ppermute(pair_send, 'row', step_by(-d))  20.3 us
    pallas_call x2, Pallas kernels, tile_grads(): pl.pallas_call(tile_kernel, in_specs=[pl.BlockSpec(memory_space=pltpu.SME...  12.6 us
    ppermute x1, starting transfers between devices, on_device(): other = lax.ppermute(both, 'row', pair).astype(jnp.float32)  8.28 us
    ppermute x6, waiting for transfers between devices, on_device(): lax.ppermute(pair_send, 'row', step_by(-d))  6.89 us
    ppermute x1, waiting for transfers between devices, on_device(): away = lax.ppermute(away, 'row', pair).astype(jnp.float32)  6.57 us
  transfers between devices with their start and end apart: 19, of which 8 were waited for; matrix products, arithmetic and copies ran while one was open for 3% of the time, Pallas kernels for 1%

profile of v3, /device:TPU:1, one launch (start us, length us, event | category | flops | bytes accessed | tf_op | source)
XLA Modules:
  0.0 151.8 jit_solution(4385924640952057733)
XLA Ops:
  1.7 8.3 %collective-permute-start = (bf16[2,300,128]{2,1,0:T(8,128)(2,1)S(1)}, bf16[2,300,128]{2,1,0:T(8,128)(2,1)S(1)}, u32[]{:S(2)}, u32[]{:S(2)}) collective-permute-start(bf16[2,300,128]{2,1,0:T(8,128)(2,1)S(1)} %pad_maximum_fusion.2), channel_id=1, source_target_pairs={{0,64},{64,0},{128,192},{192,128},{256,320},{320,256},{384,448},{4... | collective-permute-start | bytes 460808 | tf_op jit(solution)/shard_map/ppermute | solution.py:166
  11.5 12.2 %all-to-all-start = ((bf16[64,8,300]{2,1,0:T(8,128)(2,1)}), bf16[64,8,300]{2,1,0:T(8,128)(2,1)S(1)}, u32[]{:S(2)}, u32[]{:S(2)}) async-start(bf16[64,8,300]{2,1,0:T(8,128)(2,1)} %broadcast_in_dim.16), calls=%async_computation | async-start | bytes 786432 | tf_op jit(solution)/shard_map/all_to_all | solution.py:177
  24.7 3.1 %collective-permute-start.3 = (bf16[300,256]{1,0:T(8,128)(2,1)S(1)}, bf16[300,256]{1,0:T(8,128)(2,1)S(1)}, u32[]{:S(2)}, u32[]{:S(2)}) collective-permute-start(bf16[300,256]{1,0:T(8,128)(2,1)S(1)} %fusion.5.piece0), channel_id=1, source_target_pairs={{0,128},{64,192},{128,256},{192,320},{256,384},{320,448},{384,0},{... | collective-permute-start | bytes 460808 | tf_op jit(solution)/shard_map/ppermute | solution.py:178
  27.9 4.4 %collective-permute-start.2 = (bf16[300,256]{1,0:T(8,128)(2,1)S(1)}, bf16[300,256]{1,0:T(8,128)(2,1)S(1)}, u32[]{:S(2)}, u32[]{:S(2)}) collective-permute-start(bf16[300,256]{1,0:T(8,128)(2,1)S(1)} %fusion.5.piece0), channel_id=1, source_target_pairs={{0,256},{64,320},{128,384},{192,448},{256,0},{320,64},{384,128},{4... | collective-permute-start | bytes 460808 | tf_op jit(solution)/shard_map/ppermute | solution.py:178
  32.2 3.1 %collective-permute-start.1 = (bf16[300,256]{1,0:T(8,128)(2,1)S(1)}, bf16[300,256]{1,0:T(8,128)(2,1)S(1)}, u32[]{:S(2)}, u32[]{:S(2)}) collective-permute-start(bf16[300,256]{1,0:T(8,128)(2,1)S(1)} %fusion.5.piece0), channel_id=1, source_target_pairs={{0,384},{64,448},{128,0},{192,64},{256,128},{320,192},{384,256},{4... | collective-permute-start | bytes 460808 | tf_op jit(solution)/shard_map/ppermute | solution.py:178
  38.6 6.3 %shard_map.102 = (bf16[512,300]{1,0:T(8,128)(2,1)}, f32[300,256]{1,0:T(8,128)S(1)}, bf16[300,256]{1,0:T(8,128)(2,1)S(1)}, bf16[300,256]{1,0:T(8,128)(2,1)S(1)}, bf16[300,256]{1,0:T(8,128)(2,1)S(1)}) custom-call(s32[1]{0:T(128)} %bitcast.place, bf16[512,300]{1,0:T(8,128)(2,1)S(1)} %bitcast.30, bf16[300,256]{1,0:T(8,128)(2,1)S(1)} %fusion.5.piece0, ...), custom_call_target="tpu_custom_call" | custom-call | flops 943718400 | bytes 2097152 | tf_op jit(solution)/shard_map/pallas_call | solution.py:83
  45.0 12.3 %all-to-all-start.1 = ((bf16[64,8,300]{2,1,0:T(8,128)(2,1)}), bf16[64,8,300]{2,1,0:T(8,128)(2,1)S(1)}, u32[]{:S(2)}, u32[]{:S(2)}) async-start(bf16[64,8,300]{2,1,0:T(8,128)(2,1)} %bitcast.8), calls=%async_computation.1 | async-start | bytes 786432 | tf_op jit(solution)/shard_map/all_to_all | solution.py:180
  57.3 3.6 %collective-permute-start.4 = (bf16[300,256]{1,0:T(8,128)(2,1)S(1)}, bf16[300,256]{1,0:T(8,128)(2,1)S(1)}, u32[]{:S(2)}, u32[]{:S(2)}) collective-permute-start(bf16[300,256]{1,0:T(8,128)(2,1)S(1)} %get-tuple-element.22), channel_id=1, source_target_pairs={{0,128},{64,192},{128,256},{192,320},{256,384},{320,448},{384,0},{... | collective-permute-start | bytes 460808 | tf_op jit(solution)/shard_map/ppermute | solution.py:183
  60.9 3.8 %collective-permute-start.5 = (bf16[300,256]{1,0:T(8,128)(2,1)S(1)}, bf16[300,256]{1,0:T(8,128)(2,1)S(1)}, u32[]{:S(2)}, u32[]{:S(2)}) collective-permute-start(bf16[300,256]{1,0:T(8,128)(2,1)S(1)} %get-tuple-element.23), channel_id=1, source_target_pairs={{0,256},{64,320},{128,384},{192,448},{256,0},{320,64},{384,128},{4... | collective-permute-start | bytes 460808 | tf_op jit(solution)/shard_map/ppermute | solution.py:183
  64.7 2.7 %collective-permute-start.6 = (bf16[300,256]{1,0:T(8,128)(2,1)S(1)}, bf16[300,256]{1,0:T(8,128)(2,1)S(1)}, u32[]{:S(2)}, u32[]{:S(2)}) collective-permute-start(bf16[300,256]{1,0:T(8,128)(2,1)S(1)} %get-tuple-element.24), channel_id=1, source_target_pairs={{0,384},{64,448},{128,0},{192,64},{256,128},{320,192},{384,256},{4... | collective-permute-start | bytes 460808 | tf_op jit(solution)/shard_map/ppermute | solution.py:183
  71.9 4.4 %collective-permute-start.7 = (bf16[300,256]{1,0:T(8,128)(2,1)}, bf16[300,256]{1,0:T(8,128)(2,1)}, u32[]{:S(2)}, u32[]{:S(2)}) collective-permute-start(bf16[300,256]{1,0:T(8,128)(2,1)} %get-tuple-element.38.after), channel_id=1, source_target_pairs={{0,64},{64,0},{128,192},{192,128},{256,320},{320,256},{384,448},{4... | collective-permute-start | bytes 460808 | tf_op jit(solution)/shard_map/ppermute | solution.py:186
  77.2 12.7 %all-to-all-start.2 = ((bf16[64,8,300]{2,1,0:T(8,128)(2,1)}), bf16[64,8,300]{2,1,0:T(8,128)(2,1)}, u32[]{:S(2)}, u32[]{:S(2)}) async-start(bf16[64,8,300]{2,1,0:T(8,128)(2,1)} %get-tuple-element.26), calls=%async_computation.2 | async-start | bytes 786432 | tf_op jit(solution)/shard_map/all_to_all | solution.py:177
  91.1 3.3 %collective-permute-start.10 = (bf16[300,256]{1,0:T(8,128)(2,1)S(1)}, bf16[300,256]{1,0:T(8,128)(2,1)S(1)}, u32[]{:S(2)}, u32[]{:S(2)}) collective-permute-start(bf16[300,256]{1,0:T(8,128)(2,1)S(1)} %get-tuple-element.27.piece0), channel_id=1, source_target_pairs={{0,128},{64,192},{128,256},{192,320},{256,384},{320,448},{384,0},{... | collective-permute-start | bytes 460808 | tf_op jit(solution)/shard_map/ppermute | solution.py:178
  94.4 3.8 %collective-permute-start.9 = (bf16[300,256]{1,0:T(8,128)(2,1)S(1)}, bf16[300,256]{1,0:T(8,128)(2,1)S(1)}, u32[]{:S(2)}, u32[]{:S(2)}) collective-permute-start(bf16[300,256]{1,0:T(8,128)(2,1)S(1)} %get-tuple-element.27.piece0), channel_id=1, source_target_pairs={{0,256},{64,320},{128,384},{192,448},{256,0},{320,64},{384,128},{4... | collective-permute-start | bytes 460808 | tf_op jit(solution)/shard_map/ppermute | solution.py:178
  98.2 2.7 %collective-permute-start.8 = (bf16[300,256]{1,0:T(8,128)(2,1)S(1)}, bf16[300,256]{1,0:T(8,128)(2,1)S(1)}, u32[]{:S(2)}, u32[]{:S(2)}) collective-permute-start(bf16[300,256]{1,0:T(8,128)(2,1)S(1)} %get-tuple-element.27.piece0), channel_id=1, source_target_pairs={{0,384},{64,448},{128,0},{192,64},{256,128},{320,192},{384,256},{4... | collective-permute-start | bytes 460808 | tf_op jit(solution)/shard_map/ppermute | solution.py:178
  100.9 2.4 %collective-permute-done.9.piece2 = bf16[300,256]{1,0:T(8,128)(2,1)S(1)} collective-permute-done((bf16[300,256]{1,0:T(8,128)(2,1)S(1)}, bf16[300,256]{1,0:T(8,128)(2,1)S(1)}, u32[]{:S(2)}, u32[]{:S(2)}) %collective-permute-start.9) | collective-permute-done | bytes 153632 | tf_op jit(solution)/shard_map/ppermute | solution.py:178
  104.5 6.3 %shard_map.105 = (bf16[512,300]{1,0:T(8,128)(2,1)}, f32[300,256]{1,0:T(8,128)S(1)}, bf16[300,256]{1,0:T(8,128)(2,1)S(1)}, bf16[300,256]{1,0:T(8,128)(2,1)S(1)}, bf16[300,256]{1,0:T(8,128)(2,1)S(1)}) custom-call(s32[1]{0:T(128)} %bitcast.place, bf16[512,300]{1,0:T(8,128)(2,1)} %bitcast.10.rows_in, bf16[300,256]{1,0:T(8,128)(2,1)S(1)} %get-tuple-element.27.piece0, ...), custom_call_target="tpu_custom_call" | custom-call | flops 943718400 | bytes 2097152 | tf_op jit(solution)/shard_map/pallas_call | solution.py:83
  110.8 4.2 %collective-permute-start.11 = (bf16[300,256]{1,0:T(8,128)(2,1)S(1)}, bf16[300,256]{1,0:T(8,128)(2,1)S(1)}, u32[]{:S(2)}, u32[]{:S(2)}) collective-permute-start(bf16[300,256]{1,0:T(8,128)(2,1)S(1)} %get-tuple-element.32), channel_id=1, source_target_pairs={{0,128},{64,192},{128,256},{192,320},{256,384},{320,448},{384,0},{... | collective-permute-start | bytes 460808 | tf_op jit(solution)/shard_map/ppermute | solution.py:183
  115.0 3.5 %collective-permute-start.12 = (bf16[300,256]{1,0:T(8,128)(2,1)S(1)}, bf16[300,256]{1,0:T(8,128)(2,1)S(1)}, u32[]{:S(2)}, u32[]{:S(2)}) collective-permute-start(bf16[300,256]{1,0:T(8,128)(2,1)S(1)} %get-tuple-element.33), channel_id=1, source_target_pairs={{0,256},{64,320},{128,384},{192,448},{256,0},{320,64},{384,128},{4... | collective-permute-start | bytes 460808 | tf_op jit(solution)/shard_map/ppermute | solution.py:183
  118.5 2.8 %collective-permute-start.13 = (bf16[300,256]{1,0:T(8,128)(2,1)S(1)}, bf16[300,256]{1,0:T(8,128)(2,1)S(1)}, u32[]{:S(2)}, u32[]{:S(2)}) collective-permute-start(bf16[300,256]{1,0:T(8,128)(2,1)S(1)} %get-tuple-element.34), channel_id=1, source_target_pairs={{0,384},{64,448},{128,0},{192,64},{256,128},{320,192},{384,256},{4... | collective-permute-start | bytes 460808 | tf_op jit(solution)/shard_map/ppermute | solution.py:183
  121.3 12.4 %all-to-all-start.3 = ((bf16[64,8,300]{2,1,0:T(8,128)(2,1)}), bf16[64,8,300]{2,1,0:T(8,128)(2,1)S(1)}, u32[]{:S(2)}, u32[]{:S(2)}) async-start(bf16[64,8,300]{2,1,0:T(8,128)(2,1)} %bitcast.12), calls=%async_computation.3 | async-start | bytes 786432 | tf_op jit(solution)/shard_map/all_to_all | solution.py:180
  133.9 4.7 %collective-permute-start.14 = (bf16[300,128]{1,0:T(8,128)(2,1)S(1)}, bf16[300,128]{1,0:T(8,128)(2,1)S(1)}, u32[]{:S(2)}, u32[]{:S(2)}) collective-permute-start(bf16[300,128]{1,0:T(8,128)(2,1)S(1)} %select_convert_fusion), channel_id=1, source_target_pairs={{0,64},{64,0},{128,192},{192,128},{256,320},{320,256},{384,448},{4... | collective-permute-start | bytes 230408 | tf_op jit(solution)/shard_map/ppermute | solution.py:202
  138.6 6.6 %collective-permute-done.14 = bf16[300,128]{1,0:T(8,128)(2,1)S(1)} collective-permute-done((bf16[300,128]{1,0:T(8,128)(2,1)S(1)}, bf16[300,128]{1,0:T(8,128)(2,1)S(1)}, u32[]{:S(2)}, u32[]{:S(2)}) %collective-permute-start.14) | collective-permute-done | bytes 76832 | tf_op jit(solution)/shard_map/ppermute | solution.py:202
  146.0 5.1 %all-to-all-done.3 = bf16[64,8,300]{2,1,0:T(8,128)(2,1)S(1)} async-done(((bf16[64,8,300]{2,1,0:T(8,128)(2,1)}), bf16[64,8,300]{2,1,0:T(8,128)(2,1)S(1)}, u32[]{:S(2)}, u32[]{:S(2)}) %all-to-all-start.3) | async-done | bytes 307232 | tf_op jit(solution)/shard_map/all_to_all | solution.py:180
  (54 shorter events, 16.1 us)
Async XLA Ops:
  0.6 24.0 %copy-start.6 = (f32[300,128]{1,0:T(8,128)S(1)}, f32[300,128]{1,0:T(8,128)}, u32[]{:S(2)}) copy-start(f32[300,128]{1,0:T(8,128)} %param.10) | copy-start | bytes 460804
  0.6 24.0 %copy-start.7 = (f32[300,128]{1,0:T(8,128)S(1)}, f32[300,128]{1,0:T(8,128)}, u32[]{:S(2)}) copy-start(f32[300,128]{1,0:T(8,128)} %param.9) | copy-start | bytes 460804
  1.7 33.6 %copy-start.8 = (s32[1024]{0:T(1024)S(1)}, s32[1024]{0:T(1024)}, u32[]{:S(2)}) copy-start(s32[1024]{0:T(1024)} %param.13) | copy-start | bytes 12292
  1.7 22.8 %collective-permute-start = (bf16[2,300,128]{2,1,0:T(8,128)(2,1)S(1)}, bf16[2,300,128]{2,1,0:T(8,128)(2,1)S(1)}, u32[]{:S(2)}, u32[]{:S(2)}) collective-permute-start(bf16[2,300,128]{2,1,0:T(8,128)(2,1)S(1)} %pad_maximum_fusion.2), channel_id=1, source_target_pairs={{0,64},{64,0},{128,192},{192,128},{256,320},{320,256},{384,448},{4... | collective-permute-start | bytes 460808 | tf_op jit(solution)/shard_map/ppermute | solution.py:166
  11.5 27.1 %all-to-all-start = ((bf16[64,8,300]{2,1,0:T(8,128)(2,1)}), bf16[64,8,300]{2,1,0:T(8,128)(2,1)S(1)}, u32[]{:S(2)}, u32[]{:S(2)}) async-start(bf16[64,8,300]{2,1,0:T(8,128)(2,1)} %broadcast_in_dim.16), calls=%async_computation | async-start | bytes 786432 | tf_op jit(solution)/shard_map/all_to_all | solution.py:177
  24.7 10.6 %collective-permute-start.3 = (bf16[300,256]{1,0:T(8,128)(2,1)S(1)}, bf16[300,256]{1,0:T(8,128)(2,1)S(1)}, u32[]{:S(2)}, u32[]{:S(2)}) collective-permute-start(bf16[300,256]{1,0:T(8,128)(2,1)S(1)} %fusion.5.piece0), channel_id=1, source_target_pairs={{0,128},{64,192},{128,256},{192,320},{256,384},{320,448},{384,0},{... | collective-permute-start | bytes 460808 | tf_op jit(solution)/shard_map/ppermute | solution.py:178
  27.9 9.5 %collective-permute-start.2 = (bf16[300,256]{1,0:T(8,128)(2,1)S(1)}, bf16[300,256]{1,0:T(8,128)(2,1)S(1)}, u32[]{:S(2)}, u32[]{:S(2)}) collective-permute-start(bf16[300,256]{1,0:T(8,128)(2,1)S(1)} %fusion.5.piece0), channel_id=1, source_target_pairs={{0,256},{64,320},{128,384},{192,448},{256,0},{320,64},{384,128},{4... | collective-permute-start | bytes 460808 | tf_op jit(solution)/shard_map/ppermute | solution.py:178
  32.2 6.4 %collective-permute-start.1 = (bf16[300,256]{1,0:T(8,128)(2,1)S(1)}, bf16[300,256]{1,0:T(8,128)(2,1)S(1)}, u32[]{:S(2)}, u32[]{:S(2)}) collective-permute-start(bf16[300,256]{1,0:T(8,128)(2,1)S(1)} %fusion.5.piece0), channel_id=1, source_target_pairs={{0,384},{64,448},{128,0},{192,64},{256,128},{320,192},{384,256},{4... | collective-permute-start | bytes 460808 | tf_op jit(solution)/shard_map/ppermute | solution.py:178
  45.0 31.3 %copy-start.2 = (f32[300,8]{0,1:T(8,128)S(1)}, f32[300,8]{0,1:T(8,128)}, u32[]{:S(2)}) copy-start(f32[300,8]{0,1:T(8,128)} %param.7) | copy-start | bytes 28804
  45.0 31.3 %copy-start.5 = (f32[300,8]{0,1:T(8,128)S(1)}, f32[300,8]{0,1:T(8,128)}, u32[]{:S(2)}) copy-start(f32[300,8]{0,1:T(8,128)} %param.8) | copy-start | bytes 28804
  45.0 31.3 %all-to-all-start.1 = ((bf16[64,8,300]{2,1,0:T(8,128)(2,1)}), bf16[64,8,300]{2,1,0:T(8,128)(2,1)S(1)}, u32[]{:S(2)}, u32[]{:S(2)}) async-start(bf16[64,8,300]{2,1,0:T(8,128)(2,1)} %bitcast.8), calls=%async_computation.1 | async-start | bytes 786432 | tf_op jit(solution)/shard_map/all_to_all | solution.py:180
  57.3 10.2 %collective-permute-start.4 = (bf16[300,256]{1,0:T(8,128)(2,1)S(1)}, bf16[300,256]{1,0:T(8,128)(2,1)S(1)}, u32[]{:S(2)}, u32[]{:S(2)}) collective-permute-start(bf16[300,256]{1,0:T(8,128)(2,1)S(1)} %get-tuple-element.22), channel_id=1, source_target_pairs={{0,128},{64,192},{128,256},{192,320},{256,384},{320,448},{384,0},{... | collective-permute-start | bytes 460808 | tf_op jit(solution)/shard_map/ppermute | solution.py:183
  60.9 8.8 %collective-permute-start.5 = (bf16[300,256]{1,0:T(8,128)(2,1)S(1)}, bf16[300,256]{1,0:T(8,128)(2,1)S(1)}, u32[]{:S(2)}, u32[]{:S(2)}) collective-permute-start(bf16[300,256]{1,0:T(8,128)(2,1)S(1)} %get-tuple-element.23), channel_id=1, source_target_pairs={{0,256},{64,320},{128,384},{192,448},{256,0},{320,64},{384,128},{4... | collective-permute-start | bytes 460808 | tf_op jit(solution)/shard_map/ppermute | solution.py:183
  64.7 6.4 %collective-permute-start.6 = (bf16[300,256]{1,0:T(8,128)(2,1)S(1)}, bf16[300,256]{1,0:T(8,128)(2,1)S(1)}, u32[]{:S(2)}, u32[]{:S(2)}) collective-permute-start(bf16[300,256]{1,0:T(8,128)(2,1)S(1)} %get-tuple-element.24), channel_id=1, source_target_pairs={{0,384},{64,448},{128,0},{192,64},{256,128},{320,192},{384,256},{4... | collective-permute-start | bytes 460808 | tf_op jit(solution)/shard_map/ppermute | solution.py:183
  71.9 18.1 %collective-permute-start.7 = (bf16[300,256]{1,0:T(8,128)(2,1)}, bf16[300,256]{1,0:T(8,128)(2,1)}, u32[]{:S(2)}, u32[]{:S(2)}) collective-permute-start(bf16[300,256]{1,0:T(8,128)(2,1)} %get-tuple-element.38.after), channel_id=1, source_target_pairs={{0,64},{64,0},{128,192},{192,128},{256,320},{320,256},{384,448},{4... | collective-permute-start | bytes 460808 | tf_op jit(solution)/shard_map/ppermute | solution.py:186
  77.2 27.3 %all-to-all-start.2 = ((bf16[64,8,300]{2,1,0:T(8,128)(2,1)}), bf16[64,8,300]{2,1,0:T(8,128)(2,1)}, u32[]{:S(2)}, u32[]{:S(2)}) async-start(bf16[64,8,300]{2,1,0:T(8,128)(2,1)} %get-tuple-element.26), calls=%async_computation.2 | async-start | bytes 786432 | tf_op jit(solution)/shard_map/all_to_all | solution.py:177
  91.1 9.8 %collective-permute-start.10 = (bf16[300,256]{1,0:T(8,128)(2,1)S(1)}, bf16[300,256]{1,0:T(8,128)(2,1)S(1)}, u32[]{:S(2)}, u32[]{:S(2)}) collective-permute-start(bf16[300,256]{1,0:T(8,128)(2,1)S(1)} %get-tuple-element.27.piece0), channel_id=1, source_target_pairs={{0,128},{64,192},{128,256},{192,320},{256,384},{320,448},{384,0},{... | collective-permute-start | bytes 460808 | tf_op jit(solution)/shard_map/ppermute | solution.py:178
  94.4 8.9 %collective-permute-start.9 = (bf16[300,256]{1,0:T(8,128)(2,1)S(1)}, bf16[300,256]{1,0:T(8,128)(2,1)S(1)}, u32[]{:S(2)}, u32[]{:S(2)}) collective-permute-start(bf16[300,256]{1,0:T(8,128)(2,1)S(1)} %get-tuple-element.27.piece0), channel_id=1, source_target_pairs={{0,256},{64,320},{128,384},{192,448},{256,0},{320,64},{384,128},{4... | collective-permute-start | bytes 460808 | tf_op jit(solution)/shard_map/ppermute | solution.py:178
  98.2 6.3 %collective-permute-start.8 = (bf16[300,256]{1,0:T(8,128)(2,1)S(1)}, bf16[300,256]{1,0:T(8,128)(2,1)S(1)}, u32[]{:S(2)}, u32[]{:S(2)}) collective-permute-start(bf16[300,256]{1,0:T(8,128)(2,1)S(1)} %get-tuple-element.27.piece0), channel_id=1, source_target_pairs={{0,384},{64,448},{128,0},{192,64},{256,128},{320,192},{384,256},{4... | collective-permute-start | bytes 460808 | tf_op jit(solution)/shard_map/ppermute | solution.py:178
  110.8 23.0 %collective-permute-start.11 = (bf16[300,256]{1,0:T(8,128)(2,1)S(1)}, bf16[300,256]{1,0:T(8,128)(2,1)S(1)}, u32[]{:S(2)}, u32[]{:S(2)}) collective-permute-start(bf16[300,256]{1,0:T(8,128)(2,1)S(1)} %get-tuple-element.32), channel_id=1, source_target_pairs={{0,128},{64,192},{128,256},{192,320},{256,384},{320,448},{384,0},{... | collective-permute-start | bytes 460808 | tf_op jit(solution)/shard_map/ppermute | solution.py:183
  115.0 18.7 %collective-permute-start.12 = (bf16[300,256]{1,0:T(8,128)(2,1)S(1)}, bf16[300,256]{1,0:T(8,128)(2,1)S(1)}, u32[]{:S(2)}, u32[]{:S(2)}) collective-permute-start(bf16[300,256]{1,0:T(8,128)(2,1)S(1)} %get-tuple-element.33), channel_id=1, source_target_pairs={{0,256},{64,320},{128,384},{192,448},{256,0},{320,64},{384,128},{4... | collective-permute-start | bytes 460808 | tf_op jit(solution)/shard_map/ppermute | solution.py:183
  118.5 15.3 %collective-permute-start.13 = (bf16[300,256]{1,0:T(8,128)(2,1)S(1)}, bf16[300,256]{1,0:T(8,128)(2,1)S(1)}, u32[]{:S(2)}, u32[]{:S(2)}) collective-permute-start(bf16[300,256]{1,0:T(8,128)(2,1)S(1)} %get-tuple-element.34), channel_id=1, source_target_pairs={{0,384},{64,448},{128,0},{192,64},{256,128},{320,192},{384,256},{4... | collective-permute-start | bytes 460808 | tf_op jit(solution)/shard_map/ppermute | solution.py:183
  121.3 29.8 %all-to-all-start.3 = ((bf16[64,8,300]{2,1,0:T(8,128)(2,1)}), bf16[64,8,300]{2,1,0:T(8,128)(2,1)S(1)}, u32[]{:S(2)}, u32[]{:S(2)}) async-start(bf16[64,8,300]{2,1,0:T(8,128)(2,1)} %bitcast.12), calls=%async_computation.3 | async-start | bytes 786432 | tf_op jit(solution)/shard_map/all_to_all | solution.py:180
  133.9 11.3 %collective-permute-start.14 = (bf16[300,128]{1,0:T(8,128)(2,1)S(1)}, bf16[300,128]{1,0:T(8,128)(2,1)S(1)}, u32[]{:S(2)}, u32[]{:S(2)}) collective-permute-start(bf16[300,128]{1,0:T(8,128)(2,1)S(1)} %select_convert_fusion), channel_id=1, source_target_pairs={{0,64},{64,0},{128,192},{192,128},{256,320},{320,256},{384,448},{4... | collective-permute-start | bytes 230408 | tf_op jit(solution)/shard_map/ppermute | solution.py:202
  (4 other events, 59.2 us)

commit v4 on v3

v4 whole, which is shorter than its diff:
```python
import functools

import jax
import jax.numpy as jnp
from jax import lax
from jax.experimental import pallas as pl
from jax.experimental.pallas import tpu as pltpu
from jax.sharding import PartitionSpec as P

ROW_TILE = 128
VMEM_LIMIT = 24 * 1024 * 1024
TILE_COST = 16
ROW_COST = 1 << 36
PAIR_COST = 1 << 36


def tile_kernel(steps, first, place, rows_in, piece0, piece1, counts_in, row_term_in, col_term_in,
                *refs):
    if first:
        rows_out, grad0, grad1 = refs[:3]
    else:
        part_in, rows_out, grad0, grad1 = refs[:4]
    (rows, rows_t, cols, counts, row_term, col_term, slope, part,
     grad_rows, grad_own, grad_away, in_sem, out_sem) = refs[-13:]
    n_rows = rows.shape[0]
    wide = piece0.shape[1]
    pieces = (piece0, piece1)
    outs = (grad0, grad1)

    def start(source, target, sem):
        copy = pltpu.make_async_copy(source, target, sem)
        copy.start()
        return copy

    def there(k):
        return pl.ds(pl.multiple_of(lax.rem(place[0] + steps[k], 4) * wide, wide), wide)

    here = [pl.ds(k * wide, wide) for k in range(2)]
    rows_copy = start(rows_in, rows, in_sem.at[0])
    cols_copy, counts_copy = [], []
    for k in range(2):
        cols_copy.append(start(pieces[k], cols.at[:, here[k]], in_sem.at[1 + k]))
        counts_copy.append(
            start(counts_in.at[:, there(k)], counts.at[:, here[k]], in_sem.at[3 + k])
        )
        if k == 0:
            row_copy = start(row_term_in, row_term, in_sem.at[5])
            col_copy = start(col_term_in, col_term, in_sem.at[6])
    if not first:
        part_copy = start(part_in, part, in_sem.at[7])
    rows_copy.wait()
    rows_t[...] = rows[...].T
    done = []
    for k in range(2):
        cols_copy[k].wait()
        counts_copy[k].wait()
        if k == 0:
            row_copy.wait()
            col_copy.wait()
        col_part = col_term[:, there(k)]
        for top in range(0, n_rows, ROW_TILE):
            at = pl.ds(top, ROW_TILE)
            score = jnp.dot(rows[at, :], cols[:, here[k]], preferred_element_type=jnp.float32)
            count = counts[at, here[k]]
            value = jnp.maximum(count.astype(jnp.float32), 1.0)
            diff = score - (jnp.log(value) + (row_term[at, :] - col_part))
            weight = 0.1 + 0.25 * (value * lax.rsqrt(value))
            zero = 0.5 * jnp.tanh(0.5 * diff) + 0.5
            slope[at, here[k]] = jnp.where(count > 0, weight * diff, zero).astype(jnp.bfloat16)
        grad = jnp.dot(rows_t[...], slope[:, here[k]], preferred_element_type=jnp.float32)
        if steps[k] == 0:
            grad_own[...] = grad
            done.append(start(grad_own, outs[k], out_sem.at[k]))
        else:
            grad_away[k] = grad.astype(jnp.bfloat16)
            done.append(start(grad_away.at[k], outs[k], out_sem.at[k]))
    total = lax.dot_general(
        slope[...], cols[...], (((1,), (1,)), ((), ())), preferred_element_type=jnp.float32
    )
    if first:
        part[...] = total
        done.append(start(part, rows_out, out_sem.at[2]))
    else:
        part_copy.wait()
        grad_rows[...] = (part[...] + total).astype(jnp.bfloat16)
        done.append(start(grad_rows, rows_out, out_sem.at[2]))
    for copy in done:
        copy.wait()


def tile_grads(steps, place, rows, pieces, counts, row_term, col_term, part=None):
    first = part is None
    n_rows, width = rows.shape
    wide = pieces[0].shape[1]
    hbm = pl.BlockSpec(memory_space=pltpu.HBM)
    shape = jax.ShapeDtypeStruct
    return pl.pallas_call(
        functools.partial(tile_kernel, steps, first),
        in_specs=[pl.BlockSpec(memory_space=pltpu.SMEM)] + [hbm] * (6 if first else 7),
        out_specs=[hbm] * 3,
        out_shape=[
            shape((n_rows, width), jnp.float32 if first else jnp.bfloat16),
            shape((width, wide), jnp.float32 if steps[0] == 0 else jnp.bfloat16),
            shape((width, wide), jnp.bfloat16),
        ],
        scratch_shapes=[
            pltpu.VMEM((n_rows, width), jnp.bfloat16),
            pltpu.VMEM((width, n_rows), jnp.bfloat16),
            pltpu.VMEM((width, 2 * wide), jnp.bfloat16),
            pltpu.VMEM((n_rows, 2 * wide), jnp.int32),
            pltpu.VMEM((n_rows, 1), jnp.float32),
            pltpu.VMEM((1, 4 * wide), jnp.float32),
            pltpu.VMEM((n_rows, 2 * wide), jnp.bfloat16),
            pltpu.VMEM((n_rows, width), jnp.float32),
            pltpu.VMEM((n_rows, width), jnp.bfloat16),
            pltpu.VMEM((width, wide), jnp.float32),
            pltpu.VMEM((2, width, wide), jnp.bfloat16),
            pltpu.SemaphoreType.DMA((8,)),
            pltpu.SemaphoreType.DMA((3,)),
        ],
        compiler_params=pltpu.CompilerParams(vmem_limit_bytes=VMEM_LIMIT),
        cost_estimate=pl.CostEstimate(
            flops=6 * n_rows * 2 * wide * width * TILE_COST,
            bytes_accessed=4 * n_rows * 2 * wide,
            transcendentals=3 * n_rows * 2 * wide,
        ),
    )(place, rows, *pieces, counts, row_term, col_term, *(() if first else (part,)))


def adagrad(emb, acc, grad):
    acc = acc + grad * grad
    return (emb - 0.1 * grad / jnp.sqrt(acc), acc)


def whole_call(kernel, outs, cost, extra=None):
    specs = {} if extra is None else {"in_specs": extra}
    return pl.pallas_call(
        kernel,
        **specs,
        out_shape=outs,
        compiler_params=pltpu.CompilerParams(vmem_limit_bytes=VMEM_LIMIT),
        cost_estimate=pl.CostEstimate(flops=cost, bytes_accessed=cost, transcendentals=cost >> 4),
    )


def row_kernel(scale, near, far, emb, acc, after, emb_out, acc_out, send):
    grad = (near[...] + far[...]) * scale
    new_emb, new_acc = adagrad(emb[...], acc[...], grad)
    emb_out[...] = new_emb
    acc_out[...] = new_acc
    send[...] = jnp.broadcast_to(new_emb.astype(jnp.bfloat16)[None], send.shape)


def pair_kernel(scale, col_sum, away, emb, acc, emb_out, acc_out, send):
    grad = (col_sum[...] + away[...].astype(jnp.float32)) * scale
    new_emb, new_acc = adagrad(emb[...], acc[...], grad)
    emb_out[...] = new_emb
    acc_out[...] = new_acc
    send[...] = new_emb.astype(jnp.bfloat16)


def on_device(row_emb, row_acc, col_emb, col_acc, counts, row_marg, col_marg):
    n_row, n_col = lax.axis_size("row"), lax.axis_size("col")
    width = row_emb.shape[0]
    rows, cols = counts.shape
    half = cols // n_row
    row_scale = float((cols * n_col) ** -0.5)
    col_scale = float((rows * n_row) ** -0.5)
    me = lax.axis_index("row")
    odd = me % 2 == 1
    place = (me // 2).astype(jnp.int32)[None]
    row_term = (12.0 - jnp.log(row_marg.astype(jnp.float32)))[:, None]
    col_term = jnp.log(col_marg.astype(jnp.float32))[None, :]
    pair = [(i, i ^ 1) for i in range(n_row)]
    step_by = lambda d: [(i, (i // 2 + d) % 4 * 2 + i % 2) for i in range(n_row)]
    row_emb, row_acc = row_emb.T, row_acc.T
    n_chip = n_col // 2
    cores = [[2 * i, 2 * i + 1] for i in range(n_chip)]
    chips = [[2 * i + core for i in range(n_chip)] for core in range(2)]
    swap = [(i, i ^ 1) for i in range(n_col)]
    second = lax.axis_index("col") % 2 == 1
    full = lambda like, dtype=jnp.float32: jax.ShapeDtypeStruct(like, dtype)
    few = row_emb.shape[0]
    to_all = full((n_chip, 2 * few, width), jnp.bfloat16)
    both = jnp.stack([col_emb.astype(jnp.bfloat16), col_acc.astype(jnp.bfloat16)])
    shared = lax.all_gather(
        jnp.stack([row_emb, row_acc]), "col", axis=1, tiled=True, axis_index_groups=cores
    )
    shared_emb, shared_acc = shared[0], shared[1]
    row_send = jnp.broadcast_to(shared_emb.astype(jnp.bfloat16)[None], to_all.shape)
    other = lax.ppermute(both, "row", pair).astype(jnp.float32)
    in_order = lambda mine, theirs: jnp.concatenate(
        [jnp.where(odd, theirs, mine), jnp.where(odd, mine, theirs)], axis=1
    )
    pair_emb = in_order(col_emb, other[0])
    pair_acc = in_order(col_acc, other[1])
    pair_send = pair_emb.astype(jnp.bfloat16)
    vmem = pl.BlockSpec(memory_space=pltpu.VMEM)
    in_hbm = lambda values: pltpu.with_memory_space_constraint(values, pltpu.HBM)
    own = lambda wide: jnp.where(odd, wide[:, half:], wide[:, :half])
    for step in range(2):
        row_half = lax.all_to_all(row_send, "col", 0, 0, axis_index_groups=chips).reshape(rows, width)
        pieces = [pair_send] + [lax.ppermute(pair_send, "row", step_by(-d)) for d in (1, 2, 3)]
        operands = (in_hbm(counts), row_term, col_term)
        part, *grads_a = tile_grads((0, 3), place, row_half, (pieces[0], pieces[3]), *operands)
        grad_rows, *grads_b = tile_grads(
            (2, 1), place, row_half, (pieces[2], pieces[1]), *operands, part
        )
        grads = [grad_rows, grads_a[0], grads_b[1], grads_b[0], grads_a[1]]
        col_sum = grads[1]
        for d in (1, 2, 3):
            col_sum = col_sum + lax.ppermute(grads[1 + d], "row", step_by(d)).astype(jnp.float32)
        if step == 0:
            half_sum = col_sum.astype(jnp.bfloat16)
            away = lax.ppermute(half_sum, "row", pair)
            parts = lax.all_to_all(
                grads[0].reshape(to_all.shape), "col", 0, 0, axis_index_groups=chips
            )
            near = jnp.sum(parts.astype(jnp.float32), axis=0)
            far = lax.ppermute(near, "col", swap)
            shared_emb, shared_acc, row_send = whole_call(
                functools.partial(row_kernel, row_scale),
                [full(shared_emb.shape), full(shared_emb.shape), to_all],
                ROW_COST,
                [vmem, vmem, vmem, vmem, pl.BlockSpec(memory_space=pl.ANY)],
            )(near, far, shared_emb, shared_acc, half_sum)
            pair_emb, pair_acc, pair_send = whole_call(
                functools.partial(pair_kernel, col_scale),
                [full(pair_emb.shape), full(pair_emb.shape), full(pair_emb.shape, jnp.bfloat16)],
                PAIR_COST,
            )(col_sum, away, pair_emb, pair_acc)
        else:
            parts = lax.all_to_all(grads[0].reshape(n_col, few, width), "col", 0, 0)
            row_grad = jnp.sum(parts.astype(jnp.float32), axis=0) * row_scale
            mine = lambda both: jnp.where(second, both[few:], both[:few])
            row_emb, row_acc = adagrad(mine(shared_emb), mine(shared_acc), row_grad)
            away = jnp.where(odd, col_sum[:, :half], col_sum[:, half:]).astype(jnp.bfloat16)
            away = lax.ppermute(away, "row", pair).astype(jnp.float32)
            col_grad = (own(col_sum) + away) * col_scale
            col_emb, col_acc = adagrad(own(pair_emb), own(pair_acc), col_grad)
    return (row_emb.T, row_acc.T, col_emb, col_acc)


def solution(mesh):
    by_row, by_col = P(None, ("row", "col")), P(None, ("col", "row"))
    return jax.shard_map(
        on_device,
        mesh=mesh,
        in_specs=(by_row, by_row, by_col, by_col, P("row", "col"), P("row"), P("col")),
        out_specs=(by_row, by_row, by_col, by_col),
        check_vma=False,
    )
```

time: 153 us -> 147 us (0.961)
  starting transfers between devices: 108 us -> 101 us
  waiting for transfers between devices: 22.2 us -> 17.9 us
  Pallas kernels: 14.6 us -> 17.6 us
  blocking collectives: 0 us -> 2.44 us
    all_to_all x4, starting transfers between devices: 49.7 us -> 39.1 us  [the longest x2 18.2 us: on_device(): lax.all_to_all(row_send, 'col', 0, 0, axis_index_groups=chips)]
    ppermute x6, waiting for transfers between devices: 6.89 us -> 0.31 us  [on_device(): lax.ppermute(pair_send, 'row', step_by(-d))]
    ppermute x0 -> x1, starting transfers between devices: none -> 6.04 us  [on_device(): far = lax.ppermute(near, 'col', swap)]
    all_to_all x4, waiting for transfers between devices: 5.15 us -> 11.1 us  [the longest x1 5.11 us: on_device(): parts = lax.all_to_all(grads[0].reshape(n_col, few, width), 'col', 0, 0)]
    ppermute x6, waiting for transfers between devices: 3.61 us -> 0.02 us  [on_device(): lax.ppermute(grads[1 + d], 'row', step_by(d)).astype(jnp.float32)]
    pallas_call x3 -> x5, Pallas kernels: 13.5 us -> 16.5 us  [the longest x4 15.7 us: tile_grads(): pl.pallas_call(functools.partial(tile_kernel, steps, first), in_specs=[pl...]
    all_gather x0 -> x1, blocking collectives: none -> 2.44 us  [on_device(): lax.all_gather(jnp.stack([row_emb, row_acc]), 'col', axis=1, tiled=True,...]
  transfers between devices with their start and end apart: 19 -> 20, of which waited for: 8 -> 6; matrix products, arithmetic and copies ran while one was open for 3% -> 2% of each run, Pallas kernels for 1% -> 6%
where the time goes in v4:
time: 147 us; the launch traced here: 145 us
  starting transfers between devices  101 us (69%)
  waiting for transfers between devices  17.9 us (12%)
  Pallas kernels  17.6 us (12%)
  other arithmetic  4.39 us (3%)
  blocking collectives  2.44 us (2%)
    ppermute x6, starting transfers between devices, on_device(): lax.ppermute(grads[1 + d], 'row', step_by(d)).astype(jnp.float32)  19.2 us
    ppermute x6, starting transfers between devices, on_device(): lax.ppermute(pair_send, 'row', step_by(-d))  19.1 us
    all_to_all x2, starting transfers between devices, on_device(): lax.all_to_all(row_send, 'col', 0, 0, axis_index_groups=chips)  18.2 us
    pallas_call x4, Pallas kernels, tile_grads(): pl.pallas_call(functools.partial(tile_kernel, steps, first), in_specs=[pl...  15.7 us
    all_to_all x1, starting transfers between devices, on_device(): parts = lax.all_to_all(grads[0].reshape(n_col, few, width), 'col', 0, 0)  13.6 us
    ppermute x1, starting transfers between devices, on_device(): other = lax.ppermute(both, 'row', pair).astype(jnp.float32)  8.28 us
    all_to_all x1, starting transfers between devices, on_device(): lax.all_to_all(grads[0].reshape(to_all.shape), 'col', 0, 0, axis_index_gr...  7.24 us
    ppermute x1, waiting for transfers between devices, on_device(): away = lax.ppermute(away, 'row', pair).astype(jnp.float32)  6.55 us
  transfers between devices with their start and end apart: 20, of which 6 were waited for; matrix products, arithmetic and copies ran while one was open for 2% of the time, Pallas kernels for 6%

profile of v4, /device:TPU:1, one launch (start us, length us, event | category | flops | bytes accessed | tf_op | source)
XLA Modules:
  0.0 145.4 jit_solution(5999122922929894760)
XLA Ops:
  1.8 8.3 %collective-permute-start = (bf16[2,300,128]{2,1,0:T(8,128)(2,1)S(1)}, bf16[2,300,128]{2,1,0:T(8,128)(2,1)S(1)}, u32[]{:S(2)}, u32[]{:S(2)}) collective-permute-start(bf16[2,300,128]{2,1,0:T(8,128)(2,1)S(1)} %pad_maximum_fusion.2), channel_id=1, source_target_pairs={{0,64},{64,0},{128,192},{192,128},{256,320},{320,256},{384,448},{4... | collective-permute-start | bytes 460808 | tf_op jit(solution)/shard_map/ppermute | solution.py:191
  14.0 10.8 %all-to-all-start = ((bf16[32,16,300]{2,1,0:T(8,128)(2,1)}), bf16[32,16,300]{2,1,0:T(8,128)(2,1)S(1)}, u32[]{:S(2)}, u32[]{:S(2)}) async-start(bf16[32,16,300]{2,1,0:T(8,128)(2,1)} %broadcast_in_dim.19), calls=%async_computation | async-start | bytes 786432 | tf_op jit(solution)/shard_map/all_to_all | solution.py:202
  25.2 3.1 %collective-permute-start.3 = (bf16[300,256]{1,0:T(8,128)(2,1)S(1)}, bf16[300,256]{1,0:T(8,128)(2,1)S(1)}, u32[]{:S(2)}, u32[]{:S(2)}) collective-permute-start(bf16[300,256]{1,0:T(8,128)(2,1)S(1)} %fusion.6.piece0), channel_id=1, source_target_pairs={{0,128},{64,192},{128,256},{192,320},{256,384},{320,448},{384,0},{... | collective-permute-start | bytes 460808 | tf_op jit(solution)/shard_map/ppermute | solution.py:203
  28.3 3.4 %collective-permute-start.2 = (bf16[300,256]{1,0:T(8,128)(2,1)S(1)}, bf16[300,256]{1,0:T(8,128)(2,1)S(1)}, u32[]{:S(2)}, u32[]{:S(2)}) collective-permute-start(bf16[300,256]{1,0:T(8,128)(2,1)S(1)} %fusion.6.piece0), channel_id=1, source_target_pairs={{0,384},{64,448},{128,0},{192,64},{256,128},{320,192},{384,256},{4... | collective-permute-start | bytes 460808 | tf_op jit(solution)/shard_map/ppermute | solution.py:203
  31.7 3.4 %collective-permute-start.1 = (bf16[300,256]{1,0:T(8,128)(2,1)S(1)}, bf16[300,256]{1,0:T(8,128)(2,1)S(1)}, u32[]{:S(2)}, u32[]{:S(2)}) collective-permute-start(bf16[300,256]{1,0:T(8,128)(2,1)S(1)} %fusion.6.piece0), channel_id=1, source_target_pairs={{0,256},{64,320},{128,384},{192,448},{256,0},{320,64},{384,128},{4... | collective-permute-start | bytes 460808 | tf_op jit(solution)/shard_map/ppermute | solution.py:203
  35.2 2.8 %all-to-all-done = bf16[32,16,300]{2,1,0:T(8,128)(2,1)S(1)} async-done(((bf16[32,16,300]{2,1,0:T(8,128)(2,1)}), bf16[32,16,300]{2,1,0:T(8,128)(2,1)S(1)}, u32[]{:S(2)}, u32[]{:S(2)}) %all-to-all-start) | async-done | bytes 307232 | tf_op jit(solution)/shard_map/all_to_all | solution.py:202
  38.0 3.5 %shard_map.102 = (f32[512,300]{1,0:T(8,128)S(1)}, f32[300,256]{1,0:T(8,128)S(1)}, bf16[300,256]{1,0:T(8,128)(2,1)S(1)}) custom-call(s32[1]{0:T(128)} %bitcast.place, bf16[512,300]{1,0:T(8,128)(2,1)S(1)} %bitcast.39, bf16[300,256]{1,0:T(8,128)(2,1)S(1)} %fusion.6.piece0, bf16[300,256]{1,0:T(8,128)(2,1)S(1)} %collective-permute-done.3.piece1, ...), custom_call_target="tpu_custom_call" | custom-call | flops 7549747200 | bytes 1048576 | tf_op jit(solution)/shard_map/pallas_call | solution.py:97
  41.5 4.4 %shard_map.103 = (bf16[512,300]{1,0:T(8,128)(2,1)}, bf16[300,256]{1,0:T(8,128)(2,1)S(1)}, bf16[300,256]{1,0:T(8,128)(2,1)S(1)}) custom-call(s32[1]{0:T(128)} %bitcast.place, bf16[512,300]{1,0:T(8,128)(2,1)S(1)} %bitcast.40, bf16[300,256]{1,0:T(8,128)(2,1)S(1)} %collective-permute-done.1.piece0, bf16[300,256]{1,0:T(8,128)(2,1)S(1)} %collective-permute-done.2.piece1, ...), custom_call_target="tpu_custom_call" | custom-call | flops 7549747200 | bytes 1048576 | tf_op jit(solution)/shard_map/pallas_call | solution.py:97
  46.0 7.2 %all-to-all-start.1 = ((bf16[32,16,300]{2,1,0:T(8,128)(2,1)}), bf16[32,16,300]{2,1,0:T(8,128)(2,1)S(1)}, u32[]{:S(2)}, u32[]{:S(2)}) async-start(bf16[32,16,300]{2,1,0:T(8,128)(2,1)} %bitcast.12), calls=%async_computation.1 | async-start | bytes 786432 | tf_op jit(solution)/shard_map/all_to_all | solution.py:216
  55.5 4.4 %collective-permute-start.6 = (bf16[300,256]{1,0:T(8,128)(2,1)S(1)}, bf16[300,256]{1,0:T(8,128)(2,1)S(1)}, u32[]{:S(2)}, u32[]{:S(2)}) collective-permute-start(bf16[300,256]{1,0:T(8,128)(2,1)S(1)} %get-tuple-element.26), channel_id=1, source_target_pairs={{0,256},{64,320},{128,384},{192,448},{256,0},{320,64},{384,128},{4... | collective-permute-start | bytes 460808 | tf_op jit(solution)/shard_map/ppermute | solution.py:212
  59.8 3.1 %collective-permute-start.7 = (bf16[300,256]{1,0:T(8,128)(2,1)S(1)}, bf16[300,256]{1,0:T(8,128)(2,1)S(1)}, u32[]{:S(2)}, u32[]{:S(2)}) collective-permute-start(bf16[300,256]{1,0:T(8,128)(2,1)S(1)} %get-tuple-element.27), channel_id=1, source_target_pairs={{0,384},{64,448},{128,0},{192,64},{256,128},{320,192},{384,256},{4... | collective-permute-start | bytes 460808 | tf_op jit(solution)/shard_map/ppermute | solution.py:212
  64.9 6.0 %collective-permute-start.4 = (f32[16,300]{1,0:T(8,128)S(1)}, f32[16,300]{1,0:T(8,128)S(1)}, u32[]{:S(2)}, u32[]{:S(2)}) collective-permute-start(f32[16,300]{1,0:T(8,128)S(1)} %convert_reduce_fusion.1.near), channel_id=1, source_target_pairs={{0,1},{1,0},{2,3},{3,2},{4,5},{5,4},{6,7},{7,6},{8,9},{9,8},{10,11... | collective-permute-start | bytes 57608 | tf_op jit(solution)/shard_map/ppermute | solution.py:220
  71.7 4.4 %collective-permute-start.8 = (bf16[300,256]{1,0:T(8,128)(2,1)}, bf16[300,256]{1,0:T(8,128)(2,1)}, u32[]{:S(2)}, u32[]{:S(2)}) collective-permute-start(bf16[300,256]{1,0:T(8,128)(2,1)} %get-tuple-element.42.after), channel_id=1, source_target_pairs={{0,64},{64,0},{128,192},{192,128},{256,320},{320,256},{384,448},{4... | collective-permute-start | bytes 460808 | tf_op jit(solution)/shard_map/ppermute | solution.py:215
  76.9 7.4 %all-to-all-start.2 = ((bf16[32,16,300]{2,1,0:T(8,128)(2,1)}), bf16[32,16,300]{2,1,0:T(8,128)(2,1)}, u32[]{:S(2)}, u32[]{:S(2)}) async-start(bf16[32,16,300]{2,1,0:T(8,128)(2,1)} %get-tuple-element.29), calls=%async_computation.2 | async-start | bytes 786432 | tf_op jit(solution)/shard_map/all_to_all | solution.py:202
  87.9 4.2 %collective-permute-start.10 = (bf16[300,256]{1,0:T(8,128)(2,1)S(1)}, bf16[300,256]{1,0:T(8,128)(2,1)S(1)}, u32[]{:S(2)}, u32[]{:S(2)}) collective-permute-start(bf16[300,256]{1,0:T(8,128)(2,1)S(1)} %get-tuple-element.30.piece0), channel_id=1, source_target_pairs={{0,384},{64,448},{128,0},{192,64},{256,128},{320,192},{384,256},{4... | collective-permute-start | bytes 460808 | tf_op jit(solution)/shard_map/ppermute | solution.py:203
  92.1 2.6 %collective-permute-start.9 = (bf16[300,256]{1,0:T(8,128)(2,1)S(1)}, bf16[300,256]{1,0:T(8,128)(2,1)S(1)}, u32[]{:S(2)}, u32[]{:S(2)}) collective-permute-start(bf16[300,256]{1,0:T(8,128)(2,1)S(1)} %get-tuple-element.30.piece0), channel_id=1, source_target_pairs={{0,256},{64,320},{128,384},{192,448},{256,0},{320,64},{384,128},{4... | collective-permute-start | bytes 460808 | tf_op jit(solution)/shard_map/ppermute | solution.py:203
  96.0 3.4 %shard_map.106 = (f32[512,300]{1,0:T(8,128)S(1)}, f32[300,256]{1,0:T(8,128)S(1)}, bf16[300,256]{1,0:T(8,128)(2,1)S(1)}) custom-call(s32[1]{0:T(128)} %bitcast.place, bf16[512,300]{1,0:T(8,128)(2,1)} %bitcast.15.rows_in, bf16[300,256]{1,0:T(8,128)(2,1)S(1)} %get-tuple-element.30.piece0, bf16[300,256]{1,0:T(8,128)(2,1)S(1)} %collective-permute-done.11.piece1, ...), custom_call_target="tpu_custom_call" | custom-call | flops 7549747200 | bytes 1048576 | tf_op jit(solution)/shard_map/pallas_call | solution.py:97
  99.8 4.3 %shard_map.107 = (bf16[512,300]{1,0:T(8,128)(2,1)}, bf16[300,256]{1,0:T(8,128)(2,1)S(1)}, bf16[300,256]{1,0:T(8,128)(2,1)S(1)}) custom-call(s32[1]{0:T(128)} %bitcast.place, bf16[512,300]{1,0:T(8,128)(2,1)} %bitcast.15.rows_in, bf16[300,256]{1,0:T(8,128)(2,1)S(1)} %collective-permute-done.9.piece0, bf16[300,256]{1,0:T(8,128)(2,1)S(1)} %collective-permute-done.10.piece1, ...), custom_call_target="tpu_custom_call" | custom-call | flops 7549747200 | bytes 1048576 | tf_op jit(solution)/shard_map/pallas_call | solution.py:97
  106.4 4.4 %collective-permute-start.13 = (bf16[300,256]{1,0:T(8,128)(2,1)S(1)}, bf16[300,256]{1,0:T(8,128)(2,1)S(1)}, u32[]{:S(2)}, u32[]{:S(2)}) collective-permute-start(bf16[300,256]{1,0:T(8,128)(2,1)S(1)} %get-tuple-element.37), channel_id=1, source_target_pairs={{0,256},{64,320},{128,384},{192,448},{256,0},{320,64},{384,128},{4... | collective-permute-start | bytes 460808 | tf_op jit(solution)/shard_map/ppermute | solution.py:212
  110.8 2.9 %collective-permute-start.14 = (bf16[300,256]{1,0:T(8,128)(2,1)S(1)}, bf16[300,256]{1,0:T(8,128)(2,1)S(1)}, u32[]{:S(2)}, u32[]{:S(2)}) collective-permute-start(bf16[300,256]{1,0:T(8,128)(2,1)S(1)} %get-tuple-element.38), channel_id=1, source_target_pairs={{0,384},{64,448},{128,0},{192,64},{256,128},{320,192},{384,256},{4... | collective-permute-start | bytes 460808 | tf_op jit(solution)/shard_map/ppermute | solution.py:212
  113.7 13.6 %all-to-all-start.3 = ((bf16[64,8,300]{2,1,0:T(8,128)(2,1)}), bf16[64,8,300]{2,1,0:T(8,128)(2,1)S(1)}, u32[]{:S(2)}, u32[]{:S(2)}) async-start(bf16[64,8,300]{2,1,0:T(8,128)(2,1)} %bitcast.17), calls=%async_computation.3 | async-start | bytes 786432 | tf_op jit(solution)/shard_map/all_to_all | solution.py:233
  127.5 4.8 %collective-permute-start.15 = (bf16[300,128]{1,0:T(8,128)(2,1)S(1)}, bf16[300,128]{1,0:T(8,128)(2,1)S(1)}, u32[]{:S(2)}, u32[]{:S(2)}) collective-permute-start(bf16[300,128]{1,0:T(8,128)(2,1)S(1)} %select_convert_fusion), channel_id=1, source_target_pairs={{0,64},{64,0},{128,192},{192,128},{256,320},{320,256},{384,448},{4... | collective-permute-start | bytes 230408 | tf_op jit(solution)/shard_map/ppermute | solution.py:238
  132.3 6.6 %collective-permute-done.15 = bf16[300,128]{1,0:T(8,128)(2,1)S(1)} collective-permute-done((bf16[300,128]{1,0:T(8,128)(2,1)S(1)}, bf16[300,128]{1,0:T(8,128)(2,1)S(1)}, u32[]{:S(2)}, u32[]{:S(2)}) %collective-permute-start.15) | collective-permute-done | bytes 76832 | tf_op jit(solution)/shard_map/ppermute | solution.py:238
  139.6 5.1 %all-to-all-done.3 = bf16[64,8,300]{2,1,0:T(8,128)(2,1)S(1)} async-done(((bf16[64,8,300]{2,1,0:T(8,128)(2,1)}), bf16[64,8,300]{2,1,0:T(8,128)(2,1)S(1)}, u32[]{:S(2)}, u32[]{:S(2)}) %all-to-all-start.3) | async-done | bytes 307232 | tf_op jit(solution)/shard_map/all_to_all | solution.py:233
  (60 shorter events, 20.0 us)
Async XLA Ops:
  0.6 24.4 %copy-start.4 = (f32[300,128]{1,0:T(8,128)S(1)}, f32[300,128]{1,0:T(8,128)}, u32[]{:S(2)}) copy-start(f32[300,128]{1,0:T(8,128)} %param.10) | copy-start | bytes 460804
  0.6 24.4 %copy-start.5 = (f32[300,128]{1,0:T(8,128)S(1)}, f32[300,128]{1,0:T(8,128)}, u32[]{:S(2)}) copy-start(f32[300,128]{1,0:T(8,128)} %param.9) | copy-start | bytes 460804
  0.7 24.2 %copy-start.7 = (s32[512]{0:T(512)S(1)}, s32[512]{0:T(512)}, u32[]{:S(2)}) copy-start(s32[512]{0:T(512)} %param.12) | copy-start | bytes 6148
  1.7 26.6 %copy-start.6 = (s32[1024]{0:T(1024)S(1)}, s32[1024]{0:T(1024)}, u32[]{:S(2)}) copy-start(s32[1024]{0:T(1024)} %param.13) | copy-start | bytes 12292
  1.8 23.3 %collective-permute-start = (bf16[2,300,128]{2,1,0:T(8,128)(2,1)S(1)}, bf16[2,300,128]{2,1,0:T(8,128)(2,1)S(1)}, u32[]{:S(2)}, u32[]{:S(2)}) collective-permute-start(bf16[2,300,128]{2,1,0:T(8,128)(2,1)S(1)} %pad_maximum_fusion.2), channel_id=1, source_target_pairs={{0,64},{64,0},{128,192},{192,128},{256,320},{320,256},{384,448},{4... | collective-permute-start | bytes 460808 | tf_op jit(solution)/shard_map/ppermute | solution.py:191
  14.0 23.9 %all-to-all-start = ((bf16[32,16,300]{2,1,0:T(8,128)(2,1)}), bf16[32,16,300]{2,1,0:T(8,128)(2,1)S(1)}, u32[]{:S(2)}, u32[]{:S(2)}) async-start(bf16[32,16,300]{2,1,0:T(8,128)(2,1)} %broadcast_in_dim.19), calls=%async_computation | async-start | bytes 786432 | tf_op jit(solution)/shard_map/all_to_all | solution.py:202
  25.2 10.0 %collective-permute-start.3 = (bf16[300,256]{1,0:T(8,128)(2,1)S(1)}, bf16[300,256]{1,0:T(8,128)(2,1)S(1)}, u32[]{:S(2)}, u32[]{:S(2)}) collective-permute-start(bf16[300,256]{1,0:T(8,128)(2,1)S(1)} %fusion.6.piece0), channel_id=1, source_target_pairs={{0,128},{64,192},{128,256},{192,320},{256,384},{320,448},{384,0},{... | collective-permute-start | bytes 460808 | tf_op jit(solution)/shard_map/ppermute | solution.py:203
  28.3 13.2 %collective-permute-start.2 = (bf16[300,256]{1,0:T(8,128)(2,1)S(1)}, bf16[300,256]{1,0:T(8,128)(2,1)S(1)}, u32[]{:S(2)}, u32[]{:S(2)}) collective-permute-start(bf16[300,256]{1,0:T(8,128)(2,1)S(1)} %fusion.6.piece0), channel_id=1, source_target_pairs={{0,384},{64,448},{128,0},{192,64},{256,128},{320,192},{384,256},{4... | collective-permute-start | bytes 460808 | tf_op jit(solution)/shard_map/ppermute | solution.py:203
  31.7 9.8 %collective-permute-start.1 = (bf16[300,256]{1,0:T(8,128)(2,1)S(1)}, bf16[300,256]{1,0:T(8,128)(2,1)S(1)}, u32[]{:S(2)}, u32[]{:S(2)}) collective-permute-start(bf16[300,256]{1,0:T(8,128)(2,1)S(1)} %fusion.6.piece0), channel_id=1, source_target_pairs={{0,256},{64,320},{128,384},{192,448},{256,0},{320,64},{384,128},{4... | collective-permute-start | bytes 460808 | tf_op jit(solution)/shard_map/ppermute | solution.py:203
  46.0 18.8 %all-to-all-start.1 = ((bf16[32,16,300]{2,1,0:T(8,128)(2,1)}), bf16[32,16,300]{2,1,0:T(8,128)(2,1)S(1)}, u32[]{:S(2)}, u32[]{:S(2)}) async-start(bf16[32,16,300]{2,1,0:T(8,128)(2,1)} %bitcast.12), calls=%async_computation.1 | async-start | bytes 786432 | tf_op jit(solution)/shard_map/all_to_all | solution.py:216
  53.3 17.7 %collective-permute-start.5 = (bf16[300,256]{1,0:T(8,128)(2,1)S(1)}, bf16[300,256]{1,0:T(8,128)(2,1)S(1)}, u32[]{:S(2)}, u32[]{:S(2)}) collective-permute-start(bf16[300,256]{1,0:T(8,128)(2,1)S(1)} %get-tuple-element.25), channel_id=1, source_target_pairs={{0,128},{64,192},{128,256},{192,320},{256,384},{320,448},{384,0},{... | collective-permute-start | bytes 460808 | tf_op jit(solution)/shard_map/ppermute | solution.py:212
  55.5 15.5 %collective-permute-start.6 = (bf16[300,256]{1,0:T(8,128)(2,1)S(1)}, bf16[300,256]{1,0:T(8,128)(2,1)S(1)}, u32[]{:S(2)}, u32[]{:S(2)}) collective-permute-start(bf16[300,256]{1,0:T(8,128)(2,1)S(1)} %get-tuple-element.26), channel_id=1, source_target_pairs={{0,256},{64,320},{128,384},{192,448},{256,0},{320,64},{384,128},{4... | collective-permute-start | bytes 460808 | tf_op jit(solution)/shard_map/ppermute | solution.py:212
  59.8 11.1 %collective-permute-start.7 = (bf16[300,256]{1,0:T(8,128)(2,1)S(1)}, bf16[300,256]{1,0:T(8,128)(2,1)S(1)}, u32[]{:S(2)}, u32[]{:S(2)}) collective-permute-start(bf16[300,256]{1,0:T(8,128)(2,1)S(1)} %get-tuple-element.27), channel_id=1, source_target_pairs={{0,384},{64,448},{128,0},{192,64},{256,128},{320,192},{384,256},{4... | collective-permute-start | bytes 460808 | tf_op jit(solution)/shard_map/ppermute | solution.py:212
  64.9 11.3 %collective-permute-start.4 = (f32[16,300]{1,0:T(8,128)S(1)}, f32[16,300]{1,0:T(8,128)S(1)}, u32[]{:S(2)}, u32[]{:S(2)}) collective-permute-start(f32[16,300]{1,0:T(8,128)S(1)} %convert_reduce_fusion.1.near), channel_id=1, source_target_pairs={{0,1},{1,0},{2,3},{3,2},{4,5},{5,4},{6,7},{7,6},{8,9},{9,8},{10,11... | collective-permute-start | bytes 57608 | tf_op jit(solution)/shard_map/ppermute | solution.py:220
  71.7 12.7 %collective-permute-start.8 = (bf16[300,256]{1,0:T(8,128)(2,1)}, bf16[300,256]{1,0:T(8,128)(2,1)}, u32[]{:S(2)}, u32[]{:S(2)}) collective-permute-start(bf16[300,256]{1,0:T(8,128)(2,1)} %get-tuple-element.42.after), channel_id=1, source_target_pairs={{0,64},{64,0},{128,192},{192,128},{256,320},{320,256},{384,448},{4... | collective-permute-start | bytes 460808 | tf_op jit(solution)/shard_map/ppermute | solution.py:215
  76.9 19.1 %all-to-all-start.2 = ((bf16[32,16,300]{2,1,0:T(8,128)(2,1)}), bf16[32,16,300]{2,1,0:T(8,128)(2,1)}, u32[]{:S(2)}, u32[]{:S(2)}) async-start(bf16[32,16,300]{2,1,0:T(8,128)(2,1)} %get-tuple-element.29), calls=%async_computation.2 | async-start | bytes 786432 | tf_op jit(solution)/shard_map/all_to_all | solution.py:202
  85.5 9.2 %collective-permute-start.11 = (bf16[300,256]{1,0:T(8,128)(2,1)S(1)}, bf16[300,256]{1,0:T(8,128)(2,1)S(1)}, u32[]{:S(2)}, u32[]{:S(2)}) collective-permute-start(bf16[300,256]{1,0:T(8,128)(2,1)S(1)} %get-tuple-element.30.piece0), channel_id=1, source_target_pairs={{0,128},{64,192},{128,256},{192,320},{256,384},{320,448},{384,0},{... | collective-permute-start | bytes 460808 | tf_op jit(solution)/shard_map/ppermute | solution.py:203
  87.9 11.6 %collective-permute-start.10 = (bf16[300,256]{1,0:T(8,128)(2,1)S(1)}, bf16[300,256]{1,0:T(8,128)(2,1)S(1)}, u32[]{:S(2)}, u32[]{:S(2)}) collective-permute-start(bf16[300,256]{1,0:T(8,128)(2,1)S(1)} %get-tuple-element.30.piece0), channel_id=1, source_target_pairs={{0,384},{64,448},{128,0},{192,64},{256,128},{320,192},{384,256},{4... | collective-permute-start | bytes 460808 | tf_op jit(solution)/shard_map/ppermute | solution.py:203
  92.1 7.7 %collective-permute-start.9 = (bf16[300,256]{1,0:T(8,128)(2,1)S(1)}, bf16[300,256]{1,0:T(8,128)(2,1)S(1)}, u32[]{:S(2)}, u32[]{:S(2)}) collective-permute-start(bf16[300,256]{1,0:T(8,128)(2,1)S(1)} %get-tuple-element.30.piece0), channel_id=1, source_target_pairs={{0,256},{64,320},{128,384},{192,448},{256,0},{320,64},{384,128},{4... | collective-permute-start | bytes 460808 | tf_op jit(solution)/shard_map/ppermute | solution.py:203
  104.1 23.2 %collective-permute-start.12 = (bf16[300,256]{1,0:T(8,128)(2,1)S(1)}, bf16[300,256]{1,0:T(8,128)(2,1)S(1)}, u32[]{:S(2)}, u32[]{:S(2)}) collective-permute-start(bf16[300,256]{1,0:T(8,128)(2,1)S(1)} %get-tuple-element.36), channel_id=1, source_target_pairs={{0,128},{64,192},{128,256},{192,320},{256,384},{320,448},{384,0},{... | collective-permute-start | bytes 460808 | tf_op jit(solution)/shard_map/ppermute | solution.py:212
  106.4 21.0 %collective-permute-start.13 = (bf16[300,256]{1,0:T(8,128)(2,1)S(1)}, bf16[300,256]{1,0:T(8,128)(2,1)S(1)}, u32[]{:S(2)}, u32[]{:S(2)}) collective-permute-start(bf16[300,256]{1,0:T(8,128)(2,1)S(1)} %get-tuple-element.37), channel_id=1, source_target_pairs={{0,256},{64,320},{128,384},{192,448},{256,0},{320,64},{384,128},{4... | collective-permute-start | bytes 460808 | tf_op jit(solution)/shard_map/ppermute | solution.py:212
  110.8 16.6 %collective-permute-start.14 = (bf16[300,256]{1,0:T(8,128)(2,1)S(1)}, bf16[300,256]{1,0:T(8,128)(2,1)S(1)}, u32[]{:S(2)}, u32[]{:S(2)}) collective-permute-start(bf16[300,256]{1,0:T(8,128)(2,1)S(1)} %get-tuple-element.38), channel_id=1, source_target_pairs={{0,384},{64,448},{128,0},{192,64},{256,128},{320,192},{384,256},{4... | collective-permute-start | bytes 460808 | tf_op jit(solution)/shard_map/ppermute | solution.py:212
  113.7 31.0 %all-to-all-start.3 = ((bf16[64,8,300]{2,1,0:T(8,128)(2,1)}), bf16[64,8,300]{2,1,0:T(8,128)(2,1)S(1)}, u32[]{:S(2)}, u32[]{:S(2)}) async-start(bf16[64,8,300]{2,1,0:T(8,128)(2,1)} %bitcast.17), calls=%async_computation.3 | async-start | bytes 786432 | tf_op jit(solution)/shard_map/all_to_all | solution.py:233
  127.5 11.3 %collective-permute-start.15 = (bf16[300,128]{1,0:T(8,128)(2,1)S(1)}, bf16[300,128]{1,0:T(8,128)(2,1)S(1)}, u32[]{:S(2)}, u32[]{:S(2)}) collective-permute-start(bf16[300,128]{1,0:T(8,128)(2,1)S(1)} %select_convert_fusion), channel_id=1, source_target_pairs={{0,64},{64,0},{128,192},{192,128},{256,320},{320,256},{384,448},{4... | collective-permute-start | bytes 230408 | tf_op jit(solution)/shard_map/ppermute | solution.py:238
  (4 other events, 52.9 us)

commit v5 on v4

--- a/solution.py
+++ b/solution.py
@@ -67,6 +67,17 @@
             weight = 0.1 + 0.25 * (value * lax.rsqrt(value))
             zero = 0.5 * jnp.tanh(0.5 * diff) + 0.5
             slope[at, here[k]] = jnp.where(count > 0, weight * diff, zero).astype(jnp.bfloat16)
+    total = lax.dot_general(
+        slope[...], cols[...], (((1,), (1,)), ((), ())), preferred_element_type=jnp.float32
+    )
+    if first:
+        part[...] = total
+        done.append(start(part, rows_out, out_sem.at[2]))
+    else:
+        part_copy.wait()
+        grad_rows[...] = (part[...] + total).astype(jnp.bfloat16)
+        done.append(start(grad_rows, rows_out, out_sem.at[2]))
+    for k in range(2):
         grad = jnp.dot(rows_t[...], slope[:, here[k]], preferred_element_type=jnp.float32)
         if steps[k] == 0:
             grad_own[...] = grad
@@ -74,16 +85,6 @@
         else:
             grad_away[k] = grad.astype(jnp.bfloat16)
             done.append(start(grad_away.at[k], outs[k], out_sem.at[k]))
-    total = lax.dot_general(
-        slope[...], cols[...], (((1,), (1,)), ((), ())), preferred_element_type=jnp.float32
-    )
-    if first:
-        part[...] = total
-        done.append(start(part, rows_out, out_sem.at[2]))
-    else:
-        part_copy.wait()
-        grad_rows[...] = (part[...] + total).astype(jnp.bfloat16)
-        done.append(start(grad_rows, rows_out, out_sem.at[2]))
     for copy in done:
         copy.wait()
 
@@ -151,7 +152,14 @@
     send[...] = jnp.broadcast_to(new_emb.astype(jnp.bfloat16)[None], send.shape)
 
 
-def pair_kernel(scale, col_sum, away, emb, acc, emb_out, acc_out, send):
+def last_kernel(scale, near, far, emb, acc, after, emb_out, acc_out):
+    grad = (near[...] + far[...].astype(jnp.float32)) * scale
+    new_emb, new_acc = adagrad(emb[...], acc[...], grad)
+    emb_out[...] = new_emb
+    acc_out[...] = new_acc
+
+
+def pair_kernel(scale, col_sum, away, emb, acc, after, emb_out, acc_out, send):
     grad = (col_sum[...] + away[...].astype(jnp.float32)) * scale
     new_emb, new_acc = adagrad(emb[...], acc[...], grad)
     emb_out[...] = new_emb
@@ -196,6 +204,7 @@
     pair_acc = in_order(col_acc, other[1])
     pair_send = pair_emb.astype(jnp.bfloat16)
     vmem = pl.BlockSpec(memory_space=pltpu.VMEM)
+    anywhere = pl.BlockSpec(memory_space=pl.ANY)
     in_hbm = lambda values: pltpu.with_memory_space_constraint(values, pltpu.HBM)
     own = lambda wide: jnp.where(odd, wide[:, half:], wide[:, :half])
     for step in range(2):
@@ -210,34 +219,43 @@
         col_sum = grads[1]
         for d in (1, 2, 3):
             col_sum = col_sum + lax.ppermute(grads[1 + d], "row", step_by(d)).astype(jnp.float32)
+        parts = lax.all_to_all(
+            grads[0].reshape(to_all.shape), "col", 0, 0, axis_index_groups=chips
+        )
+        near = jnp.sum(parts.astype(jnp.float32), axis=0)
         if step == 0:
+            far = lax.ppermute(near, "col", swap)
             half_sum = col_sum.astype(jnp.bfloat16)
             away = lax.ppermute(half_sum, "row", pair)
-            parts = lax.all_to_all(
-                grads[0].reshape(to_all.shape), "col", 0, 0, axis_index_groups=chips
-            )
-            near = jnp.sum(parts.astype(jnp.float32), axis=0)
-            far = lax.ppermute(near, "col", swap)
             shared_emb, shared_acc, row_send = whole_call(
                 functools.partial(row_kernel, row_scale),
                 [full(shared_emb.shape), full(shared_emb.shape), to_all],
                 ROW_COST,
-                [vmem, vmem, vmem, vmem, pl.BlockSpec(memory_space=pl.ANY)],
+                [vmem, vmem, vmem, vmem, anywhere],
             )(near, far, shared_emb, shared_acc, half_sum)
             pair_emb, pair_acc, pair_send = whole_call(
                 functools.partial(pair_kernel, col_scale),
                 [full(pair_emb.shape), full(pair_emb.shape), full(pair_emb.shape, jnp.bfloat16)],
                 PAIR_COST,
-            )(col_sum, away, pair_emb, pair_acc)
+                [vmem, vmem, vmem, vmem, anywhere],
+            )(col_sum, away, pair_emb, pair_acc, row_send)
         else:
-            parts = lax.all_to_all(grads[0].reshape(n_col, few, width), "col", 0, 0)
-            row_grad = jnp.sum(parts.astype(jnp.float32), axis=0) * row_scale
             mine = lambda both: jnp.where(second, both[few:], both[:few])
-            row_emb, row_acc = adagrad(mine(shared_emb), mine(shared_acc), row_grad)
-            away = jnp.where(odd, col_sum[:, :half], col_sum[:, half:]).astype(jnp.bfloat16)
-            away = lax.ppermute(away, "row", pair).astype(jnp.float32)
-            col_grad = (own(col_sum) + away) * col_scale
-            col_emb, col_acc = adagrad(own(pair_emb), own(pair_acc), col_grad)
+            far = lax.ppermute(jnp.where(second, near[:few], near[few:]), "col", swap)
+            half_sum = jnp.where(odd, col_sum[:, :half], col_sum[:, half:]).astype(jnp.bfloat16)
+            away = lax.ppermute(half_sum, "row", pair)
+            row_emb, row_acc = whole_call(
+                functools.partial(last_kernel, row_scale),
+                [full(row_emb.shape)] * 2,
+                1 << 20,
+                [vmem, vmem, vmem, vmem, anywhere],
+            )(mine(near), far, mine(shared_emb), mine(shared_acc), half_sum)
+            col_emb, col_acc = whole_call(
+                functools.partial(last_kernel, col_scale),
+                [full(col_emb.shape)] * 2,
+                1 << 20,
+                [vmem, vmem, vmem, vmem, anywhere],
+            )(own(col_sum), away, own(pair_emb), own(pair_acc), row_emb)
     return (row_emb.T, row_acc.T, col_emb, col_acc)
 
 

time: 147 us -> 143 us (0.973)
  waiting for transfers between devices: 17.9 us -> 11.3 us
  starting transfers between devices: 101 us -> 103 us
    all_to_all x1 -> x0, starting transfers between devices: 13.6 us -> none  [on_device(): parts = lax.all_to_all(grads[0].reshape(n_col, few, width), 'col', 0, 0)]
    all_to_all x1 -> x2, starting transfers between devices: 7.24 us -> 16.6 us  [on_device(): lax.all_to_all(grads[0].reshape(to_all.shape), 'col', 0, 0, axis_index_gr...]
    ppermute x1, waiting for transfers between devices: 6.55 us -> 0.79 us  [on_device(): far = lax.ppermute(jnp.where(second, near[:few], near[few:]), 'col', swap)]
    all_to_all x1 -> x0, waiting for transfers between devices: 5.11 us -> none  [on_device(): parts = lax.all_to_all(grads[0].reshape(n_col, few, width), 'col', 0, 0)]
    ppermute x1 -> x2, starting transfers between devices: 4.42 us -> 9.17 us  [on_device(): away = lax.ppermute(half_sum, 'row', pair)]
    ppermute x6, waiting for transfers between devices: 0.02 us -> 3.96 us  [on_device(): lax.ppermute(grads[1 + d], 'row', step_by(d)).astype(jnp.float32)]
    ppermute x1, starting transfers between devices: 4.76 us -> 7.9 us  [on_device(): far = lax.ppermute(jnp.where(second, near[:few], near[few:]), 'col', swap)]
    pallas_call x4, Pallas kernels: 15.7 us -> 13.8 us  [tile_grads(): pl.pallas_call(functools.partial(tile_kernel, steps, first), in_specs=[pl...]
  transfers between devices with their start and end apart: 20 -> 21, of which waited for: 6 -> 7; matrix products, arithmetic and copies ran while one was open for 2% -> 2% of each run, Pallas kernels for 6% -> 7%
where the time goes in v5:
time: 143 us; the launch traced here: 140 us
  starting transfers between devices  103 us (72%)
  Pallas kernels  17.2 us (12%)
  waiting for transfers between devices  11.3 us (8%)
  other arithmetic  3.07 us (2%)
  blocking collectives  2.44 us (2%)
  local copies, waits for them, and re-layouts  1.68 us (1%)
    ppermute x6, starting transfers between devices, on_device(): lax.ppermute(pair_send, 'row', step_by(-d))  18.9 us
    all_to_all x2, starting transfers between devices, on_device(): lax.all_to_all(row_send, 'col', 0, 0, axis_index_groups=chips)  18.2 us
    ppermute x6, starting transfers between devices, on_device(): lax.ppermute(grads[1 + d], 'row', step_by(d)).astype(jnp.float32)  18.2 us
    all_to_all x2, starting transfers between devices, on_device(): lax.all_to_all(grads[0].reshape(to_all.shape), 'col', 0, 0, axis_index_gr...  16.6 us
    pallas_call x4, Pallas kernels, tile_grads(): pl.pallas_call(functools.partial(tile_kernel, steps, first), in_specs=[pl...  13.8 us
    ppermute x2, starting transfers between devices, on_device(): away = lax.ppermute(half_sum, 'row', pair)  9.17 us
    ppermute x1, starting transfers between devices, on_device(): other = lax.ppermute(both, 'row', pair).astype(jnp.float32)  8.28 us
    ppermute x1, starting transfers between devices, on_device(): far = lax.ppermute(jnp.where(second, near[:few], near[few:]), 'col', swap)  7.9 us
  transfers between devices with their start and end apart: 21, of which 7 were waited for; matrix products, arithmetic and copies ran while one was open for 2% of the time, Pallas kernels for 7%

profile of v5, /device:TPU:1, one launch (start us, length us, event | category | flops | bytes accessed | tf_op | source)
XLA Modules:
  0.0 140.2 jit_solution(855504976043599205)
XLA Ops:
  1.8 8.3 %collective-permute-start = (bf16[2,300,128]{2,1,0:T(8,128)(2,1)S(1)}, bf16[2,300,128]{2,1,0:T(8,128)(2,1)S(1)}, u32[]{:S(2)}, u32[]{:S(2)}) collective-permute-start(bf16[2,300,128]{2,1,0:T(8,128)(2,1)S(1)} %pad_maximum_fusion.2), channel_id=1, source_target_pairs={{0,64},{64,0},{128,192},{192,128},{256,320},{320,256},{384,448},{4... | collective-permute-start | bytes 460808 | tf_op jit(solution)/shard_map/ppermute | solution.py:199
  10.8 2.4 %all_gather.3 = f32[2,16,300]{2,1,0:T(8,128)S(1)} all-gather(f32[2,8,300]{2,1,0:T(8,128)S(1)} %pad_maximum_fusion.3), channel_id=1, replica_groups={{0,1},{2,3},{4,5},{6,7},{8,9},{10,11},{12,13},{14,15},{16,17},{18,19},{..., dimensions={1}, use_global_device_ids=true | all-gather | bytes 57600 | tf_op jit(solution)/shard_map/all_gather | solution.py:194
  14.0 10.8 %all-to-all-start = ((bf16[32,16,300]{2,1,0:T(8,128)(2,1)}), bf16[32,16,300]{2,1,0:T(8,128)(2,1)S(1)}, u32[]{:S(2)}, u32[]{:S(2)}) async-start(bf16[32,16,300]{2,1,0:T(8,128)(2,1)} %broadcast_in_dim.19), calls=%async_computation | async-start | bytes 786432 | tf_op jit(solution)/shard_map/all_to_all | solution.py:211
  25.2 3.1 %collective-permute-start.3 = (bf16[300,256]{1,0:T(8,128)(2,1)S(1)}, bf16[300,256]{1,0:T(8,128)(2,1)S(1)}, u32[]{:S(2)}, u32[]{:S(2)}) collective-permute-start(bf16[300,256]{1,0:T(8,128)(2,1)S(1)} %fusion.5.piece0), channel_id=1, source_target_pairs={{0,128},{64,192},{128,256},{192,320},{256,384},{320,448},{384,0},{... | collective-permute-start | bytes 460808 | tf_op jit(solution)/shard_map/ppermute | solution.py:212
  28.3 3.4 %collective-permute-start.2 = (bf16[300,256]{1,0:T(8,128)(2,1)S(1)}, bf16[300,256]{1,0:T(8,128)(2,1)S(1)}, u32[]{:S(2)}, u32[]{:S(2)}) collective-permute-start(bf16[300,256]{1,0:T(8,128)(2,1)S(1)} %fusion.5.piece0), channel_id=1, source_target_pairs={{0,384},{64,448},{128,0},{192,64},{256,128},{320,192},{384,256},{4... | collective-permute-start | bytes 460808 | tf_op jit(solution)/shard_map/ppermute | solution.py:212
  31.7 3.4 %collective-permute-start.1 = (bf16[300,256]{1,0:T(8,128)(2,1)S(1)}, bf16[300,256]{1,0:T(8,128)(2,1)S(1)}, u32[]{:S(2)}, u32[]{:S(2)}) collective-permute-start(bf16[300,256]{1,0:T(8,128)(2,1)S(1)} %fusion.5.piece0), channel_id=1, source_target_pairs={{0,256},{64,320},{128,384},{192,448},{256,0},{320,64},{384,128},{4... | collective-permute-start | bytes 460808 | tf_op jit(solution)/shard_map/ppermute | solution.py:212
  35.2 2.8 %all-to-all-done = bf16[32,16,300]{2,1,0:T(8,128)(2,1)S(1)} async-done(((bf16[32,16,300]{2,1,0:T(8,128)(2,1)}), bf16[32,16,300]{2,1,0:T(8,128)(2,1)S(1)}, u32[]{:S(2)}, u32[]{:S(2)}) %all-to-all-start) | async-done | bytes 307232 | tf_op jit(solution)/shard_map/all_to_all | solution.py:211
  38.0 3.4 %shard_map.102 = (f32[512,300]{1,0:T(8,128)S(1)}, f32[300,256]{1,0:T(8,128)S(1)}, bf16[300,256]{1,0:T(8,128)(2,1)S(1)}) custom-call(s32[1]{0:T(128)} %bitcast.place, bf16[512,300]{1,0:T(8,128)(2,1)S(1)} %bitcast.37, bf16[300,256]{1,0:T(8,128)(2,1)S(1)} %fusion.5.piece0, bf16[300,256]{1,0:T(8,128)(2,1)S(1)} %collective-permute-done.3.piece1, ...), custom_call_target="tpu_custom_call" | custom-call | flops 7549747200 | bytes 1048576 | tf_op jit(solution)/shard_map/pallas_call | solution.py:98
  41.4 3.6 %shard_map.103 = (bf16[512,300]{1,0:T(8,128)(2,1)}, bf16[300,256]{1,0:T(8,128)(2,1)S(1)}, bf16[300,256]{1,0:T(8,128)(2,1)S(1)}) custom-call(s32[1]{0:T(128)} %bitcast.place, bf16[512,300]{1,0:T(8,128)(2,1)S(1)} %bitcast.38, bf16[300,256]{1,0:T(8,128)(2,1)S(1)} %collective-permute-done.1.piece0, bf16[300,256]{1,0:T(8,128)(2,1)S(1)} %collective-permute-done.2.piece1, ...), custom_call_target="tpu_custom_call" | custom-call | flops 7549747200 | bytes 1048576 | tf_op jit(solution)/shard_map/pallas_call | solution.py:98
  45.0 7.3 %all-to-all-start.1 = ((bf16[32,16,300]{2,1,0:T(8,128)(2,1)}), bf16[32,16,300]{2,1,0:T(8,128)(2,1)S(1)}, u32[]{:S(2)}, u32[]{:S(2)}) async-start(bf16[32,16,300]{2,1,0:T(8,128)(2,1)} %bitcast.12), calls=%async_computation.1 | async-start | bytes 786432 | tf_op jit(solution)/shard_map/all_to_all | solution.py:222
  54.6 4.2 %collective-permute-start.6 = (bf16[300,256]{1,0:T(8,128)(2,1)S(1)}, bf16[300,256]{1,0:T(8,128)(2,1)S(1)}, u32[]{:S(2)}, u32[]{:S(2)}) collective-permute-start(bf16[300,256]{1,0:T(8,128)(2,1)S(1)} %get-tuple-element.30), channel_id=1, source_target_pairs={{0,256},{64,320},{128,384},{192,448},{256,0},{320,64},{384,128},{4... | collective-permute-start | bytes 460808 | tf_op jit(solution)/shard_map/ppermute | solution.py:221
  58.9 3.1 %collective-permute-start.7 = (bf16[300,256]{1,0:T(8,128)(2,1)S(1)}, bf16[300,256]{1,0:T(8,128)(2,1)S(1)}, u32[]{:S(2)}, u32[]{:S(2)}) collective-permute-start(bf16[300,256]{1,0:T(8,128)(2,1)S(1)} %get-tuple-element.31), channel_id=1, source_target_pairs={{0,384},{64,448},{128,0},{192,64},{256,128},{320,192},{384,256},{4... | collective-permute-start | bytes 460808 | tf_op jit(solution)/shard_map/ppermute | solution.py:221
  64.0 6.0 %collective-permute-start.4 = (f32[16,300]{1,0:T(8,128)S(1)}, f32[16,300]{1,0:T(8,128)S(1)}, u32[]{:S(2)}, u32[]{:S(2)}) collective-permute-start(f32[16,300]{1,0:T(8,128)S(1)} %convert_reduce_fusion.1.near), channel_id=1, source_target_pairs={{0,1},{1,0},{2,3},{3,2},{4,5},{5,4},{6,7},{7,6},{8,9},{9,8},{10,11... | collective-permute-start | bytes 57608 | tf_op jit(solution)/shard_map/ppermute | solution.py:227
  70.8 4.4 %collective-permute-start.8 = (bf16[300,256]{1,0:T(8,128)(2,1)}, bf16[300,256]{1,0:T(8,128)(2,1)}, u32[]{:S(2)}, u32[]{:S(2)}) collective-permute-start(bf16[300,256]{1,0:T(8,128)(2,1)} %get-tuple-element.48.after), channel_id=1, source_target_pairs={{0,64},{64,0},{128,192},{192,128},{256,320},{320,256},{384,448},{4... | collective-permute-start | bytes 460808 | tf_op jit(solution)/shard_map/ppermute | solution.py:229
  76.1 7.4 %all-to-all-start.2 = ((bf16[32,16,300]{2,1,0:T(8,128)(2,1)}), bf16[32,16,300]{2,1,0:T(8,128)(2,1)}, u32[]{:S(2)}, u32[]{:S(2)}) async-start(bf16[32,16,300]{2,1,0:T(8,128)(2,1)} %get-tuple-element.32.after), calls=%async_computation.2 | async-start | bytes 786432 | tf_op jit(solution)/shard_map/all_to_all | solution.py:211
  87.0 4.2 %collective-permute-start.10 = (bf16[300,256]{1,0:T(8,128)(2,1)S(1)}, bf16[300,256]{1,0:T(8,128)(2,1)S(1)}, u32[]{:S(2)}, u32[]{:S(2)}) collective-permute-start(bf16[300,256]{1,0:T(8,128)(2,1)S(1)} %get-tuple-element.33.piece0), channel_id=1, source_target_pairs={{0,384},{64,448},{128,0},{192,64},{256,128},{320,192},{384,256},{4... | collective-permute-start | bytes 460808 | tf_op jit(solution)/shard_map/ppermute | solution.py:212
  91.2 2.5 %collective-permute-start.9 = (bf16[300,256]{1,0:T(8,128)(2,1)S(1)}, bf16[300,256]{1,0:T(8,128)(2,1)S(1)}, u32[]{:S(2)}, u32[]{:S(2)}) collective-permute-start(bf16[300,256]{1,0:T(8,128)(2,1)S(1)} %get-tuple-element.33.piece0), channel_id=1, source_target_pairs={{0,256},{64,320},{128,384},{192,448},{256,0},{320,64},{384,128},{4... | collective-permute-start | bytes 460808 | tf_op jit(solution)/shard_map/ppermute | solution.py:212
  95.2 3.3 %shard_map.106 = (f32[512,300]{1,0:T(8,128)S(1)}, f32[300,256]{1,0:T(8,128)S(1)}, bf16[300,256]{1,0:T(8,128)(2,1)S(1)}) custom-call(s32[1]{0:T(128)} %bitcast.place, bf16[512,300]{1,0:T(8,128)(2,1)} %bitcast.15.rows_in, bf16[300,256]{1,0:T(8,128)(2,1)S(1)} %get-tuple-element.33.piece0, bf16[300,256]{1,0:T(8,128)(2,1)S(1)} %collective-permute-done.11.piece1, ...), custom_call_target="tpu_custom_call" | custom-call | flops 7549747200 | bytes 1048576 | tf_op jit(solution)/shard_map/pallas_call | solution.py:98
  98.9 3.5 %shard_map.107 = (bf16[512,300]{1,0:T(8,128)(2,1)}, bf16[300,256]{1,0:T(8,128)(2,1)S(1)}, bf16[300,256]{1,0:T(8,128)(2,1)S(1)}) custom-call(s32[1]{0:T(128)} %bitcast.place, bf16[512,300]{1,0:T(8,128)(2,1)} %bitcast.15.rows_in, bf16[300,256]{1,0:T(8,128)(2,1)S(1)} %collective-permute-done.9.piece0, bf16[300,256]{1,0:T(8,128)(2,1)S(1)} %collective-permute-done.10.piece1, ...), custom_call_target="tpu_custom_call" | custom-call | flops 7549747200 | bytes 1048576 | tf_op jit(solution)/shard_map/pallas_call | solution.py:98
  102.4 9.3 %all-to-all-start.3 = ((bf16[32,16,300]{2,1,0:T(8,128)(2,1)}), bf16[32,16,300]{2,1,0:T(8,128)(2,1)S(1)}, u32[]{:S(2)}, u32[]{:S(2)}) async-start(bf16[32,16,300]{2,1,0:T(8,128)(2,1)} %bitcast.17), calls=%async_computation.3 | async-start | bytes 786432 | tf_op jit(solution)/shard_map/all_to_all | solution.py:222
  113.6 4.5 %collective-permute-start.14 = (bf16[300,256]{1,0:T(8,128)(2,1)S(1)}, bf16[300,256]{1,0:T(8,128)(2,1)S(1)}, u32[]{:S(2)}, u32[]{:S(2)}) collective-permute-start(bf16[300,256]{1,0:T(8,128)(2,1)S(1)} %get-tuple-element.40), channel_id=1, source_target_pairs={{0,256},{64,320},{128,384},{192,448},{256,0},{320,64},{384,128},{4... | collective-permute-start | bytes 460808 | tf_op jit(solution)/shard_map/ppermute | solution.py:221
  121.7 2.7 %collective-permute-done.15 = bf16[300,256]{1,0:T(8,128)(2,1)S(1)} collective-permute-done((bf16[300,256]{1,0:T(8,128)(2,1)S(1)}, bf16[300,256]{1,0:T(8,128)(2,1)S(1)}, u32[]{:S(2)}, u32[]{:S(2)}) %collective-permute-start.15) | collective-permute-done | bytes 153632 | tf_op jit(solution)/shard_map/ppermute | solution.py:221
  124.5 4.7 %collective-permute-start.16 = (bf16[300,128]{1,0:T(8,128)(2,1)S(1)}, bf16[300,128]{1,0:T(8,128)(2,1)S(1)}, u32[]{:S(2)}, u32[]{:S(2)}) collective-permute-start(bf16[300,128]{1,0:T(8,128)(2,1)S(1)} %select_convert_fusion.after), channel_id=1, source_target_pairs={{0,64},{64,0},{128,192},{192,128},{256,320},{320,256},{384,448},{4... | collective-permute-start | bytes 230408 | tf_op jit(solution)/shard_map/ppermute | solution.py:246
  129.4 7.9 %collective-permute-start.12 = (f32[8,300]{1,0:T(8,128)S(1)}, f32[8,300]{1,0:T(8,128)S(1)}, u32[]{:S(2)}, u32[]{:S(2)}) collective-permute-start(f32[8,300]{1,0:T(8,128)S(1)} %get-tuple-element.58), channel_id=1, source_target_pairs={{0,1},{1,0},{2,3},{3,2},{4,5},{5,4},{6,7},{7,6},{8,9},{9,8},{10,11... | collective-permute-start | bytes 28808 | tf_op jit(solution)/shard_map/ppermute | solution.py:244
  (70 shorter events, 22.7 us)
Async XLA Ops:
  0.6 24.4 %copy-start.5 = (f32[300,128]{1,0:T(8,128)S(1)}, f32[300,128]{1,0:T(8,128)}, u32[]{:S(2)}) copy-start(f32[300,128]{1,0:T(8,128)} %param.10) | copy-start | bytes 460804
  0.6 24.4 %copy-start.6 = (f32[300,128]{1,0:T(8,128)S(1)}, f32[300,128]{1,0:T(8,128)}, u32[]{:S(2)}) copy-start(f32[300,128]{1,0:T(8,128)} %param.9) | copy-start | bytes 460804
  1.7 26.6 %copy-start.7 = (s32[1024]{0:T(1024)S(1)}, s32[1024]{0:T(1024)}, u32[]{:S(2)}) copy-start(s32[1024]{0:T(1024)} %param.13) | copy-start | bytes 12292
  1.8 23.2 %collective-permute-start = (bf16[2,300,128]{2,1,0:T(8,128)(2,1)S(1)}, bf16[2,300,128]{2,1,0:T(8,128)(2,1)S(1)}, u32[]{:S(2)}, u32[]{:S(2)}) collective-permute-start(bf16[2,300,128]{2,1,0:T(8,128)(2,1)S(1)} %pad_maximum_fusion.2), channel_id=1, source_target_pairs={{0,64},{64,0},{128,192},{192,128},{256,320},{320,256},{384,448},{4... | collective-permute-start | bytes 460808 | tf_op jit(solution)/shard_map/ppermute | solution.py:199
  14.0 23.9 %all-to-all-start = ((bf16[32,16,300]{2,1,0:T(8,128)(2,1)}), bf16[32,16,300]{2,1,0:T(8,128)(2,1)S(1)}, u32[]{:S(2)}, u32[]{:S(2)}) async-start(bf16[32,16,300]{2,1,0:T(8,128)(2,1)} %broadcast_in_dim.19), calls=%async_computation | async-start | bytes 786432 | tf_op jit(solution)/shard_map/all_to_all | solution.py:211
  25.2 10.0 %collective-permute-start.3 = (bf16[300,256]{1,0:T(8,128)(2,1)S(1)}, bf16[300,256]{1,0:T(8,128)(2,1)S(1)}, u32[]{:S(2)}, u32[]{:S(2)}) collective-permute-start(bf16[300,256]{1,0:T(8,128)(2,1)S(1)} %fusion.5.piece0), channel_id=1, source_target_pairs={{0,128},{64,192},{128,256},{192,320},{256,384},{320,448},{384,0},{... | collective-permute-start | bytes 460808 | tf_op jit(solution)/shard_map/ppermute | solution.py:212
  28.3 13.1 %collective-permute-start.2 = (bf16[300,256]{1,0:T(8,128)(2,1)S(1)}, bf16[300,256]{1,0:T(8,128)(2,1)S(1)}, u32[]{:S(2)}, u32[]{:S(2)}) collective-permute-start(bf16[300,256]{1,0:T(8,128)(2,1)S(1)} %fusion.5.piece0), channel_id=1, source_target_pairs={{0,384},{64,448},{128,0},{192,64},{256,128},{320,192},{384,256},{4... | collective-permute-start | bytes 460808 | tf_op jit(solution)/shard_map/ppermute | solution.py:212
  31.7 9.7 %collective-permute-start.1 = (bf16[300,256]{1,0:T(8,128)(2,1)S(1)}, bf16[300,256]{1,0:T(8,128)(2,1)S(1)}, u32[]{:S(2)}, u32[]{:S(2)}) collective-permute-start(bf16[300,256]{1,0:T(8,128)(2,1)S(1)} %fusion.5.piece0), channel_id=1, source_target_pairs={{0,256},{64,320},{128,384},{192,448},{256,0},{320,64},{384,128},{4... | collective-permute-start | bytes 460808 | tf_op jit(solution)/shard_map/ppermute | solution.py:212
  45.0 18.9 %all-to-all-start.1 = ((bf16[32,16,300]{2,1,0:T(8,128)(2,1)}), bf16[32,16,300]{2,1,0:T(8,128)(2,1)S(1)}, u32[]{:S(2)}, u32[]{:S(2)}) async-start(bf16[32,16,300]{2,1,0:T(8,128)(2,1)} %bitcast.12), calls=%async_computation.1 | async-start | bytes 786432 | tf_op jit(solution)/shard_map/all_to_all | solution.py:222
  52.4 17.6 %collective-permute-start.5 = (bf16[300,256]{1,0:T(8,128)(2,1)S(1)}, bf16[300,256]{1,0:T(8,128)(2,1)S(1)}, u32[]{:S(2)}, u32[]{:S(2)}) collective-permute-start(bf16[300,256]{1,0:T(8,128)(2,1)S(1)} %get-tuple-element.29), channel_id=1, source_target_pairs={{0,128},{64,192},{128,256},{192,320},{256,384},{320,448},{384,0},{... | collective-permute-start | bytes 460808 | tf_op jit(solution)/shard_map/ppermute | solution.py:221
  54.6 15.4 %collective-permute-start.6 = (bf16[300,256]{1,0:T(8,128)(2,1)S(1)}, bf16[300,256]{1,0:T(8,128)(2,1)S(1)}, u32[]{:S(2)}, u32[]{:S(2)}) collective-permute-start(bf16[300,256]{1,0:T(8,128)(2,1)S(1)} %get-tuple-element.30), channel_id=1, source_target_pairs={{0,256},{64,320},{128,384},{192,448},{256,0},{320,64},{384,128},{4... | collective-permute-start | bytes 460808 | tf_op jit(solution)/shard_map/ppermute | solution.py:221
  58.9 11.2 %collective-permute-start.7 = (bf16[300,256]{1,0:T(8,128)(2,1)S(1)}, bf16[300,256]{1,0:T(8,128)(2,1)S(1)}, u32[]{:S(2)}, u32[]{:S(2)}) collective-permute-start(bf16[300,256]{1,0:T(8,128)(2,1)S(1)} %get-tuple-element.31), channel_id=1, source_target_pairs={{0,384},{64,448},{128,0},{192,64},{256,128},{320,192},{384,256},{4... | collective-permute-start | bytes 460808 | tf_op jit(solution)/shard_map/ppermute | solution.py:221
  64.0 11.3 %collective-permute-start.4 = (f32[16,300]{1,0:T(8,128)S(1)}, f32[16,300]{1,0:T(8,128)S(1)}, u32[]{:S(2)}, u32[]{:S(2)}) collective-permute-start(f32[16,300]{1,0:T(8,128)S(1)} %convert_reduce_fusion.1.near), channel_id=1, source_target_pairs={{0,1},{1,0},{2,3},{3,2},{4,5},{5,4},{6,7},{7,6},{8,9},{9,8},{10,11... | collective-permute-start | bytes 57608 | tf_op jit(solution)/shard_map/ppermute | solution.py:227
  70.8 12.7 %collective-permute-start.8 = (bf16[300,256]{1,0:T(8,128)(2,1)}, bf16[300,256]{1,0:T(8,128)(2,1)}, u32[]{:S(2)}, u32[]{:S(2)}) collective-permute-start(bf16[300,256]{1,0:T(8,128)(2,1)} %get-tuple-element.48.after), channel_id=1, source_target_pairs={{0,64},{64,0},{128,192},{192,128},{256,320},{320,256},{384,448},{4... | collective-permute-start | bytes 460808 | tf_op jit(solution)/shard_map/ppermute | solution.py:229
  76.1 19.1 %all-to-all-start.2 = ((bf16[32,16,300]{2,1,0:T(8,128)(2,1)}), bf16[32,16,300]{2,1,0:T(8,128)(2,1)}, u32[]{:S(2)}, u32[]{:S(2)}) async-start(bf16[32,16,300]{2,1,0:T(8,128)(2,1)} %get-tuple-element.32.after), calls=%async_computation.2 | async-start | bytes 786432 | tf_op jit(solution)/shard_map/all_to_all | solution.py:211
  84.7 9.1 %collective-permute-start.11 = (bf16[300,256]{1,0:T(8,128)(2,1)S(1)}, bf16[300,256]{1,0:T(8,128)(2,1)S(1)}, u32[]{:S(2)}, u32[]{:S(2)}) collective-permute-start(bf16[300,256]{1,0:T(8,128)(2,1)S(1)} %get-tuple-element.33.piece0), channel_id=1, source_target_pairs={{0,128},{64,192},{128,256},{192,320},{256,384},{320,448},{384,0},{... | collective-permute-start | bytes 460808 | tf_op jit(solution)/shard_map/ppermute | solution.py:212
  87.0 11.5 %collective-permute-start.10 = (bf16[300,256]{1,0:T(8,128)(2,1)S(1)}, bf16[300,256]{1,0:T(8,128)(2,1)S(1)}, u32[]{:S(2)}, u32[]{:S(2)}) collective-permute-start(bf16[300,256]{1,0:T(8,128)(2,1)S(1)} %get-tuple-element.33.piece0), channel_id=1, source_target_pairs={{0,384},{64,448},{128,0},{192,64},{256,128},{320,192},{384,256},{4... | collective-permute-start | bytes 460808 | tf_op jit(solution)/shard_map/ppermute | solution.py:212
  91.2 7.7 %collective-permute-start.9 = (bf16[300,256]{1,0:T(8,128)(2,1)S(1)}, bf16[300,256]{1,0:T(8,128)(2,1)S(1)}, u32[]{:S(2)}, u32[]{:S(2)}) collective-permute-start(bf16[300,256]{1,0:T(8,128)(2,1)S(1)} %get-tuple-element.33.piece0), channel_id=1, source_target_pairs={{0,256},{64,320},{128,384},{192,448},{256,0},{320,64},{384,128},{4... | collective-permute-start | bytes 460808 | tf_op jit(solution)/shard_map/ppermute | solution.py:212
  102.4 26.8 %all-to-all-start.3 = ((bf16[32,16,300]{2,1,0:T(8,128)(2,1)}), bf16[32,16,300]{2,1,0:T(8,128)(2,1)S(1)}, u32[]{:S(2)}, u32[]{:S(2)}) async-start(bf16[32,16,300]{2,1,0:T(8,128)(2,1)} %bitcast.17), calls=%async_computation.3 | async-start | bytes 786432 | tf_op jit(solution)/shard_map/all_to_all | solution.py:222
  111.7 8.7 %collective-permute-start.13 = (bf16[300,256]{1,0:T(8,128)(2,1)S(1)}, bf16[300,256]{1,0:T(8,128)(2,1)S(1)}, u32[]{:S(2)}, u32[]{:S(2)}) collective-permute-start(bf16[300,256]{1,0:T(8,128)(2,1)S(1)} %get-tuple-element.39), channel_id=1, source_target_pairs={{0,128},{64,192},{128,256},{192,320},{256,384},{320,448},{384,0},{... | collective-permute-start | bytes 460808 | tf_op jit(solution)/shard_map/ppermute | solution.py:221
  113.6 8.1 %collective-permute-start.14 = (bf16[300,256]{1,0:T(8,128)(2,1)S(1)}, bf16[300,256]{1,0:T(8,128)(2,1)S(1)}, u32[]{:S(2)}, u32[]{:S(2)}) collective-permute-start(bf16[300,256]{1,0:T(8,128)(2,1)S(1)} %get-tuple-element.40), channel_id=1, source_target_pairs={{0,256},{64,320},{128,384},{192,448},{256,0},{320,64},{384,128},{4... | collective-permute-start | bytes 460808 | tf_op jit(solution)/shard_map/ppermute | solution.py:221
  118.1 6.3 %collective-permute-start.15 = (bf16[300,256]{1,0:T(8,128)(2,1)S(1)}, bf16[300,256]{1,0:T(8,128)(2,1)S(1)}, u32[]{:S(2)}, u32[]{:S(2)}) collective-permute-start(bf16[300,256]{1,0:T(8,128)(2,1)S(1)} %get-tuple-element.41), channel_id=1, source_target_pairs={{0,384},{64,448},{128,0},{192,64},{256,128},{320,192},{384,256},{4... | collective-permute-start | bytes 460808 | tf_op jit(solution)/shard_map/ppermute | solution.py:221
  124.5 14.2 %collective-permute-start.16 = (bf16[300,128]{1,0:T(8,128)(2,1)S(1)}, bf16[300,128]{1,0:T(8,128)(2,1)S(1)}, u32[]{:S(2)}, u32[]{:S(2)}) collective-permute-start(bf16[300,128]{1,0:T(8,128)(2,1)S(1)} %select_convert_fusion.after), channel_id=1, source_target_pairs={{0,64},{64,0},{128,192},{192,128},{256,320},{320,256},{384,448},{4... | collective-permute-start | bytes 230408 | tf_op jit(solution)/shard_map/ppermute | solution.py:246
  129.4 8.7 %collective-permute-start.12 = (f32[8,300]{1,0:T(8,128)S(1)}, f32[8,300]{1,0:T(8,128)S(1)}, u32[]{:S(2)}, u32[]{:S(2)}) collective-permute-start(f32[8,300]{1,0:T(8,128)S(1)} %get-tuple-element.58), channel_id=1, source_target_pairs={{0,1},{1,0},{2,3},{3,2},{4,5},{5,4},{6,7},{7,6},{8,9},{9,8},{10,11... | collective-permute-start | bytes 28808 | tf_op jit(solution)/shard_map/ppermute | solution.py:244
  (6 other events, 77.6 us)

commit v6 on v5

--- a/solution.py
+++ b/solution.py
@@ -152,11 +152,15 @@
     send[...] = jnp.broadcast_to(new_emb.astype(jnp.bfloat16)[None], send.shape)
 
 
-def last_kernel(scale, near, far, emb, acc, after, emb_out, acc_out):
-    grad = (near[...] + far[...].astype(jnp.float32)) * scale
-    new_emb, new_acc = adagrad(emb[...], acc[...], grad)
+def last_kernel(row_scale, col_scale, near, far, emb, acc, col_near, col_far, col_emb, col_acc,
+                emb_out, acc_out, col_emb_out, col_acc_out):
+    new_emb, new_acc = adagrad(emb[...], acc[...], (near[...] + far[...]) * row_scale)
     emb_out[...] = new_emb
     acc_out[...] = new_acc
+    grad = (col_near[...] + col_far[...].astype(jnp.float32)) * col_scale
+    new_emb, new_acc = adagrad(col_emb[...], col_acc[...], grad)
+    col_emb_out[...] = new_emb
+    col_acc_out[...] = new_acc
 
 
 def pair_kernel(scale, col_sum, away, emb, acc, after, emb_out, acc_out, send):
@@ -177,13 +181,11 @@
     me = lax.axis_index("row")
     odd = me % 2 == 1
     place = (me // 2).astype(jnp.int32)[None]
-    row_term = (12.0 - jnp.log(row_marg.astype(jnp.float32)))[:, None]
     col_term = jnp.log(col_marg.astype(jnp.float32))[None, :]
     pair = [(i, i ^ 1) for i in range(n_row)]
     step_by = lambda d: [(i, (i // 2 + d) % 4 * 2 + i % 2) for i in range(n_row)]
     row_emb, row_acc = row_emb.T, row_acc.T
     n_chip = n_col // 2
-    cores = [[2 * i, 2 * i + 1] for i in range(n_chip)]
     chips = [[2 * i + core for i in range(n_chip)] for core in range(2)]
     swap = [(i, i ^ 1) for i in range(n_col)]
     second = lax.axis_index("col") % 2 == 1
@@ -191,11 +193,7 @@
     few = row_emb.shape[0]
     to_all = full((n_chip, 2 * few, width), jnp.bfloat16)
     both = jnp.stack([col_emb.astype(jnp.bfloat16), col_acc.astype(jnp.bfloat16)])
-    shared = lax.all_gather(
-        jnp.stack([row_emb, row_acc]), "col", axis=1, tiled=True, axis_index_groups=cores
-    )
-    shared_emb, shared_acc = shared[0], shared[1]
-    row_send = jnp.broadcast_to(shared_emb.astype(jnp.bfloat16)[None], to_all.shape)
+    row_send = jnp.broadcast_to(row_emb.astype(jnp.bfloat16)[None], (n_col, few, width))
     other = lax.ppermute(both, "row", pair).astype(jnp.float32)
     in_order = lambda mine, theirs: jnp.concatenate(
         [jnp.where(odd, theirs, mine), jnp.where(odd, mine, theirs)], axis=1
@@ -208,8 +206,12 @@
     in_hbm = lambda values: pltpu.with_memory_space_constraint(values, pltpu.HBM)
     own = lambda wide: jnp.where(odd, wide[:, half:], wide[:, :half])
     for step in range(2):
-        row_half = lax.all_to_all(row_send, "col", 0, 0, axis_index_groups=chips).reshape(rows, width)
+        peers = chips if step else None
+        row_half = lax.all_to_all(row_send, "col", 0, 0, axis_index_groups=peers).reshape(rows, width)
         pieces = [pair_send] + [lax.ppermute(pair_send, "row", step_by(-d)) for d in (1, 2, 3)]
+        if step == 0:
+            row_marg, pieces[3] = lax.optimization_barrier((row_marg, pieces[3]))
+            row_term = (12.0 - jnp.log(row_marg.astype(jnp.float32)))[:, None]
         operands = (in_hbm(counts), row_term, col_term)
         part, *grads_a = tile_grads((0, 3), place, row_half, (pieces[0], pieces[3]), *operands)
         grad_rows, *grads_b = tile_grads(
@@ -224,7 +226,13 @@
         )
         near = jnp.sum(parts.astype(jnp.float32), axis=0)
         if step == 0:
-            far = lax.ppermute(near, "col", swap)
+            theirs = lax.ppermute(jnp.concatenate([near, row_emb, row_acc]), "col", swap)
+            far = theirs[: 2 * few]
+            both_cores = lambda mine, theirs: jnp.where(
+                second, jnp.concatenate([theirs, mine]), jnp.concatenate([mine, theirs])
+            )
+            shared_emb = both_cores(row_emb, theirs[2 * few : 3 * few])
+            shared_acc = both_cores(row_acc, theirs[3 * few :])
             half_sum = col_sum.astype(jnp.bfloat16)
             away = lax.ppermute(half_sum, "row", pair)
             shared_emb, shared_acc, row_send = whole_call(
@@ -244,18 +252,14 @@
             far = lax.ppermute(jnp.where(second, near[:few], near[few:]), "col", swap)
             half_sum = jnp.where(odd, col_sum[:, :half], col_sum[:, half:]).astype(jnp.bfloat16)
             away = lax.ppermute(half_sum, "row", pair)
-            row_emb, row_acc = whole_call(
-                functools.partial(last_kernel, row_scale),
-                [full(row_emb.shape)] * 2,
+            row_emb, row_acc, col_emb, col_acc = whole_call(
+                functools.partial(last_kernel, row_scale, col_scale),
+                [full(row_emb.shape)] * 2 + [full(col_emb.shape)] * 2,
                 1 << 20,
-                [vmem, vmem, vmem, vmem, anywhere],
-            )(mine(near), far, mine(shared_emb), mine(shared_acc), half_sum)
-            col_emb, col_acc = whole_call(
-                functools.partial(last_kernel, col_scale),
-                [full(col_emb.shape)] * 2,
-                1 << 20,
-                [vmem, vmem, vmem, vmem, anywhere],
-            )(own(col_sum), away, own(pair_emb), own(pair_acc), row_emb)
+            )(
+                mine(near), far, mine(shared_emb), mine(shared_acc),
+                own(col_sum), away, own(pair_emb), own(pair_acc),
+            )
     return (row_emb.T, row_acc.T, col_emb, col_acc)
 
 

time: 143 us -> 141 us (0.986)
  blocking collectives: 2.44 us -> 0 us
  waiting for transfers between devices: 11.3 us -> 13 us
    all_gather x1 -> x0, blocking collectives: 2.44 us -> none  [on_device(): lax.all_gather(jnp.stack([row_emb, row_acc]), 'col', axis=1, tiled=True,...]
  transfers between devices with their start and end apart: 21 -> 21, of which waited for: 7 -> 7; matrix products, arithmetic and copies ran while one was open for 2% -> 2% of each run, Pallas kernels for 7% -> 6%
where the time goes in v6:
time: 141 us; the launch traced here: 138 us
  starting transfers between devices  103 us (73%)
  Pallas kernels  16.6 us (12%)
  waiting for transfers between devices  13 us (9%)
  other arithmetic  3.07 us (2%)
    ppermute x6, starting transfers between devices, on_device(): lax.ppermute(pair_send, 'row', step_by(-d))  19.6 us
    all_to_all x2, starting transfers between devices, on_device(): lax.all_to_all(row_send, 'col', 0, 0, axis_index_groups=peers)  18.7 us
    ppermute x6, starting transfers between devices, on_device(): lax.ppermute(grads[1 + d], 'row', step_by(d)).astype(jnp.float32)  18 us
    all_to_all x2, starting transfers between devices, on_device(): lax.all_to_all(grads[0].reshape(to_all.shape), 'col', 0, 0, axis_index_gr...  15.6 us
    pallas_call x4, Pallas kernels, tile_grads(): pl.pallas_call(functools.partial(tile_kernel, steps, first), in_specs=[pl...  13.8 us
    ppermute x2, starting transfers between devices, on_device(): away = lax.ppermute(half_sum, 'row', pair)  9.2 us
    ppermute x1, starting transfers between devices, on_device(): other = lax.ppermute(both, 'row', pair).astype(jnp.float32)  8.28 us
    ppermute x1, starting transfers between devices, on_device(): far = lax.ppermute(jnp.where(second, near[:few], near[few:]), 'col', swap)  7.59 us
  transfers between devices with their start and end apart: 21, of which 7 were waited for; matrix products, arithmetic and copies ran while one was open for 2% of the time, Pallas kernels for 6%

profile of v6, /device:TPU:1, one launch (start us, length us, event | category | flops | bytes accessed | tf_op | source)
XLA Modules:
  0.0 137.8 jit_solution(3199093180722869370)
XLA Ops:
  1.8 8.3 %collective-permute-start = (bf16[2,300,128]{2,1,0:T(8,128)(2,1)S(1)}, bf16[2,300,128]{2,1,0:T(8,128)(2,1)S(1)}, u32[]{:S(2)}, u32[]{:S(2)}) collective-permute-start(bf16[2,300,128]{2,1,0:T(8,128)(2,1)S(1)} %pad_maximum_fusion.2), channel_id=1, source_target_pairs={{0,64},{64,0},{128,192},{192,128},{256,320},{320,256},{384,448},{4... | collective-permute-start | bytes 460808 | tf_op jit(solution)/shard_map/ppermute | solution.py:197
  11.6 12.2 %all-to-all-start = ((bf16[64,8,300]{2,1,0:T(8,128)(2,1)}), bf16[64,8,300]{2,1,0:T(8,128)(2,1)S(1)}, u32[]{:S(2)}, u32[]{:S(2)}) async-start(bf16[64,8,300]{2,1,0:T(8,128)(2,1)} %broadcast_in_dim.16), calls=%async_computation | async-start | bytes 786432 | tf_op jit(solution)/shard_map/all_to_all | solution.py:210
  23.9 3.1 %collective-permute-start.3 = (bf16[300,256]{1,0:T(8,128)(2,1)S(1)}, bf16[300,256]{1,0:T(8,128)(2,1)S(1)}, u32[]{:S(2)}, u32[]{:S(2)}) collective-permute-start(bf16[300,256]{1,0:T(8,128)(2,1)S(1)} %fusion.4.piece0), channel_id=1, source_target_pairs={{0,128},{64,192},{128,256},{192,320},{256,384},{320,448},{384,0},{... | collective-permute-start | bytes 460808 | tf_op jit(solution)/shard_map/ppermute | solution.py:211
  27.1 3.4 %collective-permute-start.2 = (bf16[300,256]{1,0:T(8,128)(2,1)S(1)}, bf16[300,256]{1,0:T(8,128)(2,1)S(1)}, u32[]{:S(2)}, u32[]{:S(2)}) collective-permute-start(bf16[300,256]{1,0:T(8,128)(2,1)S(1)} %fusion.4.piece0), channel_id=1, source_target_pairs={{0,384},{64,448},{128,0},{192,64},{256,128},{320,192},{384,256},{4... | collective-permute-start | bytes 460808 | tf_op jit(solution)/shard_map/ppermute | solution.py:211
  30.4 3.4 %collective-permute-start.1 = (bf16[300,256]{1,0:T(8,128)(2,1)S(1)}, bf16[300,256]{1,0:T(8,128)(2,1)S(1)}, u32[]{:S(2)}, u32[]{:S(2)}) collective-permute-start(bf16[300,256]{1,0:T(8,128)(2,1)S(1)} %fusion.4.piece0), channel_id=1, source_target_pairs={{0,256},{64,320},{128,384},{192,448},{256,0},{320,64},{384,128},{4... | collective-permute-start | bytes 460808 | tf_op jit(solution)/shard_map/ppermute | solution.py:211
  34.1 3.9 %all-to-all-done = bf16[64,8,300]{2,1,0:T(8,128)(2,1)S(1)} async-done(((bf16[64,8,300]{2,1,0:T(8,128)(2,1)}), bf16[64,8,300]{2,1,0:T(8,128)(2,1)S(1)}, u32[]{:S(2)}, u32[]{:S(2)}) %all-to-all-start) | async-done | bytes 307232 | tf_op jit(solution)/shard_map/all_to_all | solution.py:210
  38.0 3.4 %shard_map.102 = (f32[512,300]{1,0:T(8,128)S(1)}, f32[300,256]{1,0:T(8,128)S(1)}, bf16[300,256]{1,0:T(8,128)(2,1)S(1)}) custom-call(s32[1]{0:T(128)} %bitcast.place, bf16[512,300]{1,0:T(8,128)(2,1)S(1)} %bitcast.28, bf16[300,256]{1,0:T(8,128)(2,1)S(1)} %fusion.4.piece0, bf16[300,256]{1,0:T(8,128)(2,1)S(1)} %collective-permute-done.3.piece1, ...), custom_call_target="tpu_custom_call" | custom-call | flops 7549747200 | bytes 1048576 | tf_op jit(solution)/shard_map/pallas_call | solution.py:98
  41.5 3.6 %shard_map.103 = (bf16[512,300]{1,0:T(8,128)(2,1)}, bf16[300,256]{1,0:T(8,128)(2,1)S(1)}, bf16[300,256]{1,0:T(8,128)(2,1)S(1)}) custom-call(s32[1]{0:T(128)} %bitcast.place, bf16[512,300]{1,0:T(8,128)(2,1)S(1)} %bitcast.29, bf16[300,256]{1,0:T(8,128)(2,1)S(1)} %collective-permute-done.1.piece0, bf16[300,256]{1,0:T(8,128)(2,1)S(1)} %collective-permute-done.2.piece1, ...), custom_call_target="tpu_custom_call" | custom-call | flops 7549747200 | bytes 1048576 | tf_op jit(solution)/shard_map/pallas_call | solution.py:98
  45.1 6.9 %all-to-all-start.1 = ((bf16[32,16,300]{2,1,0:T(8,128)(2,1)}), bf16[32,16,300]{2,1,0:T(8,128)(2,1)S(1)}, u32[]{:S(2)}, u32[]{:S(2)}) async-start(bf16[32,16,300]{2,1,0:T(8,128)(2,1)} %bitcast.8), calls=%async_computation.1 | async-start | bytes 786432 | tf_op jit(solution)/shard_map/all_to_all | solution.py:224
  52.1 2.5 %collective-permute-start.5 = (bf16[300,256]{1,0:T(8,128)(2,1)S(1)}, bf16[300,256]{1,0:T(8,128)(2,1)S(1)}, u32[]{:S(2)}, u32[]{:S(2)}) collective-permute-start(bf16[300,256]{1,0:T(8,128)(2,1)S(1)} %get-tuple-element.33), channel_id=1, source_target_pairs={{0,128},{64,192},{128,256},{192,320},{256,384},{320,448},{384,0},{... | collective-permute-start | bytes 460808 | tf_op jit(solution)/shard_map/ppermute | solution.py:223
  54.6 3.8 %collective-permute-start.6 = (bf16[300,256]{1,0:T(8,128)(2,1)S(1)}, bf16[300,256]{1,0:T(8,128)(2,1)S(1)}, u32[]{:S(2)}, u32[]{:S(2)}) collective-permute-start(bf16[300,256]{1,0:T(8,128)(2,1)S(1)} %get-tuple-element.34), channel_id=1, source_target_pairs={{0,256},{64,320},{128,384},{192,448},{256,0},{320,64},{384,128},{4... | collective-permute-start | bytes 460808 | tf_op jit(solution)/shard_map/ppermute | solution.py:223
  58.3 3.1 %collective-permute-start.7 = (bf16[300,256]{1,0:T(8,128)(2,1)S(1)}, bf16[300,256]{1,0:T(8,128)(2,1)S(1)}, u32[]{:S(2)}, u32[]{:S(2)}) collective-permute-start(bf16[300,256]{1,0:T(8,128)(2,1)S(1)} %get-tuple-element.35), channel_id=1, source_target_pairs={{0,384},{64,448},{128,0},{192,64},{256,128},{320,192},{384,256},{4... | collective-permute-start | bytes 460808 | tf_op jit(solution)/shard_map/ppermute | solution.py:223
  63.9 5.9 %collective-permute-start.4 = (f32[32,300]{1,0:T(8,128)S(1)}, f32[32,300]{1,0:T(8,128)S(1)}, u32[]{:S(2)}, u32[]{:S(2)}) collective-permute-start(f32[32,300]{1,0:T(8,128)S(1)} %pad_maximum_fusion.3), channel_id=1, source_target_pairs={{0,1},{1,0},{2,3},{3,2},{4,5},{5,4},{6,7},{7,6},{8,9},{9,8},{10,11... | collective-permute-start | bytes 115208 | tf_op jit(solution)/shard_map/ppermute | solution.py:229
  70.6 4.4 %collective-permute-start.8 = (bf16[300,256]{1,0:T(8,128)(2,1)}, bf16[300,256]{1,0:T(8,128)(2,1)}, u32[]{:S(2)}, u32[]{:S(2)}) collective-permute-start(bf16[300,256]{1,0:T(8,128)(2,1)} %get-tuple-element.52.after), channel_id=1, source_target_pairs={{0,64},{64,0},{128,192},{192,128},{256,320},{320,256},{384,448},{4... | collective-permute-start | bytes 460808 | tf_op jit(solution)/shard_map/ppermute | solution.py:237
  75.9 6.5 %all-to-all-start.2 = ((bf16[32,16,300]{2,1,0:T(8,128)(2,1)}), bf16[32,16,300]{2,1,0:T(8,128)(2,1)}, u32[]{:S(2)}, u32[]{:S(2)}) async-start(bf16[32,16,300]{2,1,0:T(8,128)(2,1)} %get-tuple-element.36.after), calls=%async_computation.2 | async-start | bytes 786432 | tf_op jit(solution)/shard_map/all_to_all | solution.py:210
  84.5 4.1 %collective-permute-start.11 = (bf16[300,256]{1,0:T(8,128)(2,1)S(1)}, bf16[300,256]{1,0:T(8,128)(2,1)S(1)}, u32[]{:S(2)}, u32[]{:S(2)}) collective-permute-start(bf16[300,256]{1,0:T(8,128)(2,1)S(1)} %get-tuple-element.37.piece0), channel_id=1, source_target_pairs={{0,128},{64,192},{128,256},{192,320},{256,384},{320,448},{384,0},{... | collective-permute-start | bytes 460808 | tf_op jit(solution)/shard_map/ppermute | solution.py:211
  91.0 3.2 %collective-permute-start.9 = (bf16[300,256]{1,0:T(8,128)(2,1)S(1)}, bf16[300,256]{1,0:T(8,128)(2,1)S(1)}, u32[]{:S(2)}, u32[]{:S(2)}) collective-permute-start(bf16[300,256]{1,0:T(8,128)(2,1)S(1)} %get-tuple-element.37.piece0), channel_id=1, source_target_pairs={{0,256},{64,320},{128,384},{192,448},{256,0},{320,64},{384,128},{4... | collective-permute-start | bytes 460808 | tf_op jit(solution)/shard_map/ppermute | solution.py:211
  94.3 3.3 %shard_map.106 = (f32[512,300]{1,0:T(8,128)S(1)}, f32[300,256]{1,0:T(8,128)S(1)}, bf16[300,256]{1,0:T(8,128)(2,1)S(1)}) custom-call(s32[1]{0:T(128)} %bitcast.place, bf16[512,300]{1,0:T(8,128)(2,1)} %bitcast.10.rows_in, bf16[300,256]{1,0:T(8,128)(2,1)S(1)} %get-tuple-element.37.piece0, bf16[300,256]{1,0:T(8,128)(2,1)S(1)} %collective-permute-done.11.piece1, ...), custom_call_target="tpu_custom_call" | custom-call | flops 7549747200 | bytes 1048576 | tf_op jit(solution)/shard_map/pallas_call | solution.py:98
  98.5 3.5 %shard_map.107 = (bf16[512,300]{1,0:T(8,128)(2,1)}, bf16[300,256]{1,0:T(8,128)(2,1)S(1)}, bf16[300,256]{1,0:T(8,128)(2,1)S(1)}) custom-call(s32[1]{0:T(128)} %bitcast.place, bf16[512,300]{1,0:T(8,128)(2,1)} %bitcast.10.rows_in, bf16[300,256]{1,0:T(8,128)(2,1)S(1)} %collective-permute-done.9.piece0, bf16[300,256]{1,0:T(8,128)(2,1)S(1)} %collective-permute-done.10.piece1, ...), custom_call_target="tpu_custom_call" | custom-call | flops 7549747200 | bytes 1048576 | tf_op jit(solution)/shard_map/pallas_call | solution.py:98
  101.9 8.7 %all-to-all-start.3 = ((bf16[32,16,300]{2,1,0:T(8,128)(2,1)}), bf16[32,16,300]{2,1,0:T(8,128)(2,1)S(1)}, u32[]{:S(2)}, u32[]{:S(2)}) async-start(bf16[32,16,300]{2,1,0:T(8,128)(2,1)} %bitcast.12), calls=%async_computation.3 | async-start | bytes 786432 | tf_op jit(solution)/shard_map/all_to_all | solution.py:224
  112.6 4.8 %collective-permute-start.14 = (bf16[300,256]{1,0:T(8,128)(2,1)S(1)}, bf16[300,256]{1,0:T(8,128)(2,1)S(1)}, u32[]{:S(2)}, u32[]{:S(2)}) collective-permute-start(bf16[300,256]{1,0:T(8,128)(2,1)S(1)} %get-tuple-element.44), channel_id=1, source_target_pairs={{0,256},{64,320},{128,384},{192,448},{256,0},{320,64},{384,128},{4... | collective-permute-start | bytes 460808 | tf_op jit(solution)/shard_map/ppermute | solution.py:223
  121.1 2.5 %collective-permute-done.15 = bf16[300,256]{1,0:T(8,128)(2,1)S(1)} collective-permute-done((bf16[300,256]{1,0:T(8,128)(2,1)S(1)}, bf16[300,256]{1,0:T(8,128)(2,1)S(1)}, u32[]{:S(2)}, u32[]{:S(2)}) %collective-permute-start.15) | collective-permute-done | bytes 153632 | tf_op jit(solution)/shard_map/ppermute | solution.py:223
  123.7 4.8 %collective-permute-start.16 = (bf16[300,128]{1,0:T(8,128)(2,1)S(1)}, bf16[300,128]{1,0:T(8,128)(2,1)S(1)}, u32[]{:S(2)}, u32[]{:S(2)}) collective-permute-start(bf16[300,128]{1,0:T(8,128)(2,1)S(1)} %select_convert_fusion), channel_id=1, source_target_pairs={{0,64},{64,0},{128,192},{192,128},{256,320},{320,256},{384,448},{4... | collective-permute-start | bytes 230408 | tf_op jit(solution)/shard_map/ppermute | solution.py:254
  128.6 7.6 %collective-permute-start.12 = (f32[8,300]{1,0:T(8,128)S(1)}, f32[8,300]{1,0:T(8,128)S(1)}, u32[]{:S(2)}, u32[]{:S(2)}) collective-permute-start(f32[8,300]{1,0:T(8,128)S(1)} %get-tuple-element.62), channel_id=1, source_target_pairs={{0,1},{1,0},{2,3},{3,2},{4,5},{5,4},{6,7},{7,6},{8,9},{9,8},{10,11... | collective-permute-start | bytes 28808 | tf_op jit(solution)/shard_map/ppermute | solution.py:252
  (73 shorter events, 19.8 us)
Async XLA Ops:
  0.6 23.2 %copy-start.4 = (f32[300,128]{1,0:T(8,128)S(1)}, f32[300,128]{1,0:T(8,128)}, u32[]{:S(2)}) copy-start(f32[300,128]{1,0:T(8,128)} %param.10) | copy-start | bytes 460804
  0.7 26.4 %copy-start.8 = (s32[1024]{0:T(1024)S(1)}, s32[1024]{0:T(1024)}, u32[]{:S(2)}) copy-start(s32[1024]{0:T(1024)} %param.13) | copy-start | bytes 12292
  0.7 33.2 %copy-start.9 = (s32[512]{0:T(512)S(1)}, s32[512]{0:T(512)}, u32[]{:S(2)}) copy-start(s32[512]{0:T(512)} %param.12) | copy-start | bytes 6148
  1.8 22.0 %collective-permute-start = (bf16[2,300,128]{2,1,0:T(8,128)(2,1)S(1)}, bf16[2,300,128]{2,1,0:T(8,128)(2,1)S(1)}, u32[]{:S(2)}, u32[]{:S(2)}) collective-permute-start(bf16[2,300,128]{2,1,0:T(8,128)(2,1)S(1)} %pad_maximum_fusion.2), channel_id=1, source_target_pairs={{0,64},{64,0},{128,192},{192,128},{256,320},{320,256},{384,448},{4... | collective-permute-start | bytes 460808 | tf_op jit(solution)/shard_map/ppermute | solution.py:197
  11.6 26.5 %all-to-all-start = ((bf16[64,8,300]{2,1,0:T(8,128)(2,1)}), bf16[64,8,300]{2,1,0:T(8,128)(2,1)S(1)}, u32[]{:S(2)}, u32[]{:S(2)}) async-start(bf16[64,8,300]{2,1,0:T(8,128)(2,1)} %broadcast_in_dim.16), calls=%async_computation | async-start | bytes 786432 | tf_op jit(solution)/shard_map/all_to_all | solution.py:210
  23.9 10.0 %collective-permute-start.3 = (bf16[300,256]{1,0:T(8,128)(2,1)S(1)}, bf16[300,256]{1,0:T(8,128)(2,1)S(1)}, u32[]{:S(2)}, u32[]{:S(2)}) collective-permute-start(bf16[300,256]{1,0:T(8,128)(2,1)S(1)} %fusion.4.piece0), channel_id=1, source_target_pairs={{0,128},{64,192},{128,256},{192,320},{256,384},{320,448},{384,0},{... | collective-permute-start | bytes 460808 | tf_op jit(solution)/shard_map/ppermute | solution.py:211
  27.1 14.4 %collective-permute-start.2 = (bf16[300,256]{1,0:T(8,128)(2,1)S(1)}, bf16[300,256]{1,0:T(8,128)(2,1)S(1)}, u32[]{:S(2)}, u32[]{:S(2)}) collective-permute-start(bf16[300,256]{1,0:T(8,128)(2,1)S(1)} %fusion.4.piece0), channel_id=1, source_target_pairs={{0,384},{64,448},{128,0},{192,64},{256,128},{320,192},{384,256},{4... | collective-permute-start | bytes 460808 | tf_op jit(solution)/shard_map/ppermute | solution.py:211
  30.4 11.0 %collective-permute-start.1 = (bf16[300,256]{1,0:T(8,128)(2,1)S(1)}, bf16[300,256]{1,0:T(8,128)(2,1)S(1)}, u32[]{:S(2)}, u32[]{:S(2)}) collective-permute-start(bf16[300,256]{1,0:T(8,128)(2,1)S(1)} %fusion.4.piece0), channel_id=1, source_target_pairs={{0,256},{64,320},{128,384},{192,448},{256,0},{320,64},{384,128},{4... | collective-permute-start | bytes 460808 | tf_op jit(solution)/shard_map/ppermute | solution.py:211
  45.1 18.7 %all-to-all-start.1 = ((bf16[32,16,300]{2,1,0:T(8,128)(2,1)}), bf16[32,16,300]{2,1,0:T(8,128)(2,1)S(1)}, u32[]{:S(2)}, u32[]{:S(2)}) async-start(bf16[32,16,300]{2,1,0:T(8,128)(2,1)} %bitcast.8), calls=%async_computation.1 | async-start | bytes 786432 | tf_op jit(solution)/shard_map/all_to_all | solution.py:224
  52.1 17.8 %collective-permute-start.5 = (bf16[300,256]{1,0:T(8,128)(2,1)S(1)}, bf16[300,256]{1,0:T(8,128)(2,1)S(1)}, u32[]{:S(2)}, u32[]{:S(2)}) collective-permute-start(bf16[300,256]{1,0:T(8,128)(2,1)S(1)} %get-tuple-element.33), channel_id=1, source_target_pairs={{0,128},{64,192},{128,256},{192,320},{256,384},{320,448},{384,0},{... | collective-permute-start | bytes 460808 | tf_op jit(solution)/shard_map/ppermute | solution.py:223
  54.6 15.3 %collective-permute-start.6 = (bf16[300,256]{1,0:T(8,128)(2,1)S(1)}, bf16[300,256]{1,0:T(8,128)(2,1)S(1)}, u32[]{:S(2)}, u32[]{:S(2)}) collective-permute-start(bf16[300,256]{1,0:T(8,128)(2,1)S(1)} %get-tuple-element.34), channel_id=1, source_target_pairs={{0,256},{64,320},{128,384},{192,448},{256,0},{320,64},{384,128},{4... | collective-permute-start | bytes 460808 | tf_op jit(solution)/shard_map/ppermute | solution.py:223
  58.3 11.5 %collective-permute-start.7 = (bf16[300,256]{1,0:T(8,128)(2,1)S(1)}, bf16[300,256]{1,0:T(8,128)(2,1)S(1)}, u32[]{:S(2)}, u32[]{:S(2)}) collective-permute-start(bf16[300,256]{1,0:T(8,128)(2,1)S(1)} %get-tuple-element.35), channel_id=1, source_target_pairs={{0,384},{64,448},{128,0},{192,64},{256,128},{320,192},{384,256},{4... | collective-permute-start | bytes 460808 | tf_op jit(solution)/shard_map/ppermute | solution.py:223
  63.9 11.2 %collective-permute-start.4 = (f32[32,300]{1,0:T(8,128)S(1)}, f32[32,300]{1,0:T(8,128)S(1)}, u32[]{:S(2)}, u32[]{:S(2)}) collective-permute-start(f32[32,300]{1,0:T(8,128)S(1)} %pad_maximum_fusion.3), channel_id=1, source_target_pairs={{0,1},{1,0},{2,3},{3,2},{4,5},{5,4},{6,7},{7,6},{8,9},{9,8},{10,11... | collective-permute-start | bytes 115208 | tf_op jit(solution)/shard_map/ppermute | solution.py:229
  70.6 12.7 %collective-permute-start.8 = (bf16[300,256]{1,0:T(8,128)(2,1)}, bf16[300,256]{1,0:T(8,128)(2,1)}, u32[]{:S(2)}, u32[]{:S(2)}) collective-permute-start(bf16[300,256]{1,0:T(8,128)(2,1)} %get-tuple-element.52.after), channel_id=1, source_target_pairs={{0,64},{64,0},{128,192},{192,128},{256,320},{320,256},{384,448},{4... | collective-permute-start | bytes 460808 | tf_op jit(solution)/shard_map/ppermute | solution.py:237
  75.9 18.3 %all-to-all-start.2 = ((bf16[32,16,300]{2,1,0:T(8,128)(2,1)}), bf16[32,16,300]{2,1,0:T(8,128)(2,1)}, u32[]{:S(2)}, u32[]{:S(2)}) async-start(bf16[32,16,300]{2,1,0:T(8,128)(2,1)} %get-tuple-element.36.after), calls=%async_computation.2 | async-start | bytes 786432 | tf_op jit(solution)/shard_map/all_to_all | solution.py:210
  84.5 9.8 %collective-permute-start.11 = (bf16[300,256]{1,0:T(8,128)(2,1)S(1)}, bf16[300,256]{1,0:T(8,128)(2,1)S(1)}, u32[]{:S(2)}, u32[]{:S(2)}) collective-permute-start(bf16[300,256]{1,0:T(8,128)(2,1)S(1)} %get-tuple-element.37.piece0), channel_id=1, source_target_pairs={{0,128},{64,192},{128,256},{192,320},{256,384},{320,448},{384,0},{... | collective-permute-start | bytes 460808 | tf_op jit(solution)/shard_map/ppermute | solution.py:211
  88.5 9.1 %collective-permute-start.10 = (bf16[300,256]{1,0:T(8,128)(2,1)S(1)}, bf16[300,256]{1,0:T(8,128)(2,1)S(1)}, u32[]{:S(2)}, u32[]{:S(2)}) collective-permute-start(bf16[300,256]{1,0:T(8,128)(2,1)S(1)} %get-tuple-element.37.piece0), channel_id=1, source_target_pairs={{0,384},{64,448},{128,0},{192,64},{256,128},{320,192},{384,256},{4... | collective-permute-start | bytes 460808 | tf_op jit(solution)/shard_map/ppermute | solution.py:211
  91.0 7.5 %collective-permute-start.9 = (bf16[300,256]{1,0:T(8,128)(2,1)S(1)}, bf16[300,256]{1,0:T(8,128)(2,1)S(1)}, u32[]{:S(2)}, u32[]{:S(2)}) collective-permute-start(bf16[300,256]{1,0:T(8,128)(2,1)S(1)} %get-tuple-element.37.piece0), channel_id=1, source_target_pairs={{0,256},{64,320},{128,384},{192,448},{256,0},{320,64},{384,128},{4... | collective-permute-start | bytes 460808 | tf_op jit(solution)/shard_map/ppermute | solution.py:211
  101.9 26.6 %all-to-all-start.3 = ((bf16[32,16,300]{2,1,0:T(8,128)(2,1)}), bf16[32,16,300]{2,1,0:T(8,128)(2,1)S(1)}, u32[]{:S(2)}, u32[]{:S(2)}) async-start(bf16[32,16,300]{2,1,0:T(8,128)(2,1)} %bitcast.12), calls=%async_computation.3 | async-start | bytes 786432 | tf_op jit(solution)/shard_map/all_to_all | solution.py:224
  110.6 8.7 %collective-permute-start.13 = (bf16[300,256]{1,0:T(8,128)(2,1)S(1)}, bf16[300,256]{1,0:T(8,128)(2,1)S(1)}, u32[]{:S(2)}, u32[]{:S(2)}) collective-permute-start(bf16[300,256]{1,0:T(8,128)(2,1)S(1)} %get-tuple-element.43), channel_id=1, source_target_pairs={{0,128},{64,192},{128,256},{192,320},{256,384},{320,448},{384,0},{... | collective-permute-start | bytes 460808 | tf_op jit(solution)/shard_map/ppermute | solution.py:223
  112.6 8.6 %collective-permute-start.14 = (bf16[300,256]{1,0:T(8,128)(2,1)S(1)}, bf16[300,256]{1,0:T(8,128)(2,1)S(1)}, u32[]{:S(2)}, u32[]{:S(2)}) collective-permute-start(bf16[300,256]{1,0:T(8,128)(2,1)S(1)} %get-tuple-element.44), channel_id=1, source_target_pairs={{0,256},{64,320},{128,384},{192,448},{256,0},{320,64},{384,128},{4... | collective-permute-start | bytes 460808 | tf_op jit(solution)/shard_map/ppermute | solution.py:223
  117.3 6.3 %collective-permute-start.15 = (bf16[300,256]{1,0:T(8,128)(2,1)S(1)}, bf16[300,256]{1,0:T(8,128)(2,1)S(1)}, u32[]{:S(2)}, u32[]{:S(2)}) collective-permute-start(bf16[300,256]{1,0:T(8,128)(2,1)S(1)} %get-tuple-element.45), channel_id=1, source_target_pairs={{0,384},{64,448},{128,0},{192,64},{256,128},{320,192},{384,256},{4... | collective-permute-start | bytes 460808 | tf_op jit(solution)/shard_map/ppermute | solution.py:223
  123.7 12.5 %collective-permute-start.16 = (bf16[300,128]{1,0:T(8,128)(2,1)S(1)}, bf16[300,128]{1,0:T(8,128)(2,1)S(1)}, u32[]{:S(2)}, u32[]{:S(2)}) collective-permute-start(bf16[300,128]{1,0:T(8,128)(2,1)S(1)} %select_convert_fusion), channel_id=1, source_target_pairs={{0,64},{64,0},{128,192},{192,128},{256,320},{320,256},{384,448},{4... | collective-permute-start | bytes 230408 | tf_op jit(solution)/shard_map/ppermute | solution.py:254
  128.6 8.4 %collective-permute-start.12 = (f32[8,300]{1,0:T(8,128)S(1)}, f32[8,300]{1,0:T(8,128)S(1)}, u32[]{:S(2)}, u32[]{:S(2)}) collective-permute-start(f32[8,300]{1,0:T(8,128)S(1)} %get-tuple-element.62), channel_id=1, source_target_pairs={{0,1},{1,0},{2,3},{3,2},{4,5},{5,4},{6,7},{7,6},{8,9},{9,8},{10,11... | collective-permute-start | bytes 28808 | tf_op jit(solution)/shard_map/ppermute | solution.py:252
  (7 other events, 104.4 us)
